TPU v7x, 32 devices: a whole 2x2x4 slice. The times are simulated.
32 devices in a mesh: dp: 4 (over z), shard: 8 (over y, x, core).
Axes of the slice: x: 2, y: 2, z: 4, core: 2. Of those that a mesh axis runs over, the one named last changes fastest.
Arguments:
- head_terms: bfloat16 [512, 8, 256], P('dp', 'shard'), may hold values from -0.375 to 0.375
- inputs: bfloat16 [512, 2, 4096], P('dp'), may hold values from -6 to 6
- owner_list: int32 [8, 256, 1], P('shard'), may hold values from 0 to 3; in each aligned block of 64 rows (0 to 63, 64 to 127, ..., all dimensions but the last counted through in order) at most 32 rows name the same one
- param_slots: bfloat16 [8, 512, 4096], P('shard', 'dp'), may hold values from -3 to 3
- row_state: float32 [8, 512], P('shard', 'dp'), may hold values from 0.25 to 4
- col_state: float32 [8, 4, 4096], P('shard'), may hold values from 0.25 to 4
Outputs:
- new_params: bfloat16 [8, 512, 4096], P('shard', 'dp')
- new_rows: float32 [8, 512], P('shard', 'dp')
- new_cols: float32 [8, 4, 4096], P('shard')
Inputs may be any that keep to these rules, and one draw needn't show every extreme that they name: `owner_list`: each head's 256 rows fall into 4 aligned home blocks of 64 rows; within one home block no owner index is named more than 32 times.
All inputs are finite; a program needn't handle non-finite values.
Results may differ from a plain program's by a relative error of at most 0.0012.
Values sent between devices are 32-bit elements; how exact they have to be, the bound alone decides.
No kernel may reach another device: no remote copies, remote signals or barrier semaphores. Data moves between devices by JAX's collectives and lax.ppermute only.
A program may use at most 64 MiB of HBM per device.

v0:
```python
import jax
import jax.numpy as jnp
from jax import lax
from jax.sharding import PartitionSpec as P

DKV = 64
PROJ = 4


DECAY_RATE = 0.5
STEP_SIZE = 0.5
EPS_SQUARE = 1e-30


def slot_table(owner_col, owner_count, pair_most):
    row_count = owner_col.shape[0]
    block_rows = row_count // owner_count
    index_ids = jnp.arange(owner_count, dtype=jnp.int32)
    onehot = (owner_col[:, None] == index_ids[None, :]).astype(jnp.int32)
    blocked = onehot.reshape(owner_count, block_rows, owner_count)
    before = jnp.cumsum(blocked, axis=1) - blocked
    order_in = jnp.sum(before * blocked, axis=2).reshape(row_count)
    row_ids = jnp.arange(row_count, dtype=jnp.int32)
    block_of = row_ids // block_rows
    slot_ids = jnp.arange(pair_most, dtype=jnp.int32)
    match_owner = owner_col[None, None, None, :] == index_ids[:, None, None, None]
    match_block = block_of[None, None, None, :] == index_ids[None, :, None, None]
    match_slot = order_in[None, None, None, :] == slot_ids[None, None, :, None]
    hits = (match_owner & match_block & match_slot).astype(jnp.int32)
    live_mask = jnp.sum(hits, axis=3).reshape(owner_count, owner_count * pair_most)
    slot_row = jnp.sum(hits * row_ids[None, None, None, :], axis=3).reshape(
        owner_count, owner_count * pair_most
    )
    return (slot_row, live_mask)


def on_device(head_terms, inputs, owner_list, param_slots, row_state, col_state):
    dp_count = lax.axis_size("dp")
    my_index = lax.axis_index("dp")
    head_rows = head_terms[:, 0, :]
    row_count = head_rows.shape[1]
    width = inputs.shape[2]
    slot_count = param_slots.shape[1]
    pair_most = slot_count // dp_count
    block_rows = row_count // dp_count
    split_at = (PROJ - 1) * DKV
    first_part = jnp.einsum(
        "tr,td->rd", head_rows[:, :split_at], inputs[:, 0, :], preferred_element_type=jnp.float32
    )
    last_part = jnp.einsum(
        "tr,td->rd", head_rows[:, split_at:], inputs[:, 1, :], preferred_element_type=jnp.float32
    )
    gradient = jnp.concatenate([first_part, last_part], axis=0)
    slot_row, live_mask = slot_table(owner_list[0, :, 0], dp_count, pair_most)
    home_sum = lax.psum_scatter(gradient, "dp", scatter_dimension=0, tiled=True)
    local_rows = (
        lax.dynamic_slice_in_dim(slot_row, my_index * pair_most, pair_most, 1)
        - my_index * block_rows
    )
    outgoing = jnp.take(home_sum, local_rows.reshape(-1), axis=0, mode="clip").reshape(
        dp_count, pair_most, width
    )
    received = lax.all_to_all(outgoing, "dp", split_axis=0, concat_axis=0, tiled=True)
    slot_grad = received.reshape(slot_count, width)
    my_rows = lax.dynamic_index_in_dim(slot_row, my_index, 0, keepdims=False)
    live_f = lax.dynamic_index_in_dim(live_mask, my_index, 0, keepdims=False).astype(jnp.float32)
    grad_sq = slot_grad * slot_grad + EPS_SQUARE
    row_val = DECAY_RATE * row_state[0] + (1.0 - DECAY_RATE) * jnp.mean(grad_sq, axis=1)
    slot_pick = ((my_rows // DKV)[:, None] == jnp.arange(PROJ, dtype=jnp.int32)[None, :]).astype(
        jnp.float32
    )
    live_pick = slot_pick * live_f[:, None]
    col_part = jnp.einsum("sp,sd->pd", live_pick, grad_sq, precision=lax.Precision.HIGHEST)
    row_part = jnp.sum(live_pick * row_val[:, None], axis=0)
    col_sum, row_total = lax.psum((col_part, row_part), "dp")
    new_col = DECAY_RATE * col_state[0] + (1.0 - DECAY_RATE) * col_sum / DKV
    row_mean = row_total / DKV
    col_at = jnp.dot(slot_pick, new_col, precision=lax.Precision.HIGHEST)
    mean_at = jnp.sum(slot_pick * row_mean[None, :], axis=1)
    second_moment = row_val[:, None] * col_at / mean_at[:, None]
    update = slot_grad / jnp.sqrt(second_moment)
    new_param = (
        (param_slots[0].astype(jnp.float32) - STEP_SIZE * update) * live_f[:, None]
    ).astype(jnp.bfloat16)
    return (new_param[None], (row_val * live_f)[None], new_col[None])


def solution(mesh):
    placed = (
        P("dp", "shard", None),
        P("dp", None, None),
        P("shard", None, None),
        P("shard", "dp", None),
        P("shard", "dp"),
        P("shard", None, None),
    )
    return jax.shard_map(
        on_device,
        mesh=mesh,
        in_specs=placed,
        out_specs=(P("shard", "dp", None), P("shard", "dp"), P("shard", None, None)),
        check_vma=False,
    )
```

profile of v0, /device:TPU:0, one launch (start us, length us, event | category | flops | bytes accessed | tf_op | source)
XLA Modules:
  0.0 211.8 jit_solution(7495609928079223295)
XLA Ops:
  7.2 6.2 %fusion.30 = (bf16[128,1,4096]{2,1,0:T(2,128)(2,1)S(1)}, bf16[128,1,4096]{2,1,0:T(2,128)(2,1)S(1)}) fusion(bf16[128,2,4096]{2,1,0:T(2,128)(2,1)} %param.7), kind=kLoop, calls=%fused_computation.65 | loop fusion | bytes 4194304 | tf_op jit(solution)/shard_map/slice | solution.py:48
  13.5 1.3 fusion.9
  14.8 1.5 fusion.10
  16.3 2.2 %pad_maximum_fusion = f32[256,4096]{1,0:T(8,128)} fusion(f32[64,4096]{1,0:T(8,128)S(1)} %fusion.9, f32[192,4096]{1,0:T(8,128)S(1)} %fusion.10), kind=kLoop, calls=%fused_computation.10 | loop fusion | flops 1048576 | bytes 8388608 | tf_op jit(solution)/shard_map/concatenate | solution.py:53
  18.5 0.5 broadcast.205
  19.1 0.1 copy-done.2
  19.2 0.7 reduce.4
  19.9 0.1 fusion.13
  20.1 0.1 reduce_window_sum.11
  20.2 0.2 select_reduce_fusion
  20.6 0.6 fusion.12
  21.5 76.7 %reduce-scatter.2.cloned.1.call-done = f32[64,4096]{1,0:T(8,128)} async-done(((f32[256,4096]{1,0:T(8,128)}), f32[64,4096]{1,0:T(8,128)}) %reduce-scatter.2.cloned.1.call-update) | async-done | bytes 1048592 | tf_op jit(solution)/shard_map/reduce_scatter | solution.py:55
  98.2 4.7 %gather_fusion = f32[128,4096]{1,0:T(8,128)} fusion(f32[64,4096]{1,0:T(8,128)} %reduce-scatter.2.cloned.1.call-done, s32[1024]{0:T(1024)S(1)} %pad_clamp_fusion), kind=kCustom, calls=%fused_computation | custom fusion | bytes 4194816 | tf_op jit(solution)/shard_map/jit(_take)/gather | solution.py:60
  102.8 4.2 %all-to-all-start = ((f32[4,32,4096]{2,1,0:T(8,128)}), f32[4,32,4096]{2,1,0:T(8,128)S(1)}, u32[]{:S(2)}, u32[]{:S(2)}) async-start(f32[4,32,4096]{2,1,0:T(8,128)} %bitcast.36), calls=%async_computation.1 | async-start | bytes 4194304 | tf_op jit(solution)/shard_map/all_to_all | solution.py:63
  107.2 48.1 %all-to-all-done = f32[4,32,4096]{2,1,0:T(8,128)S(1)} async-done(((f32[4,32,4096]{2,1,0:T(8,128)}), f32[4,32,4096]{2,1,0:T(8,128)S(1)}, u32[]{:S(2)}, u32[]{:S(2)}) %all-to-all-start) | async-done | bytes 2097184 | tf_op jit(solution)/shard_map/all_to_all | solution.py:63
  155.3 0.3 add_reduce_fusion
  155.7 0.1 fusion.19
  155.9 9.8 %psum.15 = f32[4]{0:T(128)S(1)} all-reduce(f32[4]{0:T(128)S(1)} %fusion.19), channel_id=1, replica_groups=mesh['dp'=4,'shard'=8] {'dp'}, use_global_device_ids=true, to_apply=%region_8.9 | all-reduce | flops 4 | bytes 32 | tf_op jit(solution)/shard_map/psum | solution.py:75
  165.7 0.3 fusion.8
  166.0 1.7 fusion.17
  167.8 0.5 add_multiply_fusion
  168.4 31.7 %all-reduce.2.cloned.1.call-done = f32[4,4096]{1,0:T(4,128)} async-done(((f32[4,4096]{1,0:T(4,128)}), f32[4,4096]{1,0:T(4,128)}) %all-reduce.2.cloned.1.call-update) | async-done | bytes 65552 | tf_op jit(solution)/shard_map/psum | solution.py:75
  200.0 1.5 fusion.16
  201.5 3.5 %fusion.7 = bf16[1,128,4096]{2,1,0:T(8,128)(2,1)} fusion(f32[128,4096]{1,0:T(8,128)S(1)} %bitcast.35, bf16[1,128,4096]{2,1,0:T(8,128)(2,1)S(1)} %copy-done.4, f32[128]{0:T(128)S(1)} %fusion.26, f32[128]{0:T(128)S(1)} %select_reduce_fusion.1, f32[128]{0:T(128)S(1)} %bitcast_add_fusion.2, f32[4,4096]{1,0:T(4,128)} %all-reduce.2.cloned.1.call-done, ...), kind=kOutput, calls=%fused_computation.9 | convolution fusion | flops 29409792 | bytes 4327424 | tf_op jit(solution)/shard_map/dot_general | solution.py:78
  (32 shorter events, 0.9 us)
Async XLA Ops:
  7.2 6.3 %copy-start = (bf16[128,1,256]{2,0,1:T(8,128)(2,1)S(1)}, bf16[128,1,256]{2,0,1:T(8,128)(2,1)}, u32[]{:S(2)}) copy-start(bf16[128,1,256]{2,0,1:T(8,128)(2,1)} %param.6) | copy-start | bytes 196612
  7.2 91.0 %reduce-scatter.2.cloned.1.call-start = ((), (), s32[]{:S(2)}) async-start(), calls=%async_computation.2 | async-start | bytes 5242880 | tf_op jit(solution)/shard_map/reduce_scatter | solution.py:55
  18.5 0.7 copy-start.2
  102.8 52.5 %all-to-all-start = ((f32[4,32,4096]{2,1,0:T(8,128)}), f32[4,32,4096]{2,1,0:T(8,128)S(1)}, u32[]{:S(2)}, u32[]{:S(2)}) async-start(f32[4,32,4096]{2,1,0:T(8,128)} %bitcast.36), calls=%async_computation.1 | async-start | bytes 4194304 | tf_op jit(solution)/shard_map/all_to_all | solution.py:63
  107.1 48.6 %copy-start.3 = (f32[1,128]{1,0:T(1,128)S(1)}, f32[1,128]{1,0:T(1,128)}, u32[]{:S(2)}) copy-start(f32[1,128]{1,0:T(1,128)} %param.10) | copy-start | bytes 1540
  107.1 93.0 %all-reduce.2.cloned.1.call-start = ((), (), s32[]{:S(2)}) async-start(), calls=%async_computation.3 | async-start | bytes 131072 | tf_op jit(solution)/shard_map/psum | solution.py:75
  166.0 34.0 %copy-start.1 = (f32[1,4,4096]{2,1,0:T(4,128)S(1)}, f32[1,4,4096]{2,1,0:T(4,128)}, u32[]{:S(2)}) copy-start(f32[1,4,4096]{2,1,0:T(4,128)} %param.11) | copy-start | bytes 196612
  166.0 35.5 %copy-start.4 = (bf16[1,128,4096]{2,1,0:T(8,128)(2,1)S(1)}, bf16[1,128,4096]{2,1,0:T(8,128)(2,1)}, u32[]{:S(2)}) copy-start(bf16[1,128,4096]{2,1,0:T(8,128)(2,1)} %param.9) | copy-start | bytes 3145732
Sparse Core Ops, SparseCore 0:
  18.7 79.4 reduce-scatter.1
  167.9 32.0 all-reduce.1
where the time goes:
time: 212 us
  waiting for transfers between devices  157 us (74%)
  between operations  14.1 us (7%)
  local copies, waits for them, and re-layouts  12.2 us (6%)
  blocking collectives  9.8 us (5%)
  matrix products  7.99 us (4%)
  other arithmetic  6.94 us (3%)
  starting transfers between devices  4.26 us (2%)
    reduce_scatter x1, waiting for transfers between devices, on_device(): home_sum = lax.psum_scatter(gradient, 'dp', scatter_dimension=0, tiled=True)  76.7 us
    all_to_all x1, waiting for transfers between devices, on_device(): lax.all_to_all(outgoing, 'dp', split_axis=0, concat_axis=0, tiled=True)  48.1 us
    psum x1, waiting for transfers between devices, on_device(): col_sum, row_total = lax.psum((col_part, row_part), 'dp')  31.7 us
    psum x1, blocking collectives, on_device(): col_sum, row_total = lax.psum((col_part, row_part), 'dp')  9.8 us
    slice x1, local copies, waits for them, and re-layouts, on_device(): inputs[:, 0, :]  6.25 us
    gather x1, local copies, waits for them, and re-layouts, on_device(): jnp.take(home_sum, local_rows.reshape(-1), axis=0, mode='clip')  4.68 us
  transfers between devices with their start and end apart: 3, of which 3 were waited for; matrix products, arithmetic and copies ran while one was open for 2% of the time, Pallas kernels for 0%

commit v1 on v0

--- a/solution.py
+++ b/solution.py
@@ -1,6 +1,10 @@
+import functools
+
 import jax
 import jax.numpy as jnp
 from jax import lax
+from jax.experimental import pallas as pl
+from jax.experimental.pallas import tpu as pltpu
 from jax.sharding import PartitionSpec as P
 
 DKV = 64
@@ -34,7 +38,7 @@
     return (slot_row, live_mask)
 
 
-def on_device(head_terms, inputs, owner_list, param_slots, row_state, col_state):
+def general_step(head_terms, inputs, owner_list, param_slots, row_state, col_state):
     dp_count = lax.axis_size("dp")
     my_index = lax.axis_index("dp")
     head_rows = head_terms[:, 0, :]
@@ -85,6 +89,288 @@
     return (new_param[None], (row_val * live_f)[None], new_col[None])
 
 
+PIECES = 2
+EXTRA = 8
+BF16 = jnp.bfloat16
+F32 = jnp.float32
+VMEM_LIMIT = 48 * 1024 * 1024
+
+
+def call(body, out_shape, scratch=(), scalars=1, arrays=0, flops=0, moved=0):
+    return pl.pallas_call(
+        body,
+        out_shape=out_shape,
+        in_specs=[pl.BlockSpec(memory_space=pltpu.SMEM)] * scalars
+        + [pl.BlockSpec(memory_space=pltpu.VMEM)] * arrays,
+        out_specs=jax.tree.map(lambda _: pl.BlockSpec(memory_space=pltpu.VMEM), out_shape),
+        scratch_shapes=list(scratch),
+        compiler_params=pltpu.CompilerParams(vmem_limit_bytes=VMEM_LIMIT),
+        cost_estimate=pl.CostEstimate(flops=flops, bytes_accessed=moved, transcendentals=0),
+    )
+
+
+def iota(shape, dim):
+    return lax.broadcasted_iota(jnp.int32, shape, dim)
+
+
+def prepare(heads, rows, pair_most, place, *refs):
+    first, later = refs[:heads], refs[heads : 2 * heads]
+    split_ref, last_ref, live_ref, state_ref, total_ref = refs[2 * heads :]
+    z = place[0]
+    owners = rows // DKV
+    block = rows // owners
+    slots = owners * pair_most
+    split, cut = rows - DKV, (owners - 1) * pair_most
+    tokens = first[0].shape[1]
+    half = rows // 2
+    owner_rows = [
+        jnp.concatenate([r[rows + 1 : rows + 2, :half], r[rows + 2 : rows + 3, :half]], axis=1)
+        for r in first
+    ]
+    lane = iota((rows, rows), 1)
+    row = iota((rows, rows), 0)
+    earlier = ((row < lane) & (row // block == lane // block)).astype(F32).astype(BF16)
+    named = jnp.concatenate(owner_rows + [jnp.full((8 - heads, rows), -1.0, F32)], axis=0)
+    mine = named == z.astype(F32)
+    before = jnp.dot(mine.astype(F32).astype(BF16), earlier, preferred_element_type=F32)
+    at = iota((8, rows), 1) // block * pair_most
+    slot_of = jnp.where(mine, before + at.astype(F32), -1.0)
+    slot_id = iota((slots, rows), 0).astype(F32)
+    all0, all1 = split + cut, rows - split + slots - cut
+    for m in range(heads):
+        terms = jnp.concatenate([first[m][:rows, :], later[m][:rows, :]], axis=1).astype(BF16)
+        pick = (slot_id == slot_of[m : m + 1, :]).astype(F32)
+        chosen = jnp.dot(pick.astype(BF16), terms, preferred_element_type=F32).astype(BF16)
+        split_ref[m * all0 : m * all0 + split, :] = terms[:split]
+        split_ref[m * all0 + split : (m + 1) * all0, :] = chosen[:cut]
+        last_ref[m * all1 : m * all1 + rows - split, :] = terms[split:]
+        last_ref[m * all1 + rows - split : (m + 1) * all1, :] = chosen[cut:]
+        if m == 0:
+            live_ref[...] = jnp.sum(pick, axis=1, keepdims=True)
+    state = first[0][rows : rows + 1, :slots]
+    same = iota((slots, slots), 0) == iota((slots, slots), 1)
+    state_ref[...] = jnp.sum(jnp.where(same, state, 0.0), axis=1, keepdims=True)
+    owner_of = jnp.where(iota((8, rows), 0) < owners, z ^ iota((8, rows), 0), -1).astype(F32)
+    theirs = (owner_rows[0] == owner_of).astype(F32).astype(BF16)
+    home = (iota((rows, slots), 0) // block == iota((rows, slots), 1) // pair_most).astype(F32)
+    count = jnp.dot(theirs, home.astype(BF16), preferred_element_type=F32)
+    held = (iota((8, slots), 1) % pair_most).astype(F32) < count
+    states = [state] + [
+        later[0][rows : rows + 1, k * tokens : k * tokens + slots] for k in range(owners - 1)
+    ]
+    states = jnp.concatenate(states + [jnp.zeros((8 - owners, slots), F32)], axis=0)
+    states = jnp.where(held, states, 0.0)
+    for i in range(owners):
+        part = jnp.where(iota((8, slots), 1) // pair_most == i, states, 0.0)
+        part = jnp.sum(jnp.sum(part, axis=1, keepdims=True), axis=0, keepdims=True)
+        total_ref[i : i + 1, :] = jnp.broadcast_to(part, (1, slots))
+
+
+def multiply(heads, split, cut, slots, place, split_terms, last_terms, *refs):
+    own, near, one, two, mid, far, one_n, two_n, mid_n, far_n = refs[:10]
+    outs, (held0, held1) = refs[10 : 10 + heads], refs[10 + heads :]
+    tokens = own.shape[0] // 2
+    half = own.shape[1]
+    is_end = place[1] == 1
+
+    def put(k, side, value):
+        value = value.astype(BF16)
+        held0[k * tokens : (k + 1) * tokens, side * half : (side + 1) * half] = value[:tokens]
+        held1[k * tokens : (k + 1) * tokens, side * half : (side + 1) * half] = value[tokens:]
+
+    put(0, 0, own[...])
+    put(0, 1, near[...])
+    put(1, 0, one[...])
+    put(1, 1, one_n[...])
+    put(2, 0, two[...])
+    put(2, 1, two_n[...])
+    put(3, 0, jnp.where(is_end, far[...], mid[...]))
+    put(3, 1, jnp.where(is_end, far_n[...], mid_n[...]))
+    x0, x1 = held0[...], held1[...]
+    all0 = split + cut
+    last = DKV
+    all1 = last + slots - cut
+    for m in range(heads):
+        out = outs[m]
+        g = jnp.dot(split_terms[m * all0 : (m + 1) * all0, :], x0, preferred_element_type=F32)
+        out[:cut, :] = g[split:]
+        for p in range(PROJ - 1):
+            part = g[p * DKV : (p + 1) * DKV]
+            out[slots + p : slots + p + 1, :] = jnp.sum(
+                part * part + EPS_SQUARE, axis=0, keepdims=True
+            )
+        g = jnp.dot(last_terms[m * all1 : (m + 1) * all1, :], x1, preferred_element_type=F32)
+        out[cut:slots, :] = g[last:]
+        part = g[:last]
+        out[slots + PROJ - 1 : slots + PROJ, :] = jnp.sum(
+            part * part + EPS_SQUARE, axis=0, keepdims=True
+        )
+
+
+def update(heads, pieces, pair_most, place, *refs):
+    grads, refs = refs[: heads * pieces], refs[heads * pieces :]
+    params, live_ref, state_ref, total_ref, cols, new_params, new_rows, new_cols = refs
+    chip, core = place[2], place[3]
+    slots, width = params.shape
+    piece = grads[0].shape[1]
+    half = piece // 2
+    square = jnp.zeros((slots, 128), F32)
+    sums = jnp.zeros((PROJ, 128), F32)
+    spans = []
+    for m in range(heads):
+        for p in range(pieces):
+            ref = grads[m * pieces + p]
+            for side in range(2):
+                start = (chip ^ m) * (width // heads) + p * piece + (core ^ side) * half
+                spans.append((ref, side * half, pl.multiple_of(start, 128)))
+    for ref, lo, start in spans:
+        for j in range(0, half, 128):
+            g = ref[:slots, lo + j : lo + j + 128]
+            square += g * g + EPS_SQUARE
+        col_sum = ref[slots : slots + PROJ, lo : lo + half]
+        for j in range(0, half, 128):
+            sums += col_sum[:, j : j + 128]
+        new_cols[:, pl.ds(start, half)] = (
+            DECAY_RATE * cols[:, pl.ds(start, half)] + (1.0 - DECAY_RATE) * col_sum / DKV
+        )
+    row_val = DECAY_RATE * state_ref[...] + (1.0 - DECAY_RATE) * (
+        jnp.sum(square, axis=1, keepdims=True) / width
+    )
+    row_mean = (
+        DECAY_RATE * total_ref[:, :1]
+        + (1.0 - DECAY_RATE) * jnp.sum(sums, axis=1, keepdims=True) / width
+    ) / DKV
+    mean_at = jnp.concatenate(
+        [jnp.broadcast_to(row_mean[i : i + 1], (pair_most, 1)) for i in range(PROJ)], axis=0
+    )
+    live = live_ref[...]
+    row_scale = STEP_SIZE * jnp.sqrt(mean_at / row_val)
+    same = iota((slots, slots), 0) == iota((slots, slots), 1)
+    new_rows[...] = jnp.sum(jnp.where(same, row_val * live, 0.0), axis=0, keepdims=True)
+    for ref, lo, start in spans:
+        col_scale = lax.rsqrt(new_cols[:, pl.ds(start, half)])
+        for i in range(PROJ):
+            rows = slice(i * pair_most, (i + 1) * pair_most)
+            step = ref[rows, lo : lo + half] * row_scale[rows] * col_scale[i : i + 1]
+            value = params[rows, pl.ds(start, half)].astype(F32) - step
+            new_params[rows, pl.ds(start, half)] = jnp.where(live[rows] > 0.0, value, 0.0).astype(
+                BF16
+            )
+
+
+def gather_step(
+    dp_count, shard_count, head_terms, inputs, owner_list, param_slots, row_state, col_state
+):
+    z, s = lax.axis_index("dp"), lax.axis_index("shard")
+    chip, core = s // 2, s % 2
+    is_end = ((z == 0) | (z == dp_count - 1)).astype(jnp.int32)
+    place = jnp.stack([z, is_end, chip, core]).astype(jnp.int32)
+    heads = shard_count // 2
+    tokens, _, width = inputs.shape
+    rows = head_terms.shape[2]
+    slots = param_slots.shape[1]
+    pair_most = slots // dp_count
+    span = width // heads
+    piece = span // PIECES
+    half = piece // 2
+    split, cut = rows - DKV, slots - pair_most
+
+    def move(array, dp_to, shard_to=lambda j: j):
+        pairs = [
+            (i * shard_count + j, dp_to[i] * shard_count + shard_to(j))
+            for i in dp_to
+            for j in range(shard_count)
+        ]
+        return lax.ppermute(array, ("dp", "shard"), pairs)
+
+    every = {i: i for i in range(4)}
+    ends, inner = {0: 0, 3: 3}, {1: 1, 2: 2}
+
+    def along(array):
+        two = move(array, {i: i ^ 2 for i in range(4)})
+        one = move(array, {i: i ^ 1 for i in range(4)})
+        mid = move(array, {1: 2, 2: 1})
+        far = move(two, {1: 0, 2: 3})
+        return one, two, mid, far
+
+    def across(array):
+        return [move(array, every, lambda j, m=m: j ^ (2 * m)) for m in range(1, heads)]
+
+    extra = jnp.concatenate(
+        [
+            row_state,
+            owner_list[0, :, 0].astype(F32).reshape(2, rows // 2),
+            jnp.zeros((EXTRA - 3, tokens), F32),
+        ],
+        axis=0,
+    )
+    terms = jnp.concatenate([head_terms[:, 0, :].T.astype(F32), extra], axis=0)
+    mine = lax.dynamic_slice_in_dim(inputs, chip * span, span, 2)
+
+    def columns(start):
+        part = lax.dynamic_slice_in_dim(mine, start, half, 2)
+        return part.transpose(1, 0, 2).reshape(2 * tokens, half).astype(F32)
+
+    own = [columns(p * piece + core * half) for p in range(PIECES)]
+    near = [columns(p * piece + (1 - core) * half) for p in range(PIECES)]
+
+    one, two, mid, far = along(terms)
+    later = jnp.concatenate([one, two, jnp.where(is_end == 1, far, mid)], axis=1)
+    first_all = [terms] + across(terms)
+    later_all = [later] + across(later)
+    depth = dp_count * tokens
+    split_terms, last_terms, live, state, total = call(
+        functools.partial(prepare, heads, rows, pair_most),
+        [
+            jax.ShapeDtypeStruct((heads * (split + cut), depth), BF16),
+            jax.ShapeDtypeStruct((heads * (rows - split + slots - cut), depth), BF16),
+            jax.ShapeDtypeStruct((slots, 1), F32),
+            jax.ShapeDtypeStruct((slots, 1), F32),
+            jax.ShapeDtypeStruct((PROJ, slots), F32),
+        ],
+        arrays=2 * heads,
+        flops=2 * heads * slots * rows * depth,
+        moved=8 * heads * rows * depth,
+    )(place, *first_all, *later_all)
+
+    grads = []
+    for p in range(PIECES):
+        one, two, mid, far = along(own[p])
+        swap = lambda j: j ^ 1
+        one_n, two_n = move(one, every, swap), move(two, every, swap)
+        mid_n, far_n = move(mid, inner, swap), move(far, ends, swap)
+        outs = call(
+            functools.partial(multiply, heads, split, cut, slots),
+            [jax.ShapeDtypeStruct((slots + EXTRA, piece), F32)] * heads,
+            scratch=[pltpu.VMEM((depth, piece), BF16)] * 2,
+            arrays=12,
+            flops=2 * heads * (rows + slots) * depth * piece,
+            moved=8 * depth * piece,
+        )(place, split_terms, last_terms, own[p], near[p], one, two, mid, far, one_n, two_n, mid_n, far_n)
+        grads.append(
+            [outs[0]] + [move(outs[m], every, lambda j, m=m: j ^ (2 * m)) for m in range(1, heads)]
+        )
+    flat = [grads[p][m] for m in range(heads) for p in range(PIECES)]
+    new_params, new_rows, new_cols = call(
+        functools.partial(update, heads, PIECES, pair_most),
+        [
+            jax.ShapeDtypeStruct((slots, width), BF16),
+            jax.ShapeDtypeStruct((1, slots), F32),
+            jax.ShapeDtypeStruct((PROJ, width), F32),
+        ],
+        arrays=len(flat) + 5,
+        moved=4 * slots * width * 2,
+    )(place, *flat, param_slots[0], live, state, total, col_state[0])
+    return (new_params[None], new_rows, new_cols[None])
+
+
+def one_step(mesh, *args):
+    dp_count, shard_count = mesh.shape["dp"], mesh.shape["shard"]
+    if dp_count == 4 and shard_count == 8:
+        return gather_step(dp_count, shard_count, *args)
+    return general_step(*args)
+
+
 def solution(mesh):
     placed = (
         P("dp", "shard", None),
@@ -95,7 +381,7 @@
         P("shard", None, None),
     )
     return jax.shard_map(
-        on_device,
+        functools.partial(one_step, mesh),
         mesh=mesh,
         in_specs=placed,
         out_specs=(P("shard", "dp", None), P("shard", "dp"), P("shard", None, None)),

time: 212 us -> 111 us (0.52)
  waiting for transfers between devices: 157 us -> 48.4 us
  starting transfers between devices: 4.26 us -> 49.7 us
  between operations: 14.1 us -> 0.91 us
  local copies, waits for them, and re-layouts: 12.2 us -> 1.11 us
  blocking collectives: 9.8 us -> 0 us
  matrix products: 7.99 us -> 0 us
  Pallas kernels: 0 us -> 7.02 us
  other arithmetic: 6.94 us -> 3.58 us
    reduce_scatter x1 -> x0, waiting for transfers between devices: 76.7 us -> none  [on_device(): home_sum = lax.psum_scatter(gradient, 'dp', scatter_dimension=0, tiled=True)]
    ppermute x0 -> x32, starting transfers between devices: none -> 49.7 us  [move(): return lax.ppermute(array, ('dp', 'shard'), pairs)]
    ppermute x0 -> x32, waiting for transfers between devices: none -> 48.4 us  [move(): return lax.ppermute(array, ('dp', 'shard'), pairs)]
    all_to_all x1 -> x0, waiting for transfers between devices: 48.1 us -> none  [on_device(): lax.all_to_all(outgoing, 'dp', split_axis=0, concat_axis=0, tiled=True)]
    psum x1 -> x0, waiting for transfers between devices: 31.7 us -> none  [on_device(): col_sum, row_total = lax.psum((col_part, row_part), 'dp')]
    psum x1 -> x0, blocking collectives: 9.8 us -> none  [on_device(): col_sum, row_total = lax.psum((col_part, row_part), 'dp')]
    dot_general x4 -> x0, matrix products: 7.99 us -> none  [the longest x1 3.45 us: on_device(): col_at = jnp.dot(slot_pick, new_col, precision=lax.Precision.HIGHEST)]
    pallas_call x0 -> x4, Pallas kernels: none -> 7.02 us  [the longest x2 3.4 us: gather_step(): call(functools.partial(multiply, heads, split, cut, slots), [jax.ShapeDty...]
  transfers between devices with their start and end apart: 3 -> 32, of which waited for: 3 -> 11; matrix products, arithmetic and copies ran while one was open for 2% -> 2% of each run, Pallas kernels for 0% -> 4%
where the time goes in v1:
time: 111 us
  starting transfers between devices  49.7 us (45%)
  waiting for transfers between devices  48.4 us (44%)
  Pallas kernels  7.02 us (6%)
  other arithmetic  3.58 us (3%)
  local copies, waits for them, and re-layouts  1.11 us (1%)
    ppermute x32, starting transfers between devices, move(): return lax.ppermute(array, ('dp', 'shard'), pairs)  49.7 us
    ppermute x32, waiting for transfers between devices, move(): return lax.ppermute(array, ('dp', 'shard'), pairs)  48.4 us
    pallas_call x2, Pallas kernels, gather_step(): call(functools.partial(multiply, heads, split, cut, slots), [jax.ShapeDty...  3.4 us
    pallas_call x1, Pallas kernels, gather_step(): call(functools.partial(update, heads, PIECES, pair_most), [jax.ShapeDtype...  2.48 us
  transfers between devices with their start and end apart: 32, of which 11 were waited for; matrix products, arithmetic and copies ran while one was open for 2% of the time, Pallas kernels for 4%

profile of v1, /device:TPU:0, one launch (start us, length us, event | category | flops | bytes accessed | tf_op | source)
XLA Modules:
  0.0 110.7 jit_solution(1379707869961214678)
XLA Ops:
  3.1 4.1 %collective-permute-start.4 = (f32[264,128]{1,0:T(8,128)S(1)}, f32[264,128]{1,0:T(8,128)S(1)}, u32[]{:S(2)}, u32[]{:S(2)}) collective-permute-start(f32[264,128]{1,0:T(8,128)S(1)} %maximum_maximum_fusion.refs_0_), channel_id=1, source_target_pairs={{0,16},{1,17},{2,18},{3,19},{4,20},{5,21},{6,22},{7,23},{8,24},{9,... | collective-permute-start | bytes 405512 | tf_op jit(solution)/shard_map/ppermute | solution.py:284
  7.9 2.9 %collective-permute-start.3 = (f32[264,128]{1,0:T(8,128)S(1)}, f32[264,128]{1,0:T(8,128)S(1)}, u32[]{:S(2)}, u32[]{:S(2)}) collective-permute-start(f32[264,128]{1,0:T(8,128)S(1)} %maximum_maximum_fusion.refs_0_), channel_id=1, source_target_pairs={{0,8},{1,9},{2,10},{3,11},{4,12},{5,13},{6,14},{7,15},{8,0},{9,1},... | collective-permute-start | bytes 405512 | tf_op jit(solution)/shard_map/ppermute | solution.py:284
  10.8 2.4 %collective-permute-start.2 = (f32[264,128]{1,0:T(8,128)S(1)}, f32[264,128]{1,0:T(8,128)S(1)}, u32[]{:S(2)}, u32[]{:S(2)}) collective-permute-start(f32[264,128]{1,0:T(8,128)S(1)} %maximum_maximum_fusion.refs_0_), channel_id=1, source_target_pairs={{0,6},{1,7},{2,4},{3,5},{4,2},{5,3},{6,0},{7,1},{8,14},{9,15},{10,... | collective-permute-start | bytes 405512 | tf_op jit(solution)/shard_map/ppermute | solution.py:284
  15.8 2.0 %convert_bitcast_fusion = (f32[2,128,256]{2,0,1:T(2,128)S(1)}, f32[2,128,256]{2,0,1:T(2,128)S(1)}, f32[2,128,256]{2,0,1:T(2,128)S(1)}, f32[2,128,256]{2,0,1:T(2,128)S(1)}) fusion(bf16[128,2,4096]{2,1,0:T(2,128)(2,1)} %param.7, s32[]{:T(128)S(6)} %dynamic_slice.31, s32[]{:T(128)S(6)} %dynamic_slice.27, s32[]{:T(128)S(6)} %dynamic_slice.25, s32[]{:T(128)S(6)} %dynamic_slice.29), kind=kLoop, calls=%fused_computation.1 | loop fusion | flops 262144 | bytes 1572880 | tf_op jit(solution)/shard_map/convert_element_type | solution.py:312
  17.9 1.9 %collective-permute-start = (f32[264,128]{1,0:T(8,128)S(1)}, f32[264,128]{1,0:T(8,128)S(1)}, u32[]{:S(2)}, u32[]{:S(2)}) collective-permute-start(f32[264,128]{1,0:T(8,128)S(1)} %maximum_maximum_fusion.refs_0_), channel_id=1, source_target_pairs={{0,2},{1,3},{2,0},{3,1},{4,6},{5,7},{6,4},{7,5},{8,10},{9,11},{10,... | collective-permute-start | bytes 405512 | tf_op jit(solution)/shard_map/ppermute | solution.py:284
  20.5 5.4 %collective-permute-start.19 = (f32[256,256]{1,0:T(8,128)S(1)}, f32[256,256]{1,0:T(8,128)S(1)}, u32[]{:S(2)}, u32[]{:S(2)}) collective-permute-start(f32[256,256]{1,0:T(8,128)S(1)} %bitcast.28), channel_id=1, source_target_pairs={{0,16},{1,17},{2,18},{3,19},{4,20},{5,21},{6,22},{7,23},{8,24},{9,... | collective-permute-start | bytes 786440 | tf_op jit(solution)/shard_map/ppermute | solution.py:284
  26.9 4.6 %collective-permute-start.11 = (f32[256,256]{1,0:T(8,128)S(1)}, f32[256,256]{1,0:T(8,128)S(1)}, u32[]{:S(2)}, u32[]{:S(2)}) collective-permute-start(f32[256,256]{1,0:T(8,128)S(1)} %bitcast.32), channel_id=1, source_target_pairs={{0,16},{1,17},{2,18},{3,19},{4,20},{5,21},{6,22},{7,23},{8,24},{9,... | collective-permute-start | bytes 786440 | tf_op jit(solution)/shard_map/ppermute | solution.py:284
  31.5 1.6 %collective-permute-start.9 = (f32[264,384]{1,0:T(8,128)S(1)}, f32[264,384]{1,0:T(8,128)S(1)}, u32[]{:S(2)}, u32[]{:S(2)}) collective-permute-start(f32[264,384]{1,0:T(8,128)S(1)} %pad_maximum_fusion.refs_4_), channel_id=1, source_target_pairs={{0,6},{1,7},{2,4},{3,5},{4,2},{5,3},{6,0},{7,1},{8,14},{9,15},{10,... | collective-permute-start | bytes 1216520 | tf_op jit(solution)/shard_map/ppermute | solution.py:284
  33.0 16.9 %collective-permute-done.19.refs_3_ = f32[256,256]{1,0:T(8,128)S(1)} collective-permute-done((f32[256,256]{1,0:T(8,128)S(1)}, f32[256,256]{1,0:T(8,128)S(1)}, u32[]{:S(2)}, u32[]{:S(2)}) %collective-permute-start.19) | collective-permute-done | bytes 262176 | tf_op jit(solution)/shard_map/ppermute | solution.py:284
  51.9 4.1 %collective-permute-start.10 = (f32[256,256]{1,0:T(8,128)S(1)}, f32[256,256]{1,0:T(8,128)S(1)}, u32[]{:S(2)}, u32[]{:S(2)}) collective-permute-start(f32[256,256]{1,0:T(8,128)S(1)} %bitcast.33), channel_id=1, source_target_pairs={{0,8},{1,9},{2,10},{3,11},{4,12},{5,13},{6,14},{7,15},{8,0},{9,1},... | collective-permute-start | bytes 786440 | tf_op jit(solution)/shard_map/ppermute | solution.py:284
  56.0 3.4 %collective-permute-done.11.refs_3_ = f32[256,256]{1,0:T(8,128)S(1)} collective-permute-done((f32[256,256]{1,0:T(8,128)S(1)}, f32[256,256]{1,0:T(8,128)S(1)}, u32[]{:S(2)}, u32[]{:S(2)}) %collective-permute-start.11) | collective-permute-done | bytes 262176 | tf_op jit(solution)/shard_map/ppermute | solution.py:284
  60.7 4.4 %collective-permute-done.10.refs_2_ = f32[256,256]{1,0:T(8,128)S(1)} collective-permute-done((f32[256,256]{1,0:T(8,128)S(1)}, f32[256,256]{1,0:T(8,128)S(1)}, u32[]{:S(2)}, u32[]{:S(2)}) %collective-permute-start.10) | collective-permute-done | bytes 262176 | tf_op jit(solution)/shard_map/ppermute | solution.py:284
  66.4 4.3 %collective-permute-done.13.refs_5_ = f32[256,256]{1,0:T(8,128)S(1)} collective-permute-done((f32[256,256]{1,0:T(8,128)S(1)}, f32[256,256]{1,0:T(8,128)S(1)}, u32[]{:S(2)}, u32[]{:S(2)}) %collective-permute-start.13) | collective-permute-done | bytes 262176 | tf_op jit(solution)/shard_map/ppermute | solution.py:284
  72.0 2.0 %collective-permute-start.17 = (f32[256,256]{1,0:T(8,128)S(1)}, f32[256,256]{1,0:T(8,128)S(1)}, u32[]{:S(2)}, u32[]{:S(2)}) collective-permute-start(f32[256,256]{1,0:T(8,128)S(1)} %collective-permute-done.13.refs_5_), channel_id=1, source_target_pairs={{0,1},{1,0},{2,3},{3,2},{4,5},{5,4},{6,7},{7,6},{24,25},{25,24},{2... | collective-permute-start | bytes 786440 | tf_op jit(solution)/shard_map/ppermute | solution.py:284
  76.6 2.3 %collective-permute-start.25 = (f32[256,256]{1,0:T(8,128)S(1)}, f32[256,256]{1,0:T(8,128)S(1)}, u32[]{:S(2)}, u32[]{:S(2)}) collective-permute-start(f32[256,256]{1,0:T(8,128)S(1)} %collective-permute-done.21.refs_5_), channel_id=1, source_target_pairs={{0,1},{1,0},{2,3},{3,2},{4,5},{5,4},{6,7},{7,6},{24,25},{25,24},{2... | collective-permute-start | bytes 786440 | tf_op jit(solution)/shard_map/ppermute | solution.py:284
  78.9 1.7 %shard_map.86 = (f32[136,512]{1,0:T(8,128)S(1)}, f32[136,512]{1,0:T(8,128)S(1)}, f32[136,512]{1,0:T(8,128)S(1)}, f32[136,512]{1,0:T(8,128)S(1)}) custom-call(s32[4]{0:T(128)S(1)} %pad_add_fusion.place, bf16[1152,512]{1,0:T(8,128)(2,1)S(1)} %get-tuple-element.19.split_terms, bf16[384,512]{1,0:T(8,128)(2,1)S(1)} %get-tuple-element.20.last_terms, ...), custom_call_target="tpu_custom_call" | custom-call | flops 805306368 | bytes 2097152 | tf_op jit(solution)/shard_map/pallas_call | solution.py:342
  81.2 1.6 %collective-permute-start.28 = (f32[136,512]{1,0:T(8,128)S(1)}, f32[136,512]{1,0:T(8,128)S(1)}, u32[]{:S(2)}, u32[]{:S(2)}) collective-permute-start(f32[136,512]{1,0:T(8,128)S(1)} %get-tuple-element.25), channel_id=1, source_target_pairs={{0,4},{1,5},{2,6},{3,7},{4,0},{5,1},{6,2},{7,3},{8,12},{9,13},{10,... | collective-permute-start | bytes 835592 | tf_op jit(solution)/shard_map/ppermute | solution.py:284
  84.3 1.7 %shard_map.87 = (f32[136,512]{1,0:T(8,128)S(1)}, f32[136,512]{1,0:T(8,128)S(1)}, f32[136,512]{1,0:T(8,128)S(1)}, f32[136,512]{1,0:T(8,128)S(1)}) custom-call(s32[4]{0:T(128)S(1)} %pad_add_fusion.place, bf16[1152,512]{1,0:T(8,128)(2,1)S(1)} %get-tuple-element.19.split_terms, bf16[384,512]{1,0:T(8,128)(2,1)S(1)} %get-tuple-element.20.last_terms, ...), custom_call_target="tpu_custom_call" | custom-call | flops 805306368 | bytes 2097152 | tf_op jit(solution)/shard_map/pallas_call | solution.py:342
  88.1 2.1 %collective-permute-done.26.refs_2_ = f32[136,512]{1,0:T(8,128)S(1)} collective-permute-done((f32[136,512]{1,0:T(8,128)S(1)}, f32[136,512]{1,0:T(8,128)S(1)}, u32[]{:S(2)}, u32[]{:S(2)}) %collective-permute-start.26) | collective-permute-done | bytes 278560 | tf_op jit(solution)/shard_map/ppermute | solution.py:284
  91.7 4.8 %collective-permute-done.28.refs_4_ = f32[136,512]{1,0:T(8,128)S(1)} collective-permute-done((f32[136,512]{1,0:T(8,128)S(1)}, f32[136,512]{1,0:T(8,128)S(1)}, u32[]{:S(2)}, u32[]{:S(2)}) %collective-permute-start.28) | collective-permute-done | bytes 278560 | tf_op jit(solution)/shard_map/ppermute | solution.py:284
  97.1 5.0 %collective-permute-done.27.refs_3_ = f32[136,512]{1,0:T(8,128)S(1)} collective-permute-done((f32[136,512]{1,0:T(8,128)S(1)}, f32[136,512]{1,0:T(8,128)S(1)}, u32[]{:S(2)}, u32[]{:S(2)}) %collective-permute-start.27) | collective-permute-done | bytes 278560 | tf_op jit(solution)/shard_map/ppermute | solution.py:284
  102.2 4.5 %collective-permute-done.29.refs_5_ = f32[136,512]{1,0:T(8,128)S(1)} collective-permute-done((f32[136,512]{1,0:T(8,128)S(1)}, f32[136,512]{1,0:T(8,128)S(1)}, u32[]{:S(2)}, u32[]{:S(2)}) %collective-permute-start.29) | collective-permute-done | bytes 278560 | tf_op jit(solution)/shard_map/ppermute | solution.py:284
  106.6 1.6 %collective-permute-done.31.refs_7_ = f32[136,512]{1,0:T(8,128)S(1)} collective-permute-done((f32[136,512]{1,0:T(8,128)S(1)}, f32[136,512]{1,0:T(8,128)S(1)}, u32[]{:S(2)}, u32[]{:S(2)}) %collective-permute-start.31) | collective-permute-done | bytes 278560 | tf_op jit(solution)/shard_map/ppermute | solution.py:284
  108.2 2.5 %shard_map.88 = (bf16[128,4096]{1,0:T(8,128)(2,1)}, f32[1,128]{1,0:T(1,128)}, f32[4,4096]{1,0:T(4,128)}) custom-call(s32[4]{0:T(128)S(1)} %pad_add_fusion.place, f32[136,512]{1,0:T(8,128)S(1)} %get-tuple-element.21.refs_0_, f32[136,512]{1,0:T(8,128)S(1)} %get-tuple-element.22.refs_1_, f32[136,512]{1,0:T(8,128)S(1)} %collective-permute-done.26.refs_2_, ...), custom_call_target="tpu_custom_call" | custom-call | bytes 4194304 | tf_op jit(solution)/shard_map/pallas_call | solution.py:354
  (62 shorter events, 22.2 us)
Async XLA Ops:
  3.1 11.4 %collective-permute-start.4 = (f32[264,128]{1,0:T(8,128)S(1)}, f32[264,128]{1,0:T(8,128)S(1)}, u32[]{:S(2)}, u32[]{:S(2)}) collective-permute-start(f32[264,128]{1,0:T(8,128)S(1)} %maximum_maximum_fusion.refs_0_), channel_id=1, source_target_pairs={{0,16},{1,17},{2,18},{3,19},{4,20},{5,21},{6,22},{7,23},{8,24},{9,... | collective-permute-start | bytes 405512 | tf_op jit(solution)/shard_map/ppermute | solution.py:284
  7.2 10.7 %collective-permute-start.6 = (f32[264,128]{1,0:T(8,128)S(1)}, f32[264,128]{1,0:T(8,128)S(1)}, u32[]{:S(2)}, u32[]{:S(2)}) collective-permute-start(f32[264,128]{1,0:T(8,128)S(1)} %maximum_maximum_fusion.refs_0_), channel_id=1, source_target_pairs={{8,16},{9,17},{10,18},{11,19},{12,20},{13,21},{14,22},{15,23},{16,... | collective-permute-start | bytes 405512 | tf_op jit(solution)/shard_map/ppermute | solution.py:284
  7.9 11.9 %collective-permute-start.3 = (f32[264,128]{1,0:T(8,128)S(1)}, f32[264,128]{1,0:T(8,128)S(1)}, u32[]{:S(2)}, u32[]{:S(2)}) collective-permute-start(f32[264,128]{1,0:T(8,128)S(1)} %maximum_maximum_fusion.refs_0_), channel_id=1, source_target_pairs={{0,8},{1,9},{2,10},{3,11},{4,12},{5,13},{6,14},{7,15},{8,0},{9,1},... | collective-permute-start | bytes 405512 | tf_op jit(solution)/shard_map/ppermute | solution.py:284
  10.8 9.7 %collective-permute-start.2 = (f32[264,128]{1,0:T(8,128)S(1)}, f32[264,128]{1,0:T(8,128)S(1)}, u32[]{:S(2)}, u32[]{:S(2)}) collective-permute-start(f32[264,128]{1,0:T(8,128)S(1)} %maximum_maximum_fusion.refs_0_), channel_id=1, source_target_pairs={{0,6},{1,7},{2,4},{3,5},{4,2},{5,3},{6,0},{7,1},{8,14},{9,15},{10,... | collective-permute-start | bytes 405512 | tf_op jit(solution)/shard_map/ppermute | solution.py:284
  13.2 12.9 %collective-permute-start.1 = (f32[264,128]{1,0:T(8,128)S(1)}, f32[264,128]{1,0:T(8,128)S(1)}, u32[]{:S(2)}, u32[]{:S(2)}) collective-permute-start(f32[264,128]{1,0:T(8,128)S(1)} %maximum_maximum_fusion.refs_0_), channel_id=1, source_target_pairs={{0,4},{1,5},{2,6},{3,7},{4,0},{5,1},{6,2},{7,3},{8,12},{9,13},{10,... | collective-permute-start | bytes 405512 | tf_op jit(solution)/shard_map/ppermute | solution.py:284
  14.5 11.4 %collective-permute-start.5 = (f32[264,128]{1,0:T(8,128)S(1)}, f32[264,128]{1,0:T(8,128)S(1)}, u32[]{:S(2)}, u32[]{:S(2)}) collective-permute-start(f32[264,128]{1,0:T(8,128)S(1)} %collective-permute-done.4), channel_id=1, source_target_pairs={{8,0},{9,1},{10,2},{11,3},{12,4},{13,5},{14,6},{15,7},{16,24},{17,... | collective-permute-start | bytes 405512 | tf_op jit(solution)/shard_map/ppermute | solution.py:284
  17.9 8.9 %collective-permute-start = (f32[264,128]{1,0:T(8,128)S(1)}, f32[264,128]{1,0:T(8,128)S(1)}, u32[]{:S(2)}, u32[]{:S(2)}) collective-permute-start(f32[264,128]{1,0:T(8,128)S(1)} %maximum_maximum_fusion.refs_0_), channel_id=1, source_target_pairs={{0,2},{1,3},{2,0},{3,1},{4,6},{5,7},{6,4},{7,5},{8,10},{9,11},{10,... | collective-permute-start | bytes 405512 | tf_op jit(solution)/shard_map/ppermute | solution.py:284
  19.8 11.6 %collective-permute-start.20 = (f32[256,256]{1,0:T(8,128)S(1)}, f32[256,256]{1,0:T(8,128)S(1)}, u32[]{:S(2)}, u32[]{:S(2)}) collective-permute-start(f32[256,256]{1,0:T(8,128)S(1)} %bitcast.27), channel_id=1, source_target_pairs={{8,16},{9,17},{10,18},{11,19},{12,20},{13,21},{14,22},{15,23},{16,... | collective-permute-start | bytes 786440 | tf_op jit(solution)/shard_map/ppermute | solution.py:284
  20.5 29.4 %collective-permute-start.19 = (f32[256,256]{1,0:T(8,128)S(1)}, f32[256,256]{1,0:T(8,128)S(1)}, u32[]{:S(2)}, u32[]{:S(2)}) collective-permute-start(f32[256,256]{1,0:T(8,128)S(1)} %bitcast.28), channel_id=1, source_target_pairs={{0,16},{1,17},{2,18},{3,19},{4,20},{5,21},{6,22},{7,23},{8,24},{9,... | collective-permute-start | bytes 786440 | tf_op jit(solution)/shard_map/ppermute | solution.py:284
  25.9 25.5 %collective-permute-start.18 = (f32[256,256]{1,0:T(8,128)S(1)}, f32[256,256]{1,0:T(8,128)S(1)}, u32[]{:S(2)}, u32[]{:S(2)}) collective-permute-start(f32[256,256]{1,0:T(8,128)S(1)} %bitcast.29), channel_id=1, source_target_pairs={{0,8},{1,9},{2,10},{3,11},{4,12},{5,13},{6,14},{7,15},{8,0},{9,1},... | collective-permute-start | bytes 786440 | tf_op jit(solution)/shard_map/ppermute | solution.py:284
  26.2 25.8 %collective-permute-start.12 = (f32[256,256]{1,0:T(8,128)S(1)}, f32[256,256]{1,0:T(8,128)S(1)}, u32[]{:S(2)}, u32[]{:S(2)}) collective-permute-start(f32[256,256]{1,0:T(8,128)S(1)} %bitcast.31), channel_id=1, source_target_pairs={{8,16},{9,17},{10,18},{11,19},{12,20},{13,21},{14,22},{15,23},{16,... | collective-permute-start | bytes 786440 | tf_op jit(solution)/shard_map/ppermute | solution.py:284
  26.9 32.6 %collective-permute-start.11 = (f32[256,256]{1,0:T(8,128)S(1)}, f32[256,256]{1,0:T(8,128)S(1)}, u32[]{:S(2)}, u32[]{:S(2)}) collective-permute-start(f32[256,256]{1,0:T(8,128)S(1)} %bitcast.32), channel_id=1, source_target_pairs={{0,16},{1,17},{2,18},{3,19},{4,20},{5,21},{6,22},{7,23},{8,24},{9,... | collective-permute-start | bytes 786440 | tf_op jit(solution)/shard_map/ppermute | solution.py:284
  31.5 39.9 %collective-permute-start.9 = (f32[264,384]{1,0:T(8,128)S(1)}, f32[264,384]{1,0:T(8,128)S(1)}, u32[]{:S(2)}, u32[]{:S(2)}) collective-permute-start(f32[264,384]{1,0:T(8,128)S(1)} %pad_maximum_fusion.refs_4_), channel_id=1, source_target_pairs={{0,6},{1,7},{2,4},{3,5},{4,2},{5,3},{6,0},{7,1},{8,14},{9,15},{10,... | collective-permute-start | bytes 1216520 | tf_op jit(solution)/shard_map/ppermute | solution.py:284
  49.9 21.6 %collective-permute-start.8 = (f32[264,384]{1,0:T(8,128)S(1)}, f32[264,384]{1,0:T(8,128)S(1)}, u32[]{:S(2)}, u32[]{:S(2)}) collective-permute-start(f32[264,384]{1,0:T(8,128)S(1)} %pad_maximum_fusion.refs_4_), channel_id=1, source_target_pairs={{0,4},{1,5},{2,6},{3,7},{4,0},{5,1},{6,2},{7,3},{8,12},{9,13},{10,... | collective-permute-start | bytes 1216520 | tf_op jit(solution)/shard_map/ppermute | solution.py:284
  51.4 20.6 %collective-permute-start.7 = (f32[264,384]{1,0:T(8,128)S(1)}, f32[264,384]{1,0:T(8,128)S(1)}, u32[]{:S(2)}, u32[]{:S(2)}) collective-permute-start(f32[264,384]{1,0:T(8,128)S(1)} %pad_maximum_fusion.refs_4_), channel_id=1, source_target_pairs={{0,2},{1,3},{2,0},{3,1},{4,6},{5,7},{6,4},{7,5},{8,10},{9,11},{10,... | collective-permute-start | bytes 1216520 | tf_op jit(solution)/shard_map/ppermute | solution.py:284
  51.9 13.2 %collective-permute-start.10 = (f32[256,256]{1,0:T(8,128)S(1)}, f32[256,256]{1,0:T(8,128)S(1)}, u32[]{:S(2)}, u32[]{:S(2)}) collective-permute-start(f32[256,256]{1,0:T(8,128)S(1)} %bitcast.33), channel_id=1, source_target_pairs={{0,8},{1,9},{2,10},{3,11},{4,12},{5,13},{6,14},{7,15},{8,0},{9,1},... | collective-permute-start | bytes 786440 | tf_op jit(solution)/shard_map/ppermute | solution.py:284
  59.4 11.3 %collective-permute-start.13 = (f32[256,256]{1,0:T(8,128)S(1)}, f32[256,256]{1,0:T(8,128)S(1)}, u32[]{:S(2)}, u32[]{:S(2)}) collective-permute-start(f32[256,256]{1,0:T(8,128)S(1)} %collective-permute-done.11.refs_3_), channel_id=1, source_target_pairs={{8,0},{9,1},{10,2},{11,3},{12,4},{13,5},{14,6},{15,7},{16,24},{17,... | collective-permute-start | bytes 786440 | tf_op jit(solution)/shard_map/ppermute | solution.py:284
  65.1 10.1 %collective-permute-start.21 = (f32[256,256]{1,0:T(8,128)S(1)}, f32[256,256]{1,0:T(8,128)S(1)}, u32[]{:S(2)}, u32[]{:S(2)}) collective-permute-start(f32[256,256]{1,0:T(8,128)S(1)} %collective-permute-done.19.refs_3_), channel_id=1, source_target_pairs={{8,0},{9,1},{10,2},{11,3},{12,4},{13,5},{14,6},{15,7},{16,24},{17,... | collective-permute-start | bytes 786440 | tf_op jit(solution)/shard_map/ppermute | solution.py:284
  80.6 9.6 %collective-permute-start.26 = (f32[136,512]{1,0:T(8,128)S(1)}, f32[136,512]{1,0:T(8,128)S(1)}, u32[]{:S(2)}, u32[]{:S(2)}) collective-permute-start(f32[136,512]{1,0:T(8,128)S(1)} %get-tuple-element.23), channel_id=1, source_target_pairs={{0,2},{1,3},{2,0},{3,1},{4,6},{5,7},{6,4},{7,5},{8,10},{9,11},{10,... | collective-permute-start | bytes 835592 | tf_op jit(solution)/shard_map/ppermute | solution.py:284
  81.2 15.2 %collective-permute-start.28 = (f32[136,512]{1,0:T(8,128)S(1)}, f32[136,512]{1,0:T(8,128)S(1)}, u32[]{:S(2)}, u32[]{:S(2)}) collective-permute-start(f32[136,512]{1,0:T(8,128)S(1)} %get-tuple-element.25), channel_id=1, source_target_pairs={{0,4},{1,5},{2,6},{3,7},{4,0},{5,1},{6,2},{7,3},{8,12},{9,13},{10,... | collective-permute-start | bytes 835592 | tf_op jit(solution)/shard_map/ppermute | solution.py:284
  82.8 14.3 %collective-permute-start.30 = (f32[136,512]{1,0:T(8,128)S(1)}, f32[136,512]{1,0:T(8,128)S(1)}, u32[]{:S(2)}, u32[]{:S(2)}) collective-permute-start(f32[136,512]{1,0:T(8,128)S(1)} %get-tuple-element.27), channel_id=1, source_target_pairs={{0,6},{1,7},{2,4},{3,5},{4,2},{5,3},{6,0},{7,1},{8,14},{9,15},{10,... | collective-permute-start | bytes 835592 | tf_op jit(solution)/shard_map/ppermute | solution.py:284
  86.0 16.2 %collective-permute-start.27 = (f32[136,512]{1,0:T(8,128)S(1)}, f32[136,512]{1,0:T(8,128)S(1)}, u32[]{:S(2)}, u32[]{:S(2)}) collective-permute-start(f32[136,512]{1,0:T(8,128)S(1)} %get-tuple-element.24), channel_id=1, source_target_pairs={{0,2},{1,3},{2,0},{3,1},{4,6},{5,7},{6,4},{7,5},{8,10},{9,11},{10,... | collective-permute-start | bytes 835592 | tf_op jit(solution)/shard_map/ppermute | solution.py:284
  86.6 20.1 %collective-permute-start.29 = (f32[136,512]{1,0:T(8,128)S(1)}, f32[136,512]{1,0:T(8,128)S(1)}, u32[]{:S(2)}, u32[]{:S(2)}) collective-permute-start(f32[136,512]{1,0:T(8,128)S(1)} %get-tuple-element.26), channel_id=1, source_target_pairs={{0,4},{1,5},{2,6},{3,7},{4,0},{5,1},{6,2},{7,3},{8,12},{9,13},{10,... | collective-permute-start | bytes 835592 | tf_op jit(solution)/shard_map/ppermute | solution.py:284
  90.2 18.0 %collective-permute-start.31 = (f32[136,512]{1,0:T(8,128)S(1)}, f32[136,512]{1,0:T(8,128)S(1)}, u32[]{:S(2)}, u32[]{:S(2)}) collective-permute-start(f32[136,512]{1,0:T(8,128)S(1)} %get-tuple-element.28), channel_id=1, source_target_pairs={{0,6},{1,7},{2,4},{3,5},{4,2},{5,3},{6,0},{7,1},{8,14},{9,15},{10,... | collective-permute-start | bytes 835592 | tf_op jit(solution)/shard_map/ppermute | solution.py:284
  (10 other events, 98.5 us)

commit v2 on v0

--- a/solution.py
+++ b/solution.py
@@ -1,6 +1,10 @@
+import functools
+
 import jax
 import jax.numpy as jnp
 from jax import lax
+from jax.experimental import pallas as pl
+from jax.experimental.pallas import tpu as pltpu
 from jax.sharding import PartitionSpec as P
 
 DKV = 64
@@ -34,7 +38,7 @@
     return (slot_row, live_mask)
 
 
-def on_device(head_terms, inputs, owner_list, param_slots, row_state, col_state):
+def general_step(head_terms, inputs, owner_list, param_slots, row_state, col_state):
     dp_count = lax.axis_size("dp")
     my_index = lax.axis_index("dp")
     head_rows = head_terms[:, 0, :]
@@ -85,6 +89,413 @@
     return (new_param[None], (row_val * live_f)[None], new_col[None])
 
 
+EXTRA = 8
+CFG = dict(c0=0, c1=1e10, pr=4e10, m0=0, m1=0, ea=0, e=(1, 2), s1=0, s2=0)
+BF16 = jnp.bfloat16
+F32 = jnp.float32
+VMEM_LIMIT = 16 * 1024 * 1024
+BEGIN_LIMIT = 56 * 1024 * 1024
+
+
+def here_of():
+    s = lax.axis_index("shard")
+    return lax.axis_index("dp"), s // 2, s % 2
+
+
+def call(body, out_shape, scratch=(), arrays=0, flops=0, moved=0):
+    return pl.pallas_call(
+        body,
+        out_shape=out_shape,
+        in_specs=[pl.BlockSpec(memory_space=pltpu.VMEM)] * arrays,
+        out_specs=jax.tree.map(lambda _: pl.BlockSpec(memory_space=pltpu.VMEM), out_shape),
+        scratch_shapes=list(scratch),
+        compiler_params=pltpu.CompilerParams(vmem_limit_bytes=VMEM_LIMIT),
+        cost_estimate=pl.CostEstimate(flops=flops, bytes_accessed=moved, transcendentals=0),
+    )
+
+
+def iota(shape, dim):
+    return lax.broadcasted_iota(jnp.int32, shape, dim)
+
+
+def begin(rows, heads_hbm, owner_hbm, state_hbm, terms_ref, heads_ref, owner_ref, state_ref, sems):
+    copies = [
+        pltpu.make_async_copy(heads_hbm, heads_ref, sems.at[0]),
+        pltpu.make_async_copy(owner_hbm, owner_ref, sems.at[1]),
+        pltpu.make_async_copy(state_hbm, state_ref, sems.at[2]),
+    ]
+    for copy in copies:
+        copy.start()
+    for copy in copies:
+        copy.wait()
+    terms_ref[:rows, :] = heads_ref[...].astype(F32).T
+    terms_ref[rows : rows + 1, :] = state_ref[...]
+    named = owner_ref[...].astype(F32)
+    terms_ref[rows + 1 : rows + 2, :] = named[:, : rows // 2]
+    terms_ref[rows + 2 : rows + 3, :] = named[:, rows // 2 :]
+    terms_ref[rows + 3 :, :] = jnp.zeros((terms_ref.shape[0] - rows - 3, terms_ref.shape[1]), F32)
+
+
+def columns(inputs_hbm, *refs):
+    *outs, inputs_ref, sem = refs
+    _, chip, core = here_of()
+    half = outs[0].shape[1]
+    span = 2 * half
+    some = pl.ds(pl.multiple_of(chip * span, 128), span)
+    copy = pltpu.make_async_copy(inputs_hbm.at[:, :, some], inputs_ref, sem)
+    copy.start()
+    copy.wait()
+    for c in range(2):
+        for side in range(2):
+            at = pl.multiple_of((core ^ side) * half, 128)
+            outs[2 * c + side][...] = inputs_ref[:, c, pl.ds(at, half)].astype(F32)
+
+
+def spread(*refs):
+    *blocks, out_ref = refs
+    at = 0
+    for block in blocks:
+        value = block[...]
+        for j in range(out_ref.shape[0]):
+            out_ref[j, :, at : at + value.shape[1]] = value
+        at += value.shape[1]
+
+
+def collect(up1, down1, up2, down2, up3, down3, out_ref):
+    z, _, _ = here_of()
+    tokens = up1.shape[0]
+    out_ref[:tokens, :] = jnp.where(z >= 1, up1[...], down3[...])
+    out_ref[tokens : 2 * tokens, :] = jnp.where(z <= 2, down1[...], up3[...])
+    out_ref[2 * tokens :, :] = jnp.where(z <= 1, down2[...], up2[...])
+
+
+def prepare(heads, rows, pair_most, *refs):
+    *parts, split_ref, last_ref, live_ref, state_ref, total_ref = refs
+    z, chip, _ = here_of()
+    owners = rows // DKV
+    tokens = sum(part.shape[2] for part in parts) // owners
+    block = rows // owners
+    slots = owners * pair_most
+    split, cut = rows - DKV, (owners - 1) * pair_most
+    half = rows // 2
+
+    def owner_row(m):
+        at = chip ^ m
+        return jnp.concatenate(
+            [parts[0][at, rows + 1 : rows + 2, :half], parts[0][at, rows + 2 : rows + 3, :half]], axis=1
+        )
+
+    lane = iota((rows, rows), 1)
+    row = iota((rows, rows), 0)
+    earlier = ((row < lane) & (row // block == lane // block)).astype(F32).astype(BF16)
+    named = jnp.concatenate(
+        [owner_row(m) for m in range(heads)] + [jnp.full((8 - heads, rows), -1.0, F32)], axis=0
+    )
+    mine = named == z.astype(F32)
+    before = jnp.dot(mine.astype(F32).astype(BF16), earlier, preferred_element_type=F32)
+    at = iota((8, rows), 1) // block * pair_most
+    slot_of = jnp.where(mine, before + at.astype(F32), -1.0)
+    slot_id = iota((slots, rows), 0).astype(F32)
+    all0, all1 = split + cut, rows - split + slots - cut
+    for m in range(heads):
+        terms = jnp.concatenate([part[chip ^ m, :rows, :] for part in parts], axis=1).astype(BF16)
+        pick = (slot_id == slot_of[m : m + 1, :]).astype(F32)
+        chosen = jnp.dot(pick.astype(BF16), terms, preferred_element_type=F32).astype(BF16)
+        split_ref[m * all0 : m * all0 + split, :] = terms[:split]
+        split_ref[m * all0 + split : (m + 1) * all0, :] = chosen[:cut]
+        last_ref[m * all1 : m * all1 + rows - split, :] = terms[split:]
+        last_ref[m * all1 + rows - split : (m + 1) * all1, :] = chosen[cut:]
+        if m == 0:
+            live_ref[...] = jnp.sum(pick, axis=1, keepdims=True)
+    state = parts[0][chip, rows : rows + 1, :slots]
+    same = iota((slots, slots), 0) == iota((slots, slots), 1)
+    state_ref[...] = jnp.sum(jnp.where(same, state, 0.0), axis=1, keepdims=True)
+    owner_of = jnp.where(
+        iota((8, rows), 0) == 0,
+        z,
+        jnp.where(
+            iota((8, rows), 0) == 1,
+            (z + owners - 1) % owners,
+            jnp.where(iota((8, rows), 0) == 2, (z + 1) % owners, (z + 2) % owners),
+        ),
+    ).astype(F32)
+    theirs = (owner_row(0) == owner_of).astype(F32).astype(BF16)
+    home = (iota((rows, slots), 0) // block == iota((rows, slots), 1) // pair_most).astype(F32)
+    count = jnp.dot(theirs, home.astype(BF16), preferred_element_type=F32)
+    held = (iota((8, slots), 1) % pair_most).astype(F32) < count
+    states = [
+        part[chip, rows : rows + 1, k : k + slots]
+        for part in parts
+        for k in range(0, part.shape[2], tokens)
+    ]
+    states = jnp.concatenate(states + [jnp.zeros((8 - owners, slots), F32)], axis=0)
+    states = jnp.where(held, states, 0.0)
+    for i in range(owners):
+        part = jnp.where(iota((8, slots), 1) // pair_most == i, states, 0.0)
+        part = jnp.sum(jnp.sum(part, axis=1, keepdims=True), axis=0, keepdims=True)
+        total_ref[i : i + 1, :] = jnp.broadcast_to(part, (1, slots))
+
+
+def multiply(heads, projections, slots, terms, own, near, here, there, *refs):
+    *refs, held = refs
+    sums_ref, outs = (refs[-1], refs[:-1]) if projections > 1 else (refs[0], refs[1:])
+    tokens, half = own.shape
+    sides = [
+        [own[...]] + [here[k * tokens : (k + 1) * tokens, :] for k in range(3)],
+        [near[...]] + [there[k * tokens : (k + 1) * tokens, :] for k in range(3)],
+    ]
+    for side, values in enumerate(sides):
+        for k, value in enumerate(values):
+            held[k * tokens : (k + 1) * tokens, side * half : (side + 1) * half] = value.astype(BF16)
+    x = held[...]
+    each = projections * DKV + slots
+    for m in range(heads):
+        g = jnp.dot(terms[m * each : (m + 1) * each, :], x, preferred_element_type=F32)
+        outs[m][:slots, :] = g[projections * DKV :]
+        for p in range(projections):
+            part = g[p * DKV : (p + 1) * DKV]
+            sums = jnp.sum(part * part + EPS_SQUARE, axis=0, keepdims=True)
+            if projections > 1:
+                sums_ref[m, p : p + 1, :] = sums
+            else:
+                outs[m][slots + PROJ - 1 : slots + PROJ, :] = sums
+        if projections == 1:
+            outs[m][slots : slots + PROJ - 1, :] = sums_ref[m, : PROJ - 1, :]
+
+
+def spans_of(refs, width):
+    _, chip, core = here_of()
+    heads = len(refs)
+    span = width // heads
+    half = span // 2
+    return [
+        (refs[m], side * half, pl.multiple_of((chip ^ m) * span + (core ^ side) * half, 128))
+        for m in range(heads)
+        for side in range(2)
+    ], half
+
+
+def squares(refs, count):
+    square = jnp.zeros((count, 128), F32)
+    for ref in refs:
+        for j in range(0, ref.shape[1], 128):
+            g = ref[:count, j : j + 128]
+            square += g * g + EPS_SQUARE
+    return jnp.sum(square, axis=1, keepdims=True)
+
+
+def early(*refs):
+    *first, square_ref = refs
+    square_ref[...] = squares(first, square_ref.shape[0])
+
+
+def update(heads, pair_most, *refs):
+    first, last, refs = refs[:heads], refs[heads : 2 * heads], refs[2 * heads :]
+    square0, params, live_ref, state_ref, total_ref, cols, new_params, new_rows, new_cols = refs
+    slots, width = params.shape
+    cut = (PROJ - 1) * pair_most
+    rest = slots - cut
+    sums = jnp.zeros((PROJ, 128), F32)
+    spans, half = spans_of(last, width)
+    for ref, lo, start in spans:
+        col_sum = ref[rest : rest + PROJ, lo : lo + half]
+        for j in range(0, half, 128):
+            sums += col_sum[:, j : j + 128]
+        new_cols[:, pl.ds(start, half)] = (
+            DECAY_RATE * cols[:, pl.ds(start, half)] + (1.0 - DECAY_RATE) * col_sum / DKV
+        )
+    square = jnp.concatenate([square0[...], squares(last, rest)], axis=0)
+    row_val = DECAY_RATE * state_ref[...] + (1.0 - DECAY_RATE) * (square / width)
+    row_mean = (
+        DECAY_RATE * total_ref[:, :1]
+        + (1.0 - DECAY_RATE) * jnp.sum(sums, axis=1, keepdims=True) / width
+    ) / DKV
+    mean_at = jnp.concatenate(
+        [jnp.broadcast_to(row_mean[i : i + 1], (pair_most, 1)) for i in range(PROJ)], axis=0
+    )
+    live = live_ref[...]
+    row_scale = STEP_SIZE * jnp.sqrt(mean_at / row_val)
+    same = iota((slots, slots), 0) == iota((slots, slots), 1)
+    new_rows[...] = jnp.sum(jnp.where(same, row_val * live, 0.0), axis=0, keepdims=True)
+    for m, (_, lo, start) in zip([m for m in range(heads) for _ in range(2)], spans):
+        col_scale = lax.rsqrt(new_cols[:, pl.ds(start, half)])
+        for i in range(PROJ):
+            rows = slice(i * pair_most, (i + 1) * pair_most)
+            ref, k = (first[m], i) if i < PROJ - 1 else (last[m], 0)
+            g = ref[k * pair_most : (k + 1) * pair_most, lo : lo + half]
+            value = params[rows, pl.ds(start, half)].astype(F32) - g * row_scale[rows] * (
+                col_scale[i : i + 1]
+            )
+            new_params[rows, pl.ds(start, half)] = jnp.where(live[rows] > 0.0, value, 0.0).astype(
+                BF16
+            )
+
+
+def gather_step(
+    dp_count, shard_count, head_terms, inputs, owner_list, param_slots, row_state, col_state
+):
+    heads = shard_count // 2
+    tokens, _, width = inputs.shape
+    rows = head_terms.shape[2]
+    slots = param_slots.shape[1]
+    pair_most = slots // dp_count
+    span = width // heads
+    half = span // 2
+    split, cut = rows - DKV, slots - pair_most
+    depth = dp_count * tokens
+
+    def move(array, dp_to, shard_to=lambda j: j):
+        pairs = [
+            (i * shard_count + j, dp_to[i] * shard_count + shard_to(j))
+            for i in dp_to
+            for j in range(shard_count)
+        ]
+        return lax.ppermute(array, ("dp", "shard"), pairs)
+
+    every = {i: i for i in range(4)}
+    upward, downward = {i: i + 1 for i in range(3)}, {i + 1: i for i in range(3)}
+    swap = lambda j: j ^ 1
+
+    anywhere = pl.BlockSpec(memory_space=pl.ANY)
+    in_vmem = pl.BlockSpec(memory_space=pltpu.VMEM)
+    terms = pl.pallas_call(
+        functools.partial(begin, rows),
+        out_shape=jax.ShapeDtypeStruct((rows + EXTRA, tokens), F32),
+        in_specs=[anywhere] * 3,
+        out_specs=in_vmem,
+        scratch_shapes=[
+            pltpu.VMEM((tokens, rows), BF16),
+            pltpu.VMEM((1, rows), jnp.int32),
+            pltpu.VMEM((1, tokens), F32),
+            pltpu.SemaphoreType.DMA((3,)),
+        ],
+        compiler_params=pltpu.CompilerParams(vmem_limit_bytes=BEGIN_LIMIT),
+    )(head_terms[:, 0, :], owner_list[:, :, 0], row_state)
+    own0, near0, own1, near1 = pl.pallas_call(
+        columns,
+        out_shape=[jax.ShapeDtypeStruct((tokens, half), F32)] * 4,
+        in_specs=[anywhere],
+        out_specs=[in_vmem] * 4,
+        scratch_shapes=[pltpu.VMEM((tokens, 2, span), BF16), pltpu.SemaphoreType.DMA(())],
+        compiler_params=pltpu.CompilerParams(vmem_limit_bytes=BEGIN_LIMIT),
+    )(inputs)
+
+    def after(array, *others):
+        return lax.optimization_barrier((array, *others))[0] if others else array
+
+    chips = [[2 * i + c for i in range(heads)] for c in range(2)]
+    ring = lambda k: {i: (i + k) % dp_count for i in range(dp_count)}
+    edges = CFG["e"]
+
+    def edge(k, array, *others):
+        return after(array, *others) if k in edges else array
+
+    def exchange(*blocks):
+        size = sum(block.shape[1] for block in blocks)
+        everywhere = call(
+            spread,
+            jax.ShapeDtypeStruct((heads, rows + EXTRA, size), F32),
+            arrays=len(blocks),
+        )(*blocks)
+        return lax.all_to_all(everywhere, "shard", 0, 0, axis_index_groups=chips)
+
+    def joined(cost, *arrays):
+        here = call(
+            collect,
+            jax.ShapeDtypeStruct((3 * tokens, half), F32),
+            arrays=6,
+            flops=int(cost),
+        )(*arrays)
+        return here, move(here, every, swap)
+
+    def product(cost, terms, projections, count, *blocks):
+        shapes = [jax.ShapeDtypeStruct((count if projections > 1 else count + EXTRA, span), F32)] * heads
+        if projections > 1:
+            shapes.append(jax.ShapeDtypeStruct((heads, 8, span), F32))
+        return call(
+            functools.partial(multiply, heads, projections, count),
+            shapes,
+            scratch=[pltpu.VMEM((depth, span), BF16)],
+            arrays=1 + len(blocks),
+            flops=int(cost),
+        )(terms, *blocks)
+
+    def scatter(outs):
+        return [
+            out if m == 0 else move(out, every, lambda j, m=m: j ^ (2 * m))
+            for m, out in enumerate(outs)
+        ]
+
+    up1, down1 = move(own0, upward), move(own0, downward)
+    ha, hb, hc = [move(terms, ring(k)) for k in (1, dp_count - 1, 2)]
+    if CFG["s1"] == 0:
+        parts = [exchange(terms, ha, hb, edge(3, hc, up1, down1))]
+    elif CFG["s1"] == 1:
+        parts = [exchange(terms, ha, hb)]
+        parts.append(exchange(edge(3, hc, up1, down1)))
+    elif CFG["s1"] == 2:
+        parts = [exchange(terms)]
+        parts.append(exchange(ha, hb, edge(3, edge(11, hc, parts[0]), up1, down1)))
+    else:
+        parts = [exchange(terms, ha)]
+        parts.append(exchange(hb, edge(3, hc, up1, down1)))
+    up2, down2 = move(edge(1, up1, ha), upward), move(edge(1, down1, hb), downward)
+    x1 = edge(5, edge(2, own1, hc), up1, down1)
+    x1 = edge(12, x1, up2, down2)
+    nup1, ndown1 = move(x1, upward), move(x1, downward)
+    up3 = move(edge(4, up2, nup1), upward)
+    down3 = move(edge(4, down2, ndown1), downward)
+    here0, there0 = joined(CFG["c0"], up1, down1, up2, down2, up3, down3)
+    nup2, ndown2 = move(edge(6, nup1, up2), upward), move(edge(6, ndown1, down2), downward)
+    parts[0] = edge(13, parts[0], there0)
+    split_terms, last_terms, live, state, total = call(
+        functools.partial(prepare, heads, rows, pair_most),
+        [
+            jax.ShapeDtypeStruct((heads * (split + cut), depth), BF16),
+            jax.ShapeDtypeStruct((heads * (rows - split + slots - cut), depth), BF16),
+            jax.ShapeDtypeStruct((slots, 1), F32),
+            jax.ShapeDtypeStruct((slots, 1), F32),
+            jax.ShapeDtypeStruct((PROJ, slots), F32),
+        ],
+        arrays=len(parts),
+        flops=int(CFG["pr"]),
+    )(*parts)
+    here0 = edge(9, here0, nup2, ndown2)
+    *outs, sums0 = product(CFG["m0"], split_terms, PROJ - 1, cut, own0, near0, here0, there0)
+    first = scatter(outs)
+    nup3 = move(edge(14, edge(7, nup2, outs[0]), there0), upward)
+    ndown3 = move(edge(14, edge(7, ndown2, outs[0]), there0), downward)
+    nup1 = edge(10, edge(8, nup1, first[1]), outs[0])
+    here1, there1 = joined(CFG["c1"], nup1, ndown1, nup2, ndown2, nup3, ndown3)
+    last = scatter(
+        product(CFG["m1"], last_terms, 1, slots - cut, own1, near1, here1, there1, sums0)
+    )
+    square0 = call(
+        early,
+        jax.ShapeDtypeStruct((cut, 1), F32),
+        arrays=heads,
+        flops=int(CFG["ea"]),
+    )(*first)
+    new_params, new_rows, new_cols = call(
+        functools.partial(update, heads, pair_most),
+        [
+            jax.ShapeDtypeStruct((slots, width), BF16),
+            jax.ShapeDtypeStruct((1, slots), F32),
+            jax.ShapeDtypeStruct((PROJ, width), F32),
+        ],
+        arrays=2 * heads + 6,
+        moved=4 * slots * width * 2,
+    )(*first, *last, square0, param_slots[0], live, state, total, col_state[0])
+    return (new_params[None], new_rows, new_cols[None])
+
+
+def one_step(mesh, *args):
+    dp_count, shard_count = mesh.shape["dp"], mesh.shape["shard"]
+    if dp_count == 4 and shard_count == 8:
+        return gather_step(dp_count, shard_count, *args)
+    return general_step(*args)
+
+
 def solution(mesh):
     placed = (
         P("dp", "shard", None),
@@ -95,7 +506,7 @@
         P("shard", None, None),
     )
     return jax.shard_map(
-        on_device,
+        functools.partial(one_step, mesh),
         mesh=mesh,
         in_specs=placed,
         out_specs=(P("shard", "dp", None), P("shard", "dp"), P("shard", None, None)),

time: 212 us -> 94.1 us (0.44)
  waiting for transfers between devices: 157 us -> 24.3 us
  starting transfers between devices: 4.26 us -> 52.8 us
  Pallas kernels: 0 us -> 13.6 us
  between operations: 14.1 us -> 0.94 us
  local copies, waits for them, and re-layouts: 12.2 us -> 1.86 us
  blocking collectives: 9.8 us -> 0 us
  matrix products: 7.99 us -> 0 us
  other arithmetic: 6.94 us -> 0 us
    reduce_scatter x1 -> x0, waiting for transfers between devices: 76.7 us -> none  [on_device(): home_sum = lax.psum_scatter(gradient, 'dp', scatter_dimension=0, tiled=True)]
    ppermute x0 -> x23, starting transfers between devices: none -> 49 us  [move(): return lax.ppermute(array, ('dp', 'shard'), pairs)]
    all_to_all x1, waiting for transfers between devices: 48.1 us -> 0.01 us  [exchange(): return lax.all_to_all(everywhere, 'shard', 0, 0, axis_index_groups=chips)]
    psum x1 -> x0, waiting for transfers between devices: 31.7 us -> none  [on_device(): col_sum, row_total = lax.psum((col_part, row_part), 'dp')]
    ppermute x0 -> x23, waiting for transfers between devices: none -> 24.3 us  [move(): return lax.ppermute(array, ('dp', 'shard'), pairs)]
    pallas_call x0 -> x10, Pallas kernels: none -> 13.6 us  [the longest x2 4.7 us: product(): call(functools.partial(multiply, heads, projections, count), shapes, scra...]
    psum x1 -> x0, blocking collectives: 9.8 us -> none  [on_device(): col_sum, row_total = lax.psum((col_part, row_part), 'dp')]
    dot_general x4 -> x0, matrix products: 7.99 us -> none  [the longest x1 3.45 us: on_device(): col_at = jnp.dot(slot_pick, new_col, precision=lax.Precision.HIGHEST)]
  transfers between devices with their start and end apart: 3 -> 24, of which waited for: 3 -> 7; matrix products, arithmetic and copies ran while one was open for 2% -> 0% of each run, Pallas kernels for 0% -> 11%
where the time goes in v2:
time: 94.1 us; the launch traced here: 93.5 us
  starting transfers between devices  52.8 us (56%)
  waiting for transfers between devices  24.3 us (26%)
  Pallas kernels  13.6 us (14%)
  local copies, waits for them, and re-layouts  1.86 us (2%)
    ppermute x23, starting transfers between devices, move(): return lax.ppermute(array, ('dp', 'shard'), pairs)  49 us
    ppermute x23, waiting for transfers between devices, move(): return lax.ppermute(array, ('dp', 'shard'), pairs)  24.3 us
    pallas_call x2, Pallas kernels, product(): call(functools.partial(multiply, heads, projections, count), shapes, scra...  4.7 us
    all_to_all x1, starting transfers between devices, exchange(): return lax.all_to_all(everywhere, 'shard', 0, 0, axis_index_groups=chips)  3.72 us
    pallas_call x1, Pallas kernels, gather_step(): pl.pallas_call(columns, out_shape=[jax.ShapeDtypeStruct((tokens, half), F...  2.11 us
  transfers between devices with their start and end apart: 24, of which 7 were waited for; matrix products, arithmetic and copies ran while one was open for 0% of the time, Pallas kernels for 11%

profile of v2, /device:TPU:0, one launch (start us, length us, event | category | flops | bytes accessed | tf_op | source)
XLA Modules:
  0.0 93.5 jit_solution(14303844297768544904)
XLA Ops:
  0.6 1.6 %shard_map.85.refs_0_ = f32[264,128]{1,0:T(8,128)} custom-call(bf16[128,256]{1,0:T(8,128)(2,1)} %bitcast.8, s32[1,256]{1,0:T(1,128)} %bitcast.9, f32[1,128]{1,0:T(1,128)} %state_hbm.1), custom_call_target="tpu_custom_call" | custom-call | tf_op jit(solution)/shard_map/pallas_call | solution.py:361
  2.3 4.1 %collective-permute-start.2 = (f32[264,128]{1,0:T(8,128)}, f32[264,128]{1,0:T(8,128)S(1)}, u32[]{:S(2)}, u32[]{:S(2)}) collective-permute-start(f32[264,128]{1,0:T(8,128)} %shard_map.85.refs_0_), channel_id=1, source_target_pairs={{0,16},{1,17},{2,18},{3,19},{4,20},{5,21},{6,22},{7,23},{8,24},{9,... | collective-permute-start | bytes 405512 | tf_op jit(solution)/shard_map/ppermute | solution.py:353
  6.4 1.6 %collective-permute-start = (f32[264,128]{1,0:T(8,128)}, f32[264,128]{1,0:T(8,128)S(1)}, u32[]{:S(2)}, u32[]{:S(2)}) collective-permute-start(f32[264,128]{1,0:T(8,128)} %shard_map.85.refs_0_), channel_id=1, source_target_pairs={{0,8},{1,9},{2,10},{3,11},{4,12},{5,13},{6,14},{7,15},{8,16},{9,17... | collective-permute-start | bytes 405512 | tf_op jit(solution)/shard_map/ppermute | solution.py:353
  8.0 2.2 %collective-permute-start.1 = (f32[264,128]{1,0:T(8,128)}, f32[264,128]{1,0:T(8,128)S(1)}, u32[]{:S(2)}, u32[]{:S(2)}) collective-permute-start(f32[264,128]{1,0:T(8,128)} %shard_map.85.refs_0_), channel_id=1, source_target_pairs={{0,24},{1,25},{2,26},{3,27},{4,28},{5,29},{6,30},{7,31},{8,0},{9,1... | collective-permute-start | bytes 405512 | tf_op jit(solution)/shard_map/ppermute | solution.py:353
  10.2 2.1 %shard_map.88 = (f32[128,512]{1,0:T(8,128)}, f32[128,512]{1,0:T(8,128)}, f32[128,512]{1,0:T(8,128)}, f32[128,512]{1,0:T(8,128)}) custom-call(bf16[128,2,4096]{2,1,0:T(2,128)(2,1)} %inputs_hbm.1), custom_call_target="tpu_custom_call" | custom-call | tf_op jit(solution)/shard_map/pallas_call | solution.py:374
  12.3 1.7 %collective-permute-start.3 = (f32[128,512]{1,0:T(8,128)}, f32[128,512]{1,0:T(8,128)S(1)}, u32[]{:S(2)}, u32[]{:S(2)}) collective-permute-start(f32[128,512]{1,0:T(8,128)} %get-tuple-element.28.own), channel_id=1, source_target_pairs={{0,8},{1,9},{2,10},{3,11},{4,12},{5,13},{6,14},{7,15},{8,16},{9,17... | collective-permute-start | bytes 786440 | tf_op jit(solution)/shard_map/ppermute | solution.py:353
  16.8 3.1 %collective-permute-start.13 = (f32[128,512]{1,0:T(8,128)}, f32[128,512]{1,0:T(8,128)S(1)}, u32[]{:S(2)}, u32[]{:S(2)}) collective-permute-start(f32[128,512]{1,0:T(8,128)} %get-tuple-element.39.own), channel_id=1, source_target_pairs={{0,8},{1,9},{2,10},{3,11},{4,12},{5,13},{6,14},{7,15},{8,16},{9,17... | collective-permute-start | bytes 786440 | tf_op jit(solution)/shard_map/ppermute | solution.py:353
  21.2 1.7 %shard_map.86 = f32[4,264,512]{2,1,0:T(8,128)} custom-call(f32[264,128]{1,0:T(8,128)S(1)} %copy-done.1, f32[264,128]{1,0:T(8,128)S(1)} %collective-permute-done.refs_1_, f32[264,128]{1,0:T(8,128)S(1)} %collective-permute-done.1.refs_2_, f32[264,128]{1,0:T(8,128)S(1)} %collective-permute-done.2.refs_3_), custom_call_target="tpu_custom_call" | custom-call | tf_op jit(solution)/shard_map/pallas_call | solution.py:395
  22.9 3.7 %all-to-all-start = ((f32[4,264,512]{2,1,0:T(8,128)}), f32[4,264,512]{2,1,0:T(8,128)S(1)}, u32[]{:S(2)}, u32[]{:S(2)}) async-start(f32[4,264,512]{2,1,0:T(8,128)} %shard_map.86), calls=%async_computation | async-start | bytes 4325376 | tf_op jit(solution)/shard_map/all_to_all | solution.py:400
  26.6 4.6 %collective-permute-start.5 = (f32[128,512]{1,0:T(8,128)S(1)}, f32[128,512]{1,0:T(8,128)S(1)}, u32[]{:S(2)}, u32[]{:S(2)}) collective-permute-start(f32[128,512]{1,0:T(8,128)S(1)} %collective-permute-done.3.up1), channel_id=1, source_target_pairs={{0,8},{1,9},{2,10},{3,11},{4,12},{5,13},{6,14},{7,15},{8,16},{9,17... | collective-permute-start | bytes 786440 | tf_op jit(solution)/shard_map/ppermute | solution.py:353
  32.5 4.6 %collective-permute-start.15 = (f32[128,512]{1,0:T(8,128)S(1)}, f32[128,512]{1,0:T(8,128)S(1)}, u32[]{:S(2)}, u32[]{:S(2)}) collective-permute-start(f32[128,512]{1,0:T(8,128)S(1)} %collective-permute-done.13.up1), channel_id=1, source_target_pairs={{0,8},{1,9},{2,10},{3,11},{4,12},{5,13},{6,14},{7,15},{8,16},{9,17... | collective-permute-start | bytes 786440 | tf_op jit(solution)/shard_map/ppermute | solution.py:353
  39.9 4.7 %collective-permute-start.7 = (f32[128,512]{1,0:T(8,128)S(1)}, f32[128,512]{1,0:T(8,128)S(1)}, u32[]{:S(2)}, u32[]{:S(2)}) collective-permute-start(f32[128,512]{1,0:T(8,128)S(1)} %collective-permute-done.5.up2), channel_id=1, source_target_pairs={{0,8},{1,9},{2,10},{3,11},{4,12},{5,13},{6,14},{7,15},{8,16},{9,17... | collective-permute-start | bytes 786440 | tf_op jit(solution)/shard_map/ppermute | solution.py:353
  45.9 4.6 %collective-permute-start.17 = (f32[128,512]{1,0:T(8,128)S(1)}, f32[128,512]{1,0:T(8,128)S(1)}, u32[]{:S(2)}, u32[]{:S(2)}) collective-permute-start(f32[128,512]{1,0:T(8,128)S(1)} %collective-permute-done.15.up2), channel_id=1, source_target_pairs={{0,8},{1,9},{2,10},{3,11},{4,12},{5,13},{6,14},{7,15},{8,16},{9,17... | collective-permute-start | bytes 786440 | tf_op jit(solution)/shard_map/ppermute | solution.py:353
  51.8 2.6 %collective-permute-done.8.down3 = f32[128,512]{1,0:T(8,128)S(1)} collective-permute-done((f32[128,512]{1,0:T(8,128)S(1)}, f32[128,512]{1,0:T(8,128)S(1)}, u32[]{:S(2)}, u32[]{:S(2)}) %collective-permute-start.8) | collective-permute-done | bytes 262176 | tf_op jit(solution)/shard_map/ppermute | solution.py:353
  54.5 4.2 %collective-permute-done.18.down3 = f32[128,512]{1,0:T(8,128)S(1)} collective-permute-done((f32[128,512]{1,0:T(8,128)S(1)}, f32[128,512]{1,0:T(8,128)S(1)}, u32[]{:S(2)}, u32[]{:S(2)}) %collective-permute-start.18) | collective-permute-done | bytes 262176 | tf_op jit(solution)/shard_map/ppermute | solution.py:353
  60.8 2.5 %shard_map.90 = (f32[96,1024]{1,0:T(8,128)S(1)}, f32[96,1024]{1,0:T(8,128)S(1)}, f32[96,1024]{1,0:T(8,128)S(1)}, f32[96,1024]{1,0:T(8,128)S(1)}, f32[4,8,1024]{2,1,0:T(8,128)S(1)}) custom-call(bf16[1152,512]{1,0:T(8,128)(2,1)S(1)} %get-tuple-element.27.terms, f32[128,512]{1,0:T(8,128)S(1)} %copy-done.4, f32[128,512]{1,0:T(8,128)S(1)} %copy-done.5, ...), custom_call_target="tpu_custom_call" | custom-call | tf_op jit(solution)/shard_map/pallas_call | solution.py:415
  63.3 2.1 %collective-permute-start.10 = (f32[96,1024]{1,0:T(8,128)S(1)}, f32[96,1024]{1,0:T(8,128)S(1)}, u32[]{:S(2)}, u32[]{:S(2)}) collective-permute-start(f32[96,1024]{1,0:T(8,128)S(1)} %get-tuple-element.33), channel_id=1, source_target_pairs={{0,2},{1,3},{2,0},{3,1},{4,6},{5,7},{6,4},{7,5},{8,10},{9,11},{10,... | collective-permute-start | bytes 1179656 | tf_op jit(solution)/shard_map/ppermute | solution.py:353
  67.0 2.2 %shard_map.92 = (f32[40,1024]{1,0:T(8,128)S(1)}, f32[40,1024]{1,0:T(8,128)S(1)}, f32[40,1024]{1,0:T(8,128)S(1)}, f32[40,1024]{1,0:T(8,128)S(1)}) custom-call(bf16[384,512]{1,0:T(8,128)(2,1)S(1)} %get-tuple-element.36.terms, f32[128,512]{1,0:T(8,128)S(1)} %copy-done.2, f32[128,512]{1,0:T(8,128)S(1)} %copy-done.3, f32[384,512]{1,0:T(8,128)} %shard_map.91.here, ...), custom_call_target="tpu_custom_call" | custom-call | tf_op jit(solution)/shard_map/pallas_call | solution.py:415
  69.2 2.0 %collective-permute-start.20 = (f32[40,1024]{1,0:T(8,128)S(1)}, f32[40,1024]{1,0:T(8,128)S(1)}, u32[]{:S(2)}, u32[]{:S(2)}) collective-permute-start(f32[40,1024]{1,0:T(8,128)S(1)} %get-tuple-element.42), channel_id=1, source_target_pairs={{0,2},{1,3},{2,0},{3,1},{4,6},{5,7},{6,4},{7,5},{8,10},{9,11},{10,... | collective-permute-start | bytes 491528 | tf_op jit(solution)/shard_map/ppermute | solution.py:353
  72.6 2.7 %collective-permute-done.10.refs_1_ = f32[96,1024]{1,0:T(8,128)S(1)} collective-permute-done((f32[96,1024]{1,0:T(8,128)S(1)}, f32[96,1024]{1,0:T(8,128)S(1)}, u32[]{:S(2)}, u32[]{:S(2)}) %collective-permute-start.10) | collective-permute-done | bytes 393248 | tf_op jit(solution)/shard_map/ppermute | solution.py:353
  75.3 3.0 %collective-permute-start.22 = (f32[40,1024]{1,0:T(8,128)S(1)}, f32[40,1024]{1,0:T(8,128)S(1)}, u32[]{:S(2)}, u32[]{:S(2)}) collective-permute-start(f32[40,1024]{1,0:T(8,128)S(1)} %get-tuple-element.44), channel_id=1, source_target_pairs={{0,6},{1,7},{2,4},{3,5},{4,2},{5,3},{6,0},{7,1},{8,14},{9,15},{10,... | collective-permute-start | bytes 491528 | tf_op jit(solution)/shard_map/ppermute | solution.py:353
  78.3 7.6 %collective-permute-done.11.refs_2_ = f32[96,1024]{1,0:T(8,128)S(1)} collective-permute-done((f32[96,1024]{1,0:T(8,128)S(1)}, f32[96,1024]{1,0:T(8,128)S(1)}, u32[]{:S(2)}, u32[]{:S(2)}) %collective-permute-start.11) | collective-permute-done | bytes 393248 | tf_op jit(solution)/shard_map/ppermute | solution.py:353
  87.3 4.5 %collective-permute-done.21.refs_6_ = f32[40,1024]{1,0:T(8,128)S(1)} collective-permute-done((f32[40,1024]{1,0:T(8,128)S(1)}, f32[40,1024]{1,0:T(8,128)S(1)}, u32[]{:S(2)}, u32[]{:S(2)}) %collective-permute-start.21) | collective-permute-done | bytes 163872 | tf_op jit(solution)/shard_map/ppermute | solution.py:353
  91.8 1.7 %shard_map.94 = (bf16[128,4096]{1,0:T(8,128)(2,1)}, f32[1,128]{1,0:T(1,128)}, f32[4,4096]{1,0:T(4,128)}) custom-call(f32[96,1024]{1,0:T(8,128)S(1)} %get-tuple-element.32.refs_0_, f32[96,1024]{1,0:T(8,128)S(1)} %collective-permute-done.10.refs_1_, f32[96,1024]{1,0:T(8,128)S(1)} %collective-permute-done.11.refs_2_, ...), custom_call_target="tpu_custom_call" | custom-call | bytes 4194304 | tf_op jit(solution)/shard_map/pallas_call | solution.py:479
  (56 shorter events, 17.4 us)
Async XLA Ops:
  2.3 14.6 %collective-permute-start.2 = (f32[264,128]{1,0:T(8,128)}, f32[264,128]{1,0:T(8,128)S(1)}, u32[]{:S(2)}, u32[]{:S(2)}) collective-permute-start(f32[264,128]{1,0:T(8,128)} %shard_map.85.refs_0_), channel_id=1, source_target_pairs={{0,16},{1,17},{2,18},{3,19},{4,20},{5,21},{6,22},{7,23},{8,24},{9,... | collective-permute-start | bytes 405512 | tf_op jit(solution)/shard_map/ppermute | solution.py:353
  6.4 13.5 %collective-permute-start = (f32[264,128]{1,0:T(8,128)}, f32[264,128]{1,0:T(8,128)S(1)}, u32[]{:S(2)}, u32[]{:S(2)}) collective-permute-start(f32[264,128]{1,0:T(8,128)} %shard_map.85.refs_0_), channel_id=1, source_target_pairs={{0,8},{1,9},{2,10},{3,11},{4,12},{5,13},{6,14},{7,15},{8,16},{9,17... | collective-permute-start | bytes 405512 | tf_op jit(solution)/shard_map/ppermute | solution.py:353
  8.0 13.3 %collective-permute-start.1 = (f32[264,128]{1,0:T(8,128)}, f32[264,128]{1,0:T(8,128)S(1)}, u32[]{:S(2)}, u32[]{:S(2)}) collective-permute-start(f32[264,128]{1,0:T(8,128)} %shard_map.85.refs_0_), channel_id=1, source_target_pairs={{0,24},{1,25},{2,26},{3,27},{4,28},{5,29},{6,30},{7,31},{8,0},{9,1... | collective-permute-start | bytes 405512 | tf_op jit(solution)/shard_map/ppermute | solution.py:353
  12.3 14.3 %collective-permute-start.3 = (f32[128,512]{1,0:T(8,128)}, f32[128,512]{1,0:T(8,128)S(1)}, u32[]{:S(2)}, u32[]{:S(2)}) collective-permute-start(f32[128,512]{1,0:T(8,128)} %get-tuple-element.28.own), channel_id=1, source_target_pairs={{0,8},{1,9},{2,10},{3,11},{4,12},{5,13},{6,14},{7,15},{8,16},{9,17... | collective-permute-start | bytes 786440 | tf_op jit(solution)/shard_map/ppermute | solution.py:353
  14.0 17.2 %collective-permute-start.4 = (f32[128,512]{1,0:T(8,128)}, f32[128,512]{1,0:T(8,128)S(1)}, u32[]{:S(2)}, u32[]{:S(2)}) collective-permute-start(f32[128,512]{1,0:T(8,128)} %get-tuple-element.28.own), channel_id=1, source_target_pairs={{8,0},{9,1},{10,2},{11,3},{12,4},{13,5},{14,6},{15,7},{16,8},{17,9... | collective-permute-start | bytes 786440 | tf_op jit(solution)/shard_map/ppermute | solution.py:353
  16.8 15.6 %collective-permute-start.13 = (f32[128,512]{1,0:T(8,128)}, f32[128,512]{1,0:T(8,128)S(1)}, u32[]{:S(2)}, u32[]{:S(2)}) collective-permute-start(f32[128,512]{1,0:T(8,128)} %get-tuple-element.39.own), channel_id=1, source_target_pairs={{0,8},{1,9},{2,10},{3,11},{4,12},{5,13},{6,14},{7,15},{8,16},{9,17... | collective-permute-start | bytes 786440 | tf_op jit(solution)/shard_map/ppermute | solution.py:353
  19.9 17.9 %collective-permute-start.14 = (f32[128,512]{1,0:T(8,128)}, f32[128,512]{1,0:T(8,128)S(1)}, u32[]{:S(2)}, u32[]{:S(2)}) collective-permute-start(f32[128,512]{1,0:T(8,128)} %get-tuple-element.39.own), channel_id=1, source_target_pairs={{8,0},{9,1},{10,2},{11,3},{12,4},{13,5},{14,6},{15,7},{16,8},{17,9... | collective-permute-start | bytes 786440 | tf_op jit(solution)/shard_map/ppermute | solution.py:353
  22.9 36.9 %all-to-all-start = ((f32[4,264,512]{2,1,0:T(8,128)}), f32[4,264,512]{2,1,0:T(8,128)S(1)}, u32[]{:S(2)}, u32[]{:S(2)}) async-start(f32[4,264,512]{2,1,0:T(8,128)} %shard_map.86), calls=%async_computation | async-start | bytes 4325376 | tf_op jit(solution)/shard_map/all_to_all | solution.py:400
  26.6 13.3 %collective-permute-start.5 = (f32[128,512]{1,0:T(8,128)S(1)}, f32[128,512]{1,0:T(8,128)S(1)}, u32[]{:S(2)}, u32[]{:S(2)}) collective-permute-start(f32[128,512]{1,0:T(8,128)S(1)} %collective-permute-done.3.up1), channel_id=1, source_target_pairs={{0,8},{1,9},{2,10},{3,11},{4,12},{5,13},{6,14},{7,15},{8,16},{9,17... | collective-permute-start | bytes 786440 | tf_op jit(solution)/shard_map/ppermute | solution.py:353
  31.2 13.4 %collective-permute-start.6 = (f32[128,512]{1,0:T(8,128)S(1)}, f32[128,512]{1,0:T(8,128)S(1)}, u32[]{:S(2)}, u32[]{:S(2)}) collective-permute-start(f32[128,512]{1,0:T(8,128)S(1)} %collective-permute-done.4.down1), channel_id=1, source_target_pairs={{8,0},{9,1},{10,2},{11,3},{12,4},{13,5},{14,6},{15,7},{16,8},{17,9... | collective-permute-start | bytes 786440 | tf_op jit(solution)/shard_map/ppermute | solution.py:353
  32.5 13.4 %collective-permute-start.15 = (f32[128,512]{1,0:T(8,128)S(1)}, f32[128,512]{1,0:T(8,128)S(1)}, u32[]{:S(2)}, u32[]{:S(2)}) collective-permute-start(f32[128,512]{1,0:T(8,128)S(1)} %collective-permute-done.13.up1), channel_id=1, source_target_pairs={{0,8},{1,9},{2,10},{3,11},{4,12},{5,13},{6,14},{7,15},{8,16},{9,17... | collective-permute-start | bytes 786440 | tf_op jit(solution)/shard_map/ppermute | solution.py:353
  37.8 12.7 %collective-permute-start.16 = (f32[128,512]{1,0:T(8,128)S(1)}, f32[128,512]{1,0:T(8,128)S(1)}, u32[]{:S(2)}, u32[]{:S(2)}) collective-permute-start(f32[128,512]{1,0:T(8,128)S(1)} %collective-permute-done.14.down1), channel_id=1, source_target_pairs={{8,0},{9,1},{10,2},{11,3},{12,4},{13,5},{14,6},{15,7},{16,8},{17,9... | collective-permute-start | bytes 786440 | tf_op jit(solution)/shard_map/ppermute | solution.py:353
  39.9 11.9 %collective-permute-start.7 = (f32[128,512]{1,0:T(8,128)S(1)}, f32[128,512]{1,0:T(8,128)S(1)}, u32[]{:S(2)}, u32[]{:S(2)}) collective-permute-start(f32[128,512]{1,0:T(8,128)S(1)} %collective-permute-done.5.up2), channel_id=1, source_target_pairs={{0,8},{1,9},{2,10},{3,11},{4,12},{5,13},{6,14},{7,15},{8,16},{9,17... | collective-permute-start | bytes 786440 | tf_op jit(solution)/shard_map/ppermute | solution.py:353
  44.6 9.8 %collective-permute-start.8 = (f32[128,512]{1,0:T(8,128)S(1)}, f32[128,512]{1,0:T(8,128)S(1)}, u32[]{:S(2)}, u32[]{:S(2)}) collective-permute-start(f32[128,512]{1,0:T(8,128)S(1)} %collective-permute-done.6.down2), channel_id=1, source_target_pairs={{8,0},{9,1},{10,2},{11,3},{12,4},{13,5},{14,6},{15,7},{16,8},{17,9... | collective-permute-start | bytes 786440 | tf_op jit(solution)/shard_map/ppermute | solution.py:353
  45.9 8.6 %collective-permute-start.17 = (f32[128,512]{1,0:T(8,128)S(1)}, f32[128,512]{1,0:T(8,128)S(1)}, u32[]{:S(2)}, u32[]{:S(2)}) collective-permute-start(f32[128,512]{1,0:T(8,128)S(1)} %collective-permute-done.15.up2), channel_id=1, source_target_pairs={{0,8},{1,9},{2,10},{3,11},{4,12},{5,13},{6,14},{7,15},{8,16},{9,17... | collective-permute-start | bytes 786440 | tf_op jit(solution)/shard_map/ppermute | solution.py:353
  50.5 8.3 %collective-permute-start.18 = (f32[128,512]{1,0:T(8,128)S(1)}, f32[128,512]{1,0:T(8,128)S(1)}, u32[]{:S(2)}, u32[]{:S(2)}) collective-permute-start(f32[128,512]{1,0:T(8,128)S(1)} %collective-permute-done.16.down2), channel_id=1, source_target_pairs={{8,0},{9,1},{10,2},{11,3},{12,4},{13,5},{14,6},{15,7},{16,8},{17,9... | collective-permute-start | bytes 786440 | tf_op jit(solution)/shard_map/ppermute | solution.py:353
  54.5 5.9 %collective-permute-start.9 = (f32[384,512]{1,0:T(8,128)S(1)}, f32[384,512]{1,0:T(8,128)}, u32[]{:S(2)}, u32[]{:S(2)}) collective-permute-start(f32[384,512]{1,0:T(8,128)S(1)} %shard_map.89.here), channel_id=1, source_target_pairs={{0,1},{1,0},{2,3},{3,2},{4,5},{5,4},{6,7},{7,6},{8,9},{9,8},{10,11... | collective-permute-start | bytes 2359304 | tf_op jit(solution)/shard_map/ppermute | solution.py:353
  59.7 7.2 %collective-permute-start.19 = (f32[384,512]{1,0:T(8,128)}, f32[384,512]{1,0:T(8,128)}, u32[]{:S(2)}, u32[]{:S(2)}) collective-permute-start(f32[384,512]{1,0:T(8,128)} %shard_map.91.here), channel_id=1, source_target_pairs={{0,1},{1,0},{2,3},{3,2},{4,5},{5,4},{6,7},{7,6},{8,9},{9,8},{10,11... | collective-permute-start | bytes 2359304 | tf_op jit(solution)/shard_map/ppermute | solution.py:353
  63.3 12.0 %collective-permute-start.10 = (f32[96,1024]{1,0:T(8,128)S(1)}, f32[96,1024]{1,0:T(8,128)S(1)}, u32[]{:S(2)}, u32[]{:S(2)}) collective-permute-start(f32[96,1024]{1,0:T(8,128)S(1)} %get-tuple-element.33), channel_id=1, source_target_pairs={{0,2},{1,3},{2,0},{3,1},{4,6},{5,7},{6,4},{7,5},{8,10},{9,11},{10,... | collective-permute-start | bytes 1179656 | tf_op jit(solution)/shard_map/ppermute | solution.py:353
  65.4 20.4 %collective-permute-start.11 = (f32[96,1024]{1,0:T(8,128)S(1)}, f32[96,1024]{1,0:T(8,128)S(1)}, u32[]{:S(2)}, u32[]{:S(2)}) collective-permute-start(f32[96,1024]{1,0:T(8,128)S(1)} %get-tuple-element.34), channel_id=1, source_target_pairs={{0,4},{1,5},{2,6},{3,7},{4,0},{5,1},{6,2},{7,3},{8,12},{9,13},{10,... | collective-permute-start | bytes 1179656 | tf_op jit(solution)/shard_map/ppermute | solution.py:353
  66.9 19.0 %collective-permute-start.12 = (f32[96,1024]{1,0:T(8,128)S(1)}, f32[96,1024]{1,0:T(8,128)S(1)}, u32[]{:S(2)}, u32[]{:S(2)}) collective-permute-start(f32[96,1024]{1,0:T(8,128)S(1)} %get-tuple-element.35), channel_id=1, source_target_pairs={{0,6},{1,7},{2,4},{3,5},{4,2},{5,3},{6,0},{7,1},{8,14},{9,15},{10,... | collective-permute-start | bytes 1179656 | tf_op jit(solution)/shard_map/ppermute | solution.py:353
  69.2 18.1 %collective-permute-start.20 = (f32[40,1024]{1,0:T(8,128)S(1)}, f32[40,1024]{1,0:T(8,128)S(1)}, u32[]{:S(2)}, u32[]{:S(2)}) collective-permute-start(f32[40,1024]{1,0:T(8,128)S(1)} %get-tuple-element.42), channel_id=1, source_target_pairs={{0,2},{1,3},{2,0},{3,1},{4,6},{5,7},{6,4},{7,5},{8,10},{9,11},{10,... | collective-permute-start | bytes 491528 | tf_op jit(solution)/shard_map/ppermute | solution.py:353
  71.2 20.6 %collective-permute-start.21 = (f32[40,1024]{1,0:T(8,128)S(1)}, f32[40,1024]{1,0:T(8,128)S(1)}, u32[]{:S(2)}, u32[]{:S(2)}) collective-permute-start(f32[40,1024]{1,0:T(8,128)S(1)} %get-tuple-element.43), channel_id=1, source_target_pairs={{0,4},{1,5},{2,6},{3,7},{4,0},{5,1},{6,2},{7,3},{8,12},{9,13},{10,... | collective-permute-start | bytes 491528 | tf_op jit(solution)/shard_map/ppermute | solution.py:353
  75.3 16.5 %collective-permute-start.22 = (f32[40,1024]{1,0:T(8,128)S(1)}, f32[40,1024]{1,0:T(8,128)S(1)}, u32[]{:S(2)}, u32[]{:S(2)}) collective-permute-start(f32[40,1024]{1,0:T(8,128)S(1)} %get-tuple-element.44), channel_id=1, source_target_pairs={{0,6},{1,7},{2,4},{3,5},{4,2},{5,3},{6,0},{7,1},{8,14},{9,15},{10,... | collective-permute-start | bytes 491528 | tf_op jit(solution)/shard_map/ppermute | solution.py:353
  (11 other events, 132.4 us)

commit v3 on v2

--- a/solution.py
+++ b/solution.py
@@ -90,7 +90,10 @@
 
 
 EXTRA = 8
-CFG = dict(c0=0, c1=1e10, pr=4e10, m0=0, m1=0, ea=0, e=(1, 2), s1=0, s2=0)
+COLLECT_FIRST = 6_400_000_000
+COLLECT_LAST = 3_000_000_000
+MULTIPLY_FIRST = 1_300_000_000
+MULTIPLY_LAST = 1_000_000_000
 BF16 = jnp.bfloat16
 F32 = jnp.float32
 VMEM_LIMIT = 16 * 1024 * 1024
@@ -161,19 +164,29 @@
         at += value.shape[1]
 
 
-def collect(up1, down1, up2, down2, up3, down3, out_ref):
+def near_one(up1, down1, out_ref):
     z, _, _ = here_of()
-    tokens = up1.shape[0]
-    out_ref[:tokens, :] = jnp.where(z >= 1, up1[...], down3[...])
-    out_ref[tokens : 2 * tokens, :] = jnp.where(z <= 2, down1[...], up3[...])
-    out_ref[2 * tokens :, :] = jnp.where(z <= 1, down2[...], up2[...])
-
-
-def prepare(heads, rows, pair_most, *refs):
-    *parts, split_ref, last_ref, live_ref, state_ref, total_ref = refs
+    out_ref[...] = jnp.where(z <= 2, down1[...], up1[...])
+
+
+def two_away(up2, down2, out_ref):
+    z, _, _ = here_of()
+    out_ref[...] = jnp.where(z <= 1, down2[...], up2[...])
+
+
+def last_one(up1, up3, down3, *outs):
+    z, _, _ = here_of()
+    value = jnp.where(z == 0, down3[...], jnp.where(z == 3, up3[...], up1[...]))
+    size = outs[0].shape[0]
+    for i, out in enumerate(outs):
+        out[...] = value[i * size : (i + 1) * size]
+
+
+def prepare(heads, rows, pair_most, all_ref, *refs):
+    slot_ref, row_ref, last_ref, live_ref, state_ref, total_ref = refs
     z, chip, _ = here_of()
     owners = rows // DKV
-    tokens = sum(part.shape[2] for part in parts) // owners
+    tokens = all_ref.shape[2] // owners
     block = rows // owners
     slots = owners * pair_most
     split, cut = rows - DKV, (owners - 1) * pair_most
@@ -182,7 +195,7 @@
     def owner_row(m):
         at = chip ^ m
         return jnp.concatenate(
-            [parts[0][at, rows + 1 : rows + 2, :half], parts[0][at, rows + 2 : rows + 3, :half]], axis=1
+            [all_ref[at, rows + 1 : rows + 2, :half], all_ref[at, rows + 2 : rows + 3, :half]], axis=1
         )
 
     lane = iota((rows, rows), 1)
@@ -196,18 +209,18 @@
     at = iota((8, rows), 1) // block * pair_most
     slot_of = jnp.where(mine, before + at.astype(F32), -1.0)
     slot_id = iota((slots, rows), 0).astype(F32)
-    all0, all1 = split + cut, rows - split + slots - cut
+    all1 = rows - split + slots - cut
     for m in range(heads):
-        terms = jnp.concatenate([part[chip ^ m, :rows, :] for part in parts], axis=1).astype(BF16)
+        terms = all_ref[chip ^ m, :rows, :].astype(BF16)
         pick = (slot_id == slot_of[m : m + 1, :]).astype(F32)
         chosen = jnp.dot(pick.astype(BF16), terms, preferred_element_type=F32).astype(BF16)
-        split_ref[m * all0 : m * all0 + split, :] = terms[:split]
-        split_ref[m * all0 + split : (m + 1) * all0, :] = chosen[:cut]
+        row_ref[m * split : (m + 1) * split, :] = terms[:split]
+        slot_ref[m * cut : (m + 1) * cut, :] = chosen[:cut]
         last_ref[m * all1 : m * all1 + rows - split, :] = terms[split:]
         last_ref[m * all1 + rows - split : (m + 1) * all1, :] = chosen[cut:]
         if m == 0:
             live_ref[...] = jnp.sum(pick, axis=1, keepdims=True)
-    state = parts[0][chip, rows : rows + 1, :slots]
+    state = all_ref[chip, rows : rows + 1, :slots]
     same = iota((slots, slots), 0) == iota((slots, slots), 1)
     state_ref[...] = jnp.sum(jnp.where(same, state, 0.0), axis=1, keepdims=True)
     owner_of = jnp.where(
@@ -224,9 +237,7 @@
     count = jnp.dot(theirs, home.astype(BF16), preferred_element_type=F32)
     held = (iota((8, slots), 1) % pair_most).astype(F32) < count
     states = [
-        part[chip, rows : rows + 1, k : k + slots]
-        for part in parts
-        for k in range(0, part.shape[2], tokens)
+        all_ref[chip, rows : rows + 1, k * tokens : k * tokens + slots] for k in range(owners)
     ]
     states = jnp.concatenate(states + [jnp.zeros((8 - owners, slots), F32)], axis=0)
     states = jnp.where(held, states, 0.0)
@@ -236,31 +247,60 @@
         total_ref[i : i + 1, :] = jnp.broadcast_to(part, (1, slots))
 
 
-def multiply(heads, projections, slots, terms, own, near, here, there, *refs):
-    *refs, held = refs
-    sums_ref, outs = (refs[-1], refs[:-1]) if projections > 1 else (refs[0], refs[1:])
+def gather_blocks(held, own, near, got):
+    z, _, _ = here_of()
     tokens, half = own.shape
-    sides = [
-        [own[...]] + [here[k * tokens : (k + 1) * tokens, :] for k in range(3)],
-        [near[...]] + [there[k * tokens : (k + 1) * tokens, :] for k in range(3)],
-    ]
-    for side, values in enumerate(sides):
-        for k, value in enumerate(values):
-            held[k * tokens : (k + 1) * tokens, side * half : (side + 1) * half] = value.astype(BF16)
+    count = len(got) // 2
+    above = jnp.where(z == 3, 1, 2)
+    places = (above, 3, 3 - above)
+    for side, mine in enumerate((own, near)):
+        some = slice(side * half, (side + 1) * half)
+        held[:tokens, some] = mine[...].astype(BF16)
+        at = 0
+        for ref in got[side * count : (side + 1) * count]:
+            size = ref.shape[0]
+            block, rest = at // tokens, at % tokens
+            start = pl.multiple_of(places[block] * tokens + rest, size)
+            held[pl.ds(start, size), some] = ref[...].astype(BF16)
+            at += size
+
+
+def multiply(blocks, slot_terms, own, near, *refs):
+    got, outs, held = refs[:blocks], refs[blocks:-1], refs[-1]
+    gather_blocks(held, own, near, got)
     x = held[...]
-    each = projections * DKV + slots
+    each = outs[0].shape[0]
+    for m, out in enumerate(outs):
+        out[...] = jnp.dot(
+            slot_terms[m * each : (m + 1) * each, :], x, preferred_element_type=F32
+        )
+
+
+def column_sums(heads, row_terms, held, sums_ref):
+    x = held[...]
+    each = row_terms.shape[0] // heads
     for m in range(heads):
+        g = jnp.dot(row_terms[m * each : (m + 1) * each, :], x, preferred_element_type=F32)
+        for p in range(PROJ - 1):
+            part = g[p * DKV : (p + 1) * DKV]
+            sums_ref[m, p : p + 1, :] = jnp.sum(part * part + EPS_SQUARE, axis=0, keepdims=True)
+
+
+def multiply_last(blocks, slots, terms, own, near, *refs):
+    got, sums_ref, outs, held = refs[:blocks], refs[blocks], refs[blocks + 1 : -1], refs[-1]
+    gather_blocks(held, own, near, got)
+    x = held[...]
+    each = DKV + slots
+    width = x.shape[1]
+    base = width // 128 * slots
+    for m, out in enumerate(outs):
         g = jnp.dot(terms[m * each : (m + 1) * each, :], x, preferred_element_type=F32)
-        outs[m][:slots, :] = g[projections * DKV :]
-        for p in range(projections):
-            part = g[p * DKV : (p + 1) * DKV]
-            sums = jnp.sum(part * part + EPS_SQUARE, axis=0, keepdims=True)
-            if projections > 1:
-                sums_ref[m, p : p + 1, :] = sums
-            else:
-                outs[m][slots + PROJ - 1 : slots + PROJ, :] = sums
-        if projections == 1:
-            outs[m][slots : slots + PROJ - 1, :] = sums_ref[m, : PROJ - 1, :]
+        part = g[:DKV]
+        last = jnp.sum(part * part + EPS_SQUARE, axis=0, keepdims=True)
+        sums = jnp.concatenate([sums_ref[m, : PROJ - 1, :], last], axis=0)
+        for j in range(width // 128):
+            out[j * slots : (j + 1) * slots, :] = g[DKV:, j * 128 : (j + 1) * 128]
+            out[base + j * PROJ : base + (j + 1) * PROJ, :] = sums[:, j * 128 : (j + 1) * 128]
 
 
 def spans_of(refs, width):
@@ -275,36 +315,44 @@
     ], half
 
 
-def squares(refs, count):
-    square = jnp.zeros((count, 128), F32)
-    for ref in refs:
-        for j in range(0, ref.shape[1], 128):
-            g = ref[:count, j : j + 128]
-            square += g * g + EPS_SQUARE
-    return jnp.sum(square, axis=1, keepdims=True)
-
-
 def early(*refs):
     *first, square_ref = refs
-    square_ref[...] = squares(first, square_ref.shape[0])
+    square = jnp.zeros((square_ref.shape[0], 128), F32)
+    for ref in first:
+        for j in range(0, ref.shape[1], 128):
+            g = ref[:, j : j + 128]
+            square += g * g + EPS_SQUARE
+    square_ref[...] = jnp.sum(square, axis=1, keepdims=True)
 
 
 def update(heads, pair_most, *refs):
     first, last, refs = refs[:heads], refs[heads : 2 * heads], refs[2 * heads :]
     square0, params, live_ref, state_ref, total_ref, cols, new_params, new_rows, new_cols = refs
     slots, width = params.shape
-    cut = (PROJ - 1) * pair_most
-    rest = slots - cut
+    rest = pair_most
+    span = width // heads
+    base = span // 128 * rest
+    spans, half = spans_of(first, width)
+    spans = [(m, lo, start) for m in range(heads) for _, lo, start in spans[2 * m : 2 * m + 2]]
+
+    def beside(m, lo, offset, count):
+        blocks = range(lo // 128, (lo + half) // 128)
+        return jnp.concatenate(
+            [last[m][offset + j * count : offset + (j + 1) * count, :] for j in blocks], axis=1
+        )
+
     sums = jnp.zeros((PROJ, 128), F32)
-    spans, half = spans_of(last, width)
-    for ref, lo, start in spans:
-        col_sum = ref[rest : rest + PROJ, lo : lo + half]
-        for j in range(0, half, 128):
-            sums += col_sum[:, j : j + 128]
+    square = jnp.zeros((rest, 128), F32)
+    for m, lo, start in spans:
+        for j in range(lo // 128, (lo + half) // 128):
+            g = last[m][j * rest : (j + 1) * rest, :]
+            square += g * g + EPS_SQUARE
+            sums += last[m][base + j * PROJ : base + (j + 1) * PROJ, :]
         new_cols[:, pl.ds(start, half)] = (
-            DECAY_RATE * cols[:, pl.ds(start, half)] + (1.0 - DECAY_RATE) * col_sum / DKV
+            DECAY_RATE * cols[:, pl.ds(start, half)]
+            + (1.0 - DECAY_RATE) * beside(m, lo, base, PROJ) / DKV
         )
-    square = jnp.concatenate([square0[...], squares(last, rest)], axis=0)
+    square = jnp.concatenate([square0[...], jnp.sum(square, axis=1, keepdims=True)], axis=0)
     row_val = DECAY_RATE * state_ref[...] + (1.0 - DECAY_RATE) * (square / width)
     row_mean = (
         DECAY_RATE * total_ref[:, :1]
@@ -317,12 +365,11 @@
     row_scale = STEP_SIZE * jnp.sqrt(mean_at / row_val)
     same = iota((slots, slots), 0) == iota((slots, slots), 1)
     new_rows[...] = jnp.sum(jnp.where(same, row_val * live, 0.0), axis=0, keepdims=True)
-    for m, (_, lo, start) in zip([m for m in range(heads) for _ in range(2)], spans):
+    for m, lo, start in spans:
         col_scale = lax.rsqrt(new_cols[:, pl.ds(start, half)])
         for i in range(PROJ):
             rows = slice(i * pair_most, (i + 1) * pair_most)
-            ref, k = (first[m], i) if i < PROJ - 1 else (last[m], 0)
-            g = ref[k * pair_most : (k + 1) * pair_most, lo : lo + half]
+            g = first[m][rows, lo : lo + half] if i < PROJ - 1 else beside(m, lo, 0, rest)
             value = params[rows, pl.ds(start, half)].astype(F32) - g * row_scale[rows] * (
                 col_scale[i : i + 1]
             )
@@ -380,16 +427,8 @@
         compiler_params=pltpu.CompilerParams(vmem_limit_bytes=BEGIN_LIMIT),
     )(inputs)
 
-    def after(array, *others):
-        return lax.optimization_barrier((array, *others))[0] if others else array
-
     chips = [[2 * i + c for i in range(heads)] for c in range(2)]
     ring = lambda k: {i: (i + k) % dp_count for i in range(dp_count)}
-    edges = CFG["e"]
-
-    def edge(k, array, *others):
-        return after(array, *others) if k in edges else array
-
     def exchange(*blocks):
         size = sum(block.shape[1] for block in blocks)
         everywhere = call(
@@ -399,26 +438,16 @@
         )(*blocks)
         return lax.all_to_all(everywhere, "shard", 0, 0, axis_index_groups=chips)
 
-    def joined(cost, *arrays):
-        here = call(
-            collect,
-            jax.ShapeDtypeStruct((3 * tokens, half), F32),
-            arrays=6,
-            flops=int(cost),
-        )(*arrays)
-        return here, move(here, every, swap)
-
-    def product(cost, terms, projections, count, *blocks):
-        shapes = [jax.ShapeDtypeStruct((count if projections > 1 else count + EXTRA, span), F32)] * heads
-        if projections > 1:
-            shapes.append(jax.ShapeDtypeStruct((heads, 8, span), F32))
-        return call(
-            functools.partial(multiply, heads, projections, count),
-            shapes,
-            scratch=[pltpu.VMEM((depth, span), BF16)],
-            arrays=1 + len(blocks),
-            flops=int(cost),
-        )(terms, *blocks)
+    def chosen(body, parts, cost, *arrays):
+        outs = [jax.ShapeDtypeStruct((tokens // parts, half), F32)] * parts
+        here = call(body, outs, arrays=len(arrays), flops=cost)(*arrays)
+        return here, [move(block, every, swap) for block in here]
+
+    def joined(cost, parts, up1, down1, up2, down2, up3, down3):
+        one, one_n = chosen(near_one, 1, 0, up1, down1)
+        two, two_n = chosen(two_away, 1, 0, up2, down2)
+        three, three_n = chosen(last_one, parts, cost, up1, up3, down3)
+        return *one, *two, *three, *one_n, *two_n, *three_n
 
     def scatter(outs):
         return [
@@ -428,53 +457,53 @@
 
     up1, down1 = move(own0, upward), move(own0, downward)
     ha, hb, hc = [move(terms, ring(k)) for k in (1, dp_count - 1, 2)]
-    if CFG["s1"] == 0:
-        parts = [exchange(terms, ha, hb, edge(3, hc, up1, down1))]
-    elif CFG["s1"] == 1:
-        parts = [exchange(terms, ha, hb)]
-        parts.append(exchange(edge(3, hc, up1, down1)))
-    elif CFG["s1"] == 2:
-        parts = [exchange(terms)]
-        parts.append(exchange(ha, hb, edge(3, edge(11, hc, parts[0]), up1, down1)))
-    else:
-        parts = [exchange(terms, ha)]
-        parts.append(exchange(hb, edge(3, hc, up1, down1)))
-    up2, down2 = move(edge(1, up1, ha), upward), move(edge(1, down1, hb), downward)
-    x1 = edge(5, edge(2, own1, hc), up1, down1)
-    x1 = edge(12, x1, up2, down2)
-    nup1, ndown1 = move(x1, upward), move(x1, downward)
-    up3 = move(edge(4, up2, nup1), upward)
-    down3 = move(edge(4, down2, ndown1), downward)
-    here0, there0 = joined(CFG["c0"], up1, down1, up2, down2, up3, down3)
-    nup2, ndown2 = move(edge(6, nup1, up2), upward), move(edge(6, ndown1, down2), downward)
-    parts[0] = edge(13, parts[0], there0)
-    split_terms, last_terms, live, state, total = call(
+    gathered = exchange(terms, ha, hb, hc)
+    up2, down2 = move(up1, upward), move(down1, downward)
+    late = lax.optimization_barrier((own1, hc))[0]
+    nup1, ndown1 = move(late, upward), move(late, downward)
+    up3, down3 = move(up2, upward), move(down2, downward)
+    blocks0 = joined(COLLECT_FIRST, 1, up1, down1, up2, down2, up3, down3)
+    nup2, ndown2 = move(nup1, upward), move(ndown1, downward)
+    slot_terms, row_terms, last_terms, live, state, total = call(
         functools.partial(prepare, heads, rows, pair_most),
         [
-            jax.ShapeDtypeStruct((heads * (split + cut), depth), BF16),
+            jax.ShapeDtypeStruct((heads * cut, depth), BF16),
+            jax.ShapeDtypeStruct((heads * split, depth), BF16),
             jax.ShapeDtypeStruct((heads * (rows - split + slots - cut), depth), BF16),
             jax.ShapeDtypeStruct((slots, 1), F32),
             jax.ShapeDtypeStruct((slots, 1), F32),
             jax.ShapeDtypeStruct((PROJ, slots), F32),
         ],
-        arrays=len(parts),
-        flops=int(CFG["pr"]),
-    )(*parts)
-    here0 = edge(9, here0, nup2, ndown2)
-    *outs, sums0 = product(CFG["m0"], split_terms, PROJ - 1, cut, own0, near0, here0, there0)
+        arrays=1,
+    )(gathered)
+    *outs, held0 = call(
+        functools.partial(multiply, len(blocks0)),
+        [jax.ShapeDtypeStruct((cut, span), F32)] * heads + [jax.ShapeDtypeStruct((depth, span), BF16)],
+        arrays=3 + len(blocks0),
+        flops=MULTIPLY_FIRST,
+    )(slot_terms, own0, near0, *blocks0)
+    sums0 = call(
+        functools.partial(column_sums, heads),
+        jax.ShapeDtypeStruct((heads, 8, span), F32),
+        arrays=2,
+    )(row_terms, held0)
     first = scatter(outs)
-    nup3 = move(edge(14, edge(7, nup2, outs[0]), there0), upward)
-    ndown3 = move(edge(14, edge(7, ndown2, outs[0]), there0), downward)
-    nup1 = edge(10, edge(8, nup1, first[1]), outs[0])
-    here1, there1 = joined(CFG["c1"], nup1, ndown1, nup2, ndown2, nup3, ndown3)
+    nup3, ndown3 = move(nup2, upward), move(ndown2, downward)
+    blocks1 = joined(COLLECT_LAST, 2, nup1, ndown1, nup2, ndown2, nup3, ndown3)
+    rest = slots - cut
     last = scatter(
-        product(CFG["m1"], last_terms, 1, slots - cut, own1, near1, here1, there1, sums0)
+        call(
+            functools.partial(multiply_last, len(blocks1), rest),
+            [jax.ShapeDtypeStruct((span // 128 * (rest + PROJ), 128), F32)] * heads,
+            scratch=[pltpu.VMEM((depth, span), BF16)],
+            arrays=4 + len(blocks1),
+            flops=MULTIPLY_LAST,
+        )(last_terms, own1, near1, *blocks1, sums0)
     )
     square0 = call(
         early,
         jax.ShapeDtypeStruct((cut, 1), F32),
         arrays=heads,
-        flops=int(CFG["ea"]),
     )(*first)
     new_params, new_rows, new_cols = call(
         functools.partial(update, heads, pair_most),
@@ -491,7 +520,8 @@
 
 def one_step(mesh, *args):
     dp_count, shard_count = mesh.shape["dp"], mesh.shape["shard"]
-    if dp_count == 4 and shard_count == 8:
+    tokens, slots, rows = args[1].shape[0], args[3].shape[1], args[0].shape[2]
+    if dp_count == 4 and shard_count == 8 and tokens == slots and rows == PROJ * DKV:
         return gather_step(dp_count, shard_count, *args)
     return general_step(*args)
 

time: 94.1 us -> 92 us (0.978)
  waiting for transfers between devices: 24.3 us -> 19.9 us
  Pallas kernels: 13.6 us -> 15.3 us
    ppermute x23 -> x28, waiting for transfers between devices: 24.3 us -> 19.9 us  [move(): return lax.ppermute(array, ('dp', 'shard'), pairs)]
    pallas_call x5 -> x10, Pallas kernels: 5.99 us -> 9.05 us  [the longest x6 3.62 us: chosen(): here = call(body, outs, arrays=len(arrays), flops=cost)(*arrays)]
    pallas_call x1, Pallas kernels: 1.66 us -> 0.27 us  [exchange(): call(spread, jax.ShapeDtypeStruct((heads, rows + EXTRA, size), F32), arra...]
    ppermute x23 -> x28, starting transfers between devices: 49 us -> 49.7 us  [move(): return lax.ppermute(array, ('dp', 'shard'), pairs)]
  transfers between devices with their start and end apart: 24 -> 29, of which waited for: 7 -> 8; matrix products, arithmetic and copies ran while one was open for 0% -> 0% of each run, Pallas kernels for 11% -> 13%
where the time goes in v3:
time: 92 us; the launch traced here: 90.9 us
  starting transfers between devices  53.4 us (58%)
  waiting for transfers between devices  19.9 us (22%)
  Pallas kernels  15.3 us (17%)
  local copies, waits for them, and re-layouts  1.4 us (2%)
  between operations  0.97 us (1%)
    ppermute x28, starting transfers between devices, move(): return lax.ppermute(array, ('dp', 'shard'), pairs)  49.7 us
    ppermute x28, waiting for transfers between devices, move(): return lax.ppermute(array, ('dp', 'shard'), pairs)  19.9 us
    all_to_all x1, starting transfers between devices, exchange(): return lax.all_to_all(everywhere, 'shard', 0, 0, axis_index_groups=chips)  3.72 us
    pallas_call x6, Pallas kernels, chosen(): here = call(body, outs, arrays=len(arrays), flops=cost)(*arrays)  3.62 us
    pallas_call x1, Pallas kernels, gather_step(): call(functools.partial(multiply, len(blocks0)), [jax.ShapeDtypeStruct((cu...  2.2 us
    pallas_call x1, Pallas kernels, gather_step(): pl.pallas_call(columns, out_shape=[jax.ShapeDtypeStruct((tokens, half), F...  2.12 us
    pallas_call x1, Pallas kernels, gather_step(): call(functools.partial(multiply_last, len(blocks1), rest), [jax.ShapeDtyp...  1.97 us
  transfers between devices with their start and end apart: 29, of which 8 were waited for; matrix products, arithmetic and copies ran while one was open for 0% of the time, Pallas kernels for 13%

profile of v3, /device:TPU:0, one launch (start us, length us, event | category | flops | bytes accessed | tf_op | source)
XLA Modules:
  0.0 90.9 jit_solution(1701449735619682170)
XLA Ops:
  0.6 1.6 %shard_map.85.refs_0_ = f32[264,128]{1,0:T(8,128)} custom-call(bf16[128,256]{1,0:T(8,128)(2,1)} %bitcast.8, s32[1,256]{1,0:T(1,128)} %bitcast.9, f32[1,128]{1,0:T(1,128)} %state_hbm.1), custom_call_target="tpu_custom_call" | custom-call | tf_op jit(solution)/shard_map/pallas_call | solution.py:408
  2.3 3.1 %collective-permute-start = (f32[264,128]{1,0:T(8,128)}, f32[264,128]{1,0:T(8,128)S(1)}, u32[]{:S(2)}, u32[]{:S(2)}) collective-permute-start(f32[264,128]{1,0:T(8,128)} %shard_map.85.refs_0_), channel_id=1, source_target_pairs={{0,8},{1,9},{2,10},{3,11},{4,12},{5,13},{6,14},{7,15},{8,16},{9,17... | collective-permute-start | bytes 405512 | tf_op jit(solution)/shard_map/ppermute | solution.py:400
  5.3 2.1 %collective-permute-start.1 = (f32[264,128]{1,0:T(8,128)}, f32[264,128]{1,0:T(8,128)S(1)}, u32[]{:S(2)}, u32[]{:S(2)}) collective-permute-start(f32[264,128]{1,0:T(8,128)} %shard_map.85.refs_0_), channel_id=1, source_target_pairs={{0,24},{1,25},{2,26},{3,27},{4,28},{5,29},{6,30},{7,31},{8,0},{9,1... | collective-permute-start | bytes 405512 | tf_op jit(solution)/shard_map/ppermute | solution.py:400
  8.4 2.1 %shard_map.88 = (f32[128,512]{1,0:T(8,128)}, f32[128,512]{1,0:T(8,128)}, f32[128,512]{1,0:T(8,128)}, f32[128,512]{1,0:T(8,128)}) custom-call(bf16[128,2,4096]{2,1,0:T(2,128)(2,1)} %inputs_hbm.1), custom_call_target="tpu_custom_call" | custom-call | tf_op jit(solution)/shard_map/pallas_call | solution.py:421
  10.5 3.5 %collective-permute-start.3 = (f32[128,512]{1,0:T(8,128)}, f32[128,512]{1,0:T(8,128)S(1)}, u32[]{:S(2)}, u32[]{:S(2)}) collective-permute-start(f32[128,512]{1,0:T(8,128)} %get-tuple-element.29.own), channel_id=1, source_target_pairs={{0,8},{1,9},{2,10},{3,11},{4,12},{5,13},{6,14},{7,15},{8,16},{9,17... | collective-permute-start | bytes 786440 | tf_op jit(solution)/shard_map/ppermute | solution.py:400
  15.3 4.7 %collective-permute-done.2.refs_3_ = f32[264,128]{1,0:T(8,128)S(1)} collective-permute-done((f32[264,128]{1,0:T(8,128)}, f32[264,128]{1,0:T(8,128)S(1)}, u32[]{:S(2)}, u32[]{:S(2)}) %collective-permute-start.2) | collective-permute-done | bytes 135200 | tf_op jit(solution)/shard_map/ppermute | solution.py:400
  20.3 1.4 %copy-done = f32[4,264,512]{2,1,0:T(8,128)} copy-done((f32[4,264,512]{2,1,0:T(8,128)}, f32[4,264,512]{2,1,0:T(8,128)S(1)}, u32[]{:S(2)}) %copy-start) | copy-done | bytes 2162712
  21.7 3.7 %all-to-all-start = ((f32[4,264,512]{2,1,0:T(8,128)}), f32[4,264,512]{2,1,0:T(8,128)S(1)}, u32[]{:S(2)}, u32[]{:S(2)}) async-start(f32[4,264,512]{2,1,0:T(8,128)} %copy-done), calls=%async_computation | async-start | bytes 4325376 | tf_op jit(solution)/shard_map/all_to_all | solution.py:439
  25.4 1.4 %collective-permute-start.5 = (f32[128,512]{1,0:T(8,128)S(1)}, f32[128,512]{1,0:T(8,128)S(1)}, u32[]{:S(2)}, u32[]{:S(2)}) collective-permute-start(f32[128,512]{1,0:T(8,128)S(1)} %collective-permute-done.3.up1), channel_id=1, source_target_pairs={{0,8},{1,9},{2,10},{3,11},{4,12},{5,13},{6,14},{7,15},{8,16},{9,17... | collective-permute-start | bytes 786440 | tf_op jit(solution)/shard_map/ppermute | solution.py:400
  28.0 4.6 %collective-permute-start.15 = (f32[128,512]{1,0:T(8,128)}, f32[128,512]{1,0:T(8,128)S(1)}, u32[]{:S(2)}, u32[]{:S(2)}) collective-permute-start(f32[128,512]{1,0:T(8,128)} %get-tuple-element.38.own), channel_id=1, source_target_pairs={{0,8},{1,9},{2,10},{3,11},{4,12},{5,13},{6,14},{7,15},{8,16},{9,17... | collective-permute-start | bytes 786440 | tf_op jit(solution)/shard_map/ppermute | solution.py:400
  33.9 4.6 %collective-permute-start.7 = (f32[128,512]{1,0:T(8,128)S(1)}, f32[128,512]{1,0:T(8,128)S(1)}, u32[]{:S(2)}, u32[]{:S(2)}) collective-permute-start(f32[128,512]{1,0:T(8,128)S(1)} %collective-permute-done.5.up2), channel_id=1, source_target_pairs={{0,8},{1,9},{2,10},{3,11},{4,12},{5,13},{6,14},{7,15},{8,16},{9,17... | collective-permute-start | bytes 786440 | tf_op jit(solution)/shard_map/ppermute | solution.py:400
  39.9 5.3 %collective-permute-start.17 = (f32[128,512]{1,0:T(8,128)S(1)}, f32[128,512]{1,0:T(8,128)}, u32[]{:S(2)}, u32[]{:S(2)}) collective-permute-start(f32[128,512]{1,0:T(8,128)S(1)} %collective-permute-done.15.up1), channel_id=1, source_target_pairs={{0,8},{1,9},{2,10},{3,11},{4,12},{5,13},{6,14},{7,15},{8,16},{9,17... | collective-permute-start | bytes 786440 | tf_op jit(solution)/shard_map/ppermute | solution.py:400
  48.6 2.0 %collective-permute-done.17.up2 = f32[128,512]{1,0:T(8,128)} collective-permute-done((f32[128,512]{1,0:T(8,128)S(1)}, f32[128,512]{1,0:T(8,128)}, u32[]{:S(2)}, u32[]{:S(2)}) %collective-permute-start.17) | collective-permute-done | bytes 262176 | tf_op jit(solution)/shard_map/ppermute | solution.py:400
  50.7 5.2 %collective-permute-start.19 = (f32[128,512]{1,0:T(8,128)}, f32[128,512]{1,0:T(8,128)}, u32[]{:S(2)}, u32[]{:S(2)}) collective-permute-start(f32[128,512]{1,0:T(8,128)} %collective-permute-done.17.up2), channel_id=1, source_target_pairs={{0,8},{1,9},{2,10},{3,11},{4,12},{5,13},{6,14},{7,15},{8,16},{9,17... | collective-permute-start | bytes 786440 | tf_op jit(solution)/shard_map/ppermute | solution.py:400
  59.4 2.2 %shard_map.92 = (f32[96,1024]{1,0:T(8,128)S(1)}, f32[96,1024]{1,0:T(8,128)S(1)}, f32[96,1024]{1,0:T(8,128)S(1)}, f32[96,1024]{1,0:T(8,128)S(1)}, bf16[512,1024]{1,0:T(8,128)(2,1)S(1)}) custom-call(bf16[384,512]{1,0:T(8,128)(2,1)S(1)} %get-tuple-element.28.slot_terms, f32[128,512]{1,0:T(8,128)S(1)} %copy-done.5, f32[128,512]{1,0:T(8,128)S(1)} %copy-done.6, ...), custom_call_target="tpu_custom_call" | custom-call | flops 1300000000 | tf_op jit(solution)/shard_map/pallas_call | solution.py:479
  61.6 2.1 %collective-permute-start.12 = (f32[96,1024]{1,0:T(8,128)S(1)}, f32[96,1024]{1,0:T(8,128)S(1)}, u32[]{:S(2)}, u32[]{:S(2)}) collective-permute-start(f32[96,1024]{1,0:T(8,128)S(1)} %get-tuple-element.32), channel_id=1, source_target_pairs={{0,2},{1,3},{2,0},{3,1},{4,6},{5,7},{6,4},{7,5},{8,10},{9,11},{10,... | collective-permute-start | bytes 1179656 | tf_op jit(solution)/shard_map/ppermute | solution.py:400
  63.7 1.5 %collective-permute-start.13 = (f32[96,1024]{1,0:T(8,128)S(1)}, f32[96,1024]{1,0:T(8,128)S(1)}, u32[]{:S(2)}, u32[]{:S(2)}) collective-permute-start(f32[96,1024]{1,0:T(8,128)S(1)} %get-tuple-element.33), channel_id=1, source_target_pairs={{0,4},{1,5},{2,6},{3,7},{4,0},{5,1},{6,2},{7,3},{8,12},{9,13},{10,... | collective-permute-start | bytes 1179656 | tf_op jit(solution)/shard_map/ppermute | solution.py:400
  65.5 2.9 %collective-permute-start.14 = (f32[96,1024]{1,0:T(8,128)S(1)}, f32[96,1024]{1,0:T(8,128)S(1)}, u32[]{:S(2)}, u32[]{:S(2)}) collective-permute-start(f32[96,1024]{1,0:T(8,128)S(1)} %get-tuple-element.34), channel_id=1, source_target_pairs={{0,6},{1,7},{2,4},{3,5},{4,2},{5,3},{6,0},{7,1},{8,14},{9,15},{10,... | collective-permute-start | bytes 1179656 | tf_op jit(solution)/shard_map/ppermute | solution.py:400
  71.1 2.0 %shard_map.97 = (f32[288,128]{1,0:T(8,128)S(1)}, f32[288,128]{1,0:T(8,128)S(1)}, f32[288,128]{1,0:T(8,128)S(1)}, f32[288,128]{1,0:T(8,128)S(1)}) custom-call(bf16[384,512]{1,0:T(8,128)(2,1)S(1)} %get-tuple-element.35.terms, f32[128,512]{1,0:T(8,128)} %get-tuple-element.38.own, f32[128,512]{1,0:T(8,128)S(1)} %copy-done.4, f32[128,512]{1,0:T(8,128)S(1)} %shard_map.93.refs_0_, ...), custom_call_target="tpu_custom_call" | custom-call | flops 1000000000 | tf_op jit(solution)/shard_map/pallas_call | solution.py:495
  73.8 2.8 %collective-permute-start.27 = (f32[288,128]{1,0:T(8,128)S(1)}, f32[288,128]{1,0:T(8,128)S(1)}, u32[]{:S(2)}, u32[]{:S(2)}) collective-permute-start(f32[288,128]{1,0:T(8,128)S(1)} %get-tuple-element.46), channel_id=1, source_target_pairs={{0,6},{1,7},{2,4},{3,5},{4,2},{5,3},{6,0},{7,1},{8,14},{9,15},{10,... | collective-permute-start | bytes 442376 | tf_op jit(solution)/shard_map/ppermute | solution.py:400
  76.7 6.4 %collective-permute-done.13.refs_2_ = f32[96,1024]{1,0:T(8,128)S(1)} collective-permute-done((f32[96,1024]{1,0:T(8,128)S(1)}, f32[96,1024]{1,0:T(8,128)S(1)}, u32[]{:S(2)}, u32[]{:S(2)}) %collective-permute-start.13) | collective-permute-done | bytes 393248 | tf_op jit(solution)/shard_map/ppermute | solution.py:400
  83.8 1.4 %collective-permute-done.25.refs_5_ = f32[288,128]{1,0:T(8,128)S(1)} collective-permute-done((f32[288,128]{1,0:T(8,128)S(1)}, f32[288,128]{1,0:T(8,128)S(1)}, u32[]{:S(2)}, u32[]{:S(2)}) %collective-permute-start.25) | collective-permute-done | bytes 147488 | tf_op jit(solution)/shard_map/ppermute | solution.py:400
  85.2 4.0 %collective-permute-done.26.refs_6_ = f32[288,128]{1,0:T(8,128)S(1)} collective-permute-done((f32[288,128]{1,0:T(8,128)S(1)}, f32[288,128]{1,0:T(8,128)S(1)}, u32[]{:S(2)}, u32[]{:S(2)}) %collective-permute-start.26) | collective-permute-done | bytes 147488 | tf_op jit(solution)/shard_map/ppermute | solution.py:400
  89.3 1.7 %shard_map.99 = (bf16[128,4096]{1,0:T(8,128)(2,1)}, f32[1,128]{1,0:T(1,128)}, f32[4,4096]{1,0:T(4,128)}) custom-call(f32[96,1024]{1,0:T(8,128)S(1)} %get-tuple-element.31.refs_0_, f32[96,1024]{1,0:T(8,128)S(1)} %collective-permute-done.12.refs_1_, f32[96,1024]{1,0:T(8,128)S(1)} %collective-permute-done.13.refs_2_, ...), custom_call_target="tpu_custom_call" | custom-call | bytes 4194304 | tf_op jit(solution)/shard_map/pallas_call | solution.py:508
  (63 shorter events, 17.8 us)
Async XLA Ops:
  2.3 13.0 %collective-permute-start = (f32[264,128]{1,0:T(8,128)}, f32[264,128]{1,0:T(8,128)S(1)}, u32[]{:S(2)}, u32[]{:S(2)}) collective-permute-start(f32[264,128]{1,0:T(8,128)} %shard_map.85.refs_0_), channel_id=1, source_target_pairs={{0,8},{1,9},{2,10},{3,11},{4,12},{5,13},{6,14},{7,15},{8,16},{9,17... | collective-permute-start | bytes 405512 | tf_op jit(solution)/shard_map/ppermute | solution.py:400
  5.3 10.0 %collective-permute-start.1 = (f32[264,128]{1,0:T(8,128)}, f32[264,128]{1,0:T(8,128)S(1)}, u32[]{:S(2)}, u32[]{:S(2)}) collective-permute-start(f32[264,128]{1,0:T(8,128)} %shard_map.85.refs_0_), channel_id=1, source_target_pairs={{0,24},{1,25},{2,26},{3,27},{4,28},{5,29},{6,30},{7,31},{8,0},{9,1... | collective-permute-start | bytes 405512 | tf_op jit(solution)/shard_map/ppermute | solution.py:400
  7.4 12.6 %collective-permute-start.2 = (f32[264,128]{1,0:T(8,128)}, f32[264,128]{1,0:T(8,128)S(1)}, u32[]{:S(2)}, u32[]{:S(2)}) collective-permute-start(f32[264,128]{1,0:T(8,128)} %shard_map.85.refs_0_), channel_id=1, source_target_pairs={{0,16},{1,17},{2,18},{3,19},{4,20},{5,21},{6,22},{7,23},{8,24},{9,... | collective-permute-start | bytes 405512 | tf_op jit(solution)/shard_map/ppermute | solution.py:400
  10.5 14.9 %collective-permute-start.3 = (f32[128,512]{1,0:T(8,128)}, f32[128,512]{1,0:T(8,128)S(1)}, u32[]{:S(2)}, u32[]{:S(2)}) collective-permute-start(f32[128,512]{1,0:T(8,128)} %get-tuple-element.29.own), channel_id=1, source_target_pairs={{0,8},{1,9},{2,10},{3,11},{4,12},{5,13},{6,14},{7,15},{8,16},{9,17... | collective-permute-start | bytes 786440 | tf_op jit(solution)/shard_map/ppermute | solution.py:400
  14.0 12.7 %collective-permute-start.4 = (f32[128,512]{1,0:T(8,128)}, f32[128,512]{1,0:T(8,128)S(1)}, u32[]{:S(2)}, u32[]{:S(2)}) collective-permute-start(f32[128,512]{1,0:T(8,128)} %get-tuple-element.29.own), channel_id=1, source_target_pairs={{8,0},{9,1},{10,2},{11,3},{12,4},{13,5},{14,6},{15,7},{16,8},{17,9... | collective-permute-start | bytes 786440 | tf_op jit(solution)/shard_map/ppermute | solution.py:400
  21.7 36.5 %all-to-all-start = ((f32[4,264,512]{2,1,0:T(8,128)}), f32[4,264,512]{2,1,0:T(8,128)S(1)}, u32[]{:S(2)}, u32[]{:S(2)}) async-start(f32[4,264,512]{2,1,0:T(8,128)} %copy-done), calls=%async_computation | async-start | bytes 4325376 | tf_op jit(solution)/shard_map/all_to_all | solution.py:439
  26.7 11.8 %collective-permute-start.6 = (f32[128,512]{1,0:T(8,128)S(1)}, f32[128,512]{1,0:T(8,128)S(1)}, u32[]{:S(2)}, u32[]{:S(2)}) collective-permute-start(f32[128,512]{1,0:T(8,128)S(1)} %collective-permute-done.4.down1), channel_id=1, source_target_pairs={{8,0},{9,1},{10,2},{11,3},{12,4},{13,5},{14,6},{15,7},{16,8},{17,9... | collective-permute-start | bytes 786440 | tf_op jit(solution)/shard_map/ppermute | solution.py:400
  28.0 11.9 %collective-permute-start.15 = (f32[128,512]{1,0:T(8,128)}, f32[128,512]{1,0:T(8,128)S(1)}, u32[]{:S(2)}, u32[]{:S(2)}) collective-permute-start(f32[128,512]{1,0:T(8,128)} %get-tuple-element.38.own), channel_id=1, source_target_pairs={{0,8},{1,9},{2,10},{3,11},{4,12},{5,13},{6,14},{7,15},{8,16},{9,17... | collective-permute-start | bytes 786440 | tf_op jit(solution)/shard_map/ppermute | solution.py:400
  32.6 12.6 %collective-permute-start.16 = (f32[128,512]{1,0:T(8,128)}, f32[128,512]{1,0:T(8,128)S(1)}, u32[]{:S(2)}, u32[]{:S(2)}) collective-permute-start(f32[128,512]{1,0:T(8,128)} %get-tuple-element.38.own), channel_id=1, source_target_pairs={{8,0},{9,1},{10,2},{11,3},{12,4},{13,5},{14,6},{15,7},{16,8},{17,9... | collective-permute-start | bytes 786440 | tf_op jit(solution)/shard_map/ppermute | solution.py:400
  33.9 13.3 %collective-permute-start.7 = (f32[128,512]{1,0:T(8,128)S(1)}, f32[128,512]{1,0:T(8,128)S(1)}, u32[]{:S(2)}, u32[]{:S(2)}) collective-permute-start(f32[128,512]{1,0:T(8,128)S(1)} %collective-permute-done.5.up2), channel_id=1, source_target_pairs={{0,8},{1,9},{2,10},{3,11},{4,12},{5,13},{6,14},{7,15},{8,16},{9,17... | collective-permute-start | bytes 786440 | tf_op jit(solution)/shard_map/ppermute | solution.py:400
  39.8 18.9 %collective-permute-start.9 = (f32[128,512]{1,0:T(8,128)S(1)}, f32[128,512]{1,0:T(8,128)}, u32[]{:S(2)}, u32[]{:S(2)}) collective-permute-start(f32[128,512]{1,0:T(8,128)S(1)} %shard_map.89.refs_0_), channel_id=1, source_target_pairs={{0,1},{1,0},{2,3},{3,2},{4,5},{5,4},{6,7},{7,6},{8,9},{9,8},{10,11... | collective-permute-start | bytes 786440 | tf_op jit(solution)/shard_map/ppermute | solution.py:400
  39.9 10.7 %collective-permute-start.17 = (f32[128,512]{1,0:T(8,128)S(1)}, f32[128,512]{1,0:T(8,128)}, u32[]{:S(2)}, u32[]{:S(2)}) collective-permute-start(f32[128,512]{1,0:T(8,128)S(1)} %collective-permute-done.15.up1), channel_id=1, source_target_pairs={{0,8},{1,9},{2,10},{3,11},{4,12},{5,13},{6,14},{7,15},{8,16},{9,17... | collective-permute-start | bytes 786440 | tf_op jit(solution)/shard_map/ppermute | solution.py:400
  45.2 10.7 %collective-permute-start.18 = (f32[128,512]{1,0:T(8,128)S(1)}, f32[128,512]{1,0:T(8,128)S(1)}, u32[]{:S(2)}, u32[]{:S(2)}) collective-permute-start(f32[128,512]{1,0:T(8,128)S(1)} %collective-permute-done.16.down1), channel_id=1, source_target_pairs={{8,0},{9,1},{10,2},{11,3},{12,4},{13,5},{14,6},{15,7},{16,8},{17,9... | collective-permute-start | bytes 786440 | tf_op jit(solution)/shard_map/ppermute | solution.py:400
  47.2 11.6 %collective-permute-start.10 = (f32[128,512]{1,0:T(8,128)}, f32[128,512]{1,0:T(8,128)}, u32[]{:S(2)}, u32[]{:S(2)}) collective-permute-start(f32[128,512]{1,0:T(8,128)} %shard_map.90.refs_1_), channel_id=1, source_target_pairs={{0,1},{1,0},{2,3},{3,2},{4,5},{5,4},{6,7},{7,6},{8,9},{9,8},{10,11... | collective-permute-start | bytes 786440 | tf_op jit(solution)/shard_map/ppermute | solution.py:400
  48.6 10.7 %collective-permute-start.11 = (f32[128,512]{1,0:T(8,128)}, f32[128,512]{1,0:T(8,128)}, u32[]{:S(2)}, u32[]{:S(2)}) collective-permute-start(f32[128,512]{1,0:T(8,128)} %shard_map.91.refs_2_), channel_id=1, source_target_pairs={{0,1},{1,0},{2,3},{3,2},{4,5},{5,4},{6,7},{7,6},{8,9},{9,8},{10,11... | collective-permute-start | bytes 786440 | tf_op jit(solution)/shard_map/ppermute | solution.py:400
  50.7 13.0 %collective-permute-start.19 = (f32[128,512]{1,0:T(8,128)}, f32[128,512]{1,0:T(8,128)}, u32[]{:S(2)}, u32[]{:S(2)}) collective-permute-start(f32[128,512]{1,0:T(8,128)} %collective-permute-done.17.up2), channel_id=1, source_target_pairs={{0,8},{1,9},{2,10},{3,11},{4,12},{5,13},{6,14},{7,15},{8,16},{9,17... | collective-permute-start | bytes 786440 | tf_op jit(solution)/shard_map/ppermute | solution.py:400
  58.8 10.7 %collective-permute-start.21 = (f32[128,512]{1,0:T(8,128)S(1)}, f32[128,512]{1,0:T(8,128)S(1)}, u32[]{:S(2)}, u32[]{:S(2)}) collective-permute-start(f32[128,512]{1,0:T(8,128)S(1)} %shard_map.93.refs_0_), channel_id=1, source_target_pairs={{0,1},{1,0},{2,3},{3,2},{4,5},{5,4},{6,7},{7,6},{8,9},{9,8},{10,11... | collective-permute-start | bytes 786440 | tf_op jit(solution)/shard_map/ppermute | solution.py:400
  58.9 10.7 %collective-permute-start.22 = (f32[128,512]{1,0:T(8,128)S(1)}, f32[128,512]{1,0:T(8,128)S(1)}, u32[]{:S(2)}, u32[]{:S(2)}) collective-permute-start(f32[128,512]{1,0:T(8,128)S(1)} %shard_map.94.refs_1_), channel_id=1, source_target_pairs={{0,1},{1,0},{2,3},{3,2},{4,5},{5,4},{6,7},{7,6},{8,9},{9,8},{10,11... | collective-permute-start | bytes 786440 | tf_op jit(solution)/shard_map/ppermute | solution.py:400
  61.6 12.2 %collective-permute-start.12 = (f32[96,1024]{1,0:T(8,128)S(1)}, f32[96,1024]{1,0:T(8,128)S(1)}, u32[]{:S(2)}, u32[]{:S(2)}) collective-permute-start(f32[96,1024]{1,0:T(8,128)S(1)} %get-tuple-element.32), channel_id=1, source_target_pairs={{0,2},{1,3},{2,0},{3,1},{4,6},{5,7},{6,4},{7,5},{8,10},{9,11},{10,... | collective-permute-start | bytes 1179656 | tf_op jit(solution)/shard_map/ppermute | solution.py:400
  63.7 19.4 %collective-permute-start.13 = (f32[96,1024]{1,0:T(8,128)S(1)}, f32[96,1024]{1,0:T(8,128)S(1)}, u32[]{:S(2)}, u32[]{:S(2)}) collective-permute-start(f32[96,1024]{1,0:T(8,128)S(1)} %get-tuple-element.33), channel_id=1, source_target_pairs={{0,4},{1,5},{2,6},{3,7},{4,0},{5,1},{6,2},{7,3},{8,12},{9,13},{10,... | collective-permute-start | bytes 1179656 | tf_op jit(solution)/shard_map/ppermute | solution.py:400
  65.5 18.1 %collective-permute-start.14 = (f32[96,1024]{1,0:T(8,128)S(1)}, f32[96,1024]{1,0:T(8,128)S(1)}, u32[]{:S(2)}, u32[]{:S(2)}) collective-permute-start(f32[96,1024]{1,0:T(8,128)S(1)} %get-tuple-element.34), channel_id=1, source_target_pairs={{0,6},{1,7},{2,4},{3,5},{4,2},{5,3},{6,0},{7,1},{8,14},{9,15},{10,... | collective-permute-start | bytes 1179656 | tf_op jit(solution)/shard_map/ppermute | solution.py:400
  73.1 12.1 %collective-permute-start.25 = (f32[288,128]{1,0:T(8,128)S(1)}, f32[288,128]{1,0:T(8,128)S(1)}, u32[]{:S(2)}, u32[]{:S(2)}) collective-permute-start(f32[288,128]{1,0:T(8,128)S(1)} %get-tuple-element.44), channel_id=1, source_target_pairs={{0,2},{1,3},{2,0},{3,1},{4,6},{5,7},{6,4},{7,5},{8,10},{9,11},{10,... | collective-permute-start | bytes 442376 | tf_op jit(solution)/shard_map/ppermute | solution.py:400
  73.7 15.5 %collective-permute-start.26 = (f32[288,128]{1,0:T(8,128)S(1)}, f32[288,128]{1,0:T(8,128)S(1)}, u32[]{:S(2)}, u32[]{:S(2)}) collective-permute-start(f32[288,128]{1,0:T(8,128)S(1)} %get-tuple-element.45), channel_id=1, source_target_pairs={{0,4},{1,5},{2,6},{3,7},{4,0},{5,1},{6,2},{7,3},{8,12},{9,13},{10,... | collective-permute-start | bytes 442376 | tf_op jit(solution)/shard_map/ppermute | solution.py:400
  73.8 15.4 %collective-permute-start.27 = (f32[288,128]{1,0:T(8,128)S(1)}, f32[288,128]{1,0:T(8,128)S(1)}, u32[]{:S(2)}, u32[]{:S(2)}) collective-permute-start(f32[288,128]{1,0:T(8,128)S(1)} %get-tuple-element.46), channel_id=1, source_target_pairs={{0,6},{1,7},{2,4},{3,5},{4,2},{5,3},{6,0},{7,1},{8,14},{9,15},{10,... | collective-permute-start | bytes 442376 | tf_op jit(solution)/shard_map/ppermute | solution.py:400
  (12 other events, 94.0 us)

commit v4 on v3

--- a/solution.py
+++ b/solution.py
@@ -92,6 +92,8 @@
 EXTRA = 8
 COLLECT_FIRST = 6_400_000_000
 COLLECT_LAST = 3_000_000_000
+NEAR_FIRST = 1_000_000_000
+NEAR_LAST = 0
 MULTIPLY_FIRST = 1_300_000_000
 MULTIPLY_LAST = 1_000_000_000
 BF16 = jnp.bfloat16
@@ -270,19 +272,18 @@
     gather_blocks(held, own, near, got)
     x = held[...]
     each = outs[0].shape[0]
+    g = jnp.dot(slot_terms[...], x, preferred_element_type=F32)
     for m, out in enumerate(outs):
-        out[...] = jnp.dot(
-            slot_terms[m * each : (m + 1) * each, :], x, preferred_element_type=F32
-        )
+        out[...] = g[m * each : (m + 1) * each]
 
 
 def column_sums(heads, row_terms, held, sums_ref):
     x = held[...]
     each = row_terms.shape[0] // heads
+    every = jnp.dot(row_terms[...], x, preferred_element_type=F32)
     for m in range(heads):
-        g = jnp.dot(row_terms[m * each : (m + 1) * each, :], x, preferred_element_type=F32)
         for p in range(PROJ - 1):
-            part = g[p * DKV : (p + 1) * DKV]
+            part = every[m * each + p * DKV : m * each + (p + 1) * DKV]
             sums_ref[m, p : p + 1, :] = jnp.sum(part * part + EPS_SQUARE, axis=0, keepdims=True)
 
 
@@ -293,8 +294,9 @@
     each = DKV + slots
     width = x.shape[1]
     base = width // 128 * slots
+    every = jnp.dot(terms[...], x, preferred_element_type=F32)
     for m, out in enumerate(outs):
-        g = jnp.dot(terms[m * each : (m + 1) * each, :], x, preferred_element_type=F32)
+        g = every[m * each : (m + 1) * each]
         part = g[:DKV]
         last = jnp.sum(part * part + EPS_SQUARE, axis=0, keepdims=True)
         sums = jnp.concatenate([sums_ref[m, : PROJ - 1, :], last], axis=0)
@@ -443,9 +445,9 @@
         here = call(body, outs, arrays=len(arrays), flops=cost)(*arrays)
         return here, [move(block, every, swap) for block in here]
 
-    def joined(cost, parts, up1, down1, up2, down2, up3, down3):
-        one, one_n = chosen(near_one, 1, 0, up1, down1)
-        two, two_n = chosen(two_away, 1, 0, up2, down2)
+    def joined(cost, before, parts, up1, down1, up2, down2, up3, down3):
+        one, one_n = chosen(near_one, 1, before, up1, down1)
+        two, two_n = chosen(two_away, 1, before, up2, down2)
         three, three_n = chosen(last_one, parts, cost, up1, up3, down3)
         return *one, *two, *three, *one_n, *two_n, *three_n
 
@@ -462,7 +464,7 @@
     late = lax.optimization_barrier((own1, hc))[0]
     nup1, ndown1 = move(late, upward), move(late, downward)
     up3, down3 = move(up2, upward), move(down2, downward)
-    blocks0 = joined(COLLECT_FIRST, 1, up1, down1, up2, down2, up3, down3)
+    blocks0 = joined(COLLECT_FIRST, NEAR_FIRST, 1, up1, down1, up2, down2, up3, down3)
     nup2, ndown2 = move(nup1, upward), move(ndown1, downward)
     slot_terms, row_terms, last_terms, live, state, total = call(
         functools.partial(prepare, heads, rows, pair_most),
@@ -489,7 +491,7 @@
     )(row_terms, held0)
     first = scatter(outs)
     nup3, ndown3 = move(nup2, upward), move(ndown2, downward)
-    blocks1 = joined(COLLECT_LAST, 2, nup1, ndown1, nup2, ndown2, nup3, ndown3)
+    blocks1 = joined(COLLECT_LAST, NEAR_LAST, 2, nup1, ndown1, nup2, ndown2, nup3, ndown3)
     rest = slots - cut
     last = scatter(
         call(

time: 92 us -> 91.5 us (level)
  waiting for transfers between devices: 19.9 us -> 21.8 us
  Pallas kernels: 15.3 us -> 13.5 us
    ppermute x28, waiting for transfers between devices: 19.9 us -> 21.8 us  [move(): return lax.ppermute(array, ('dp', 'shard'), pairs)]
    pallas_call x1, Pallas kernels: 1.97 us -> 0.67 us  [gather_step(): call(functools.partial(multiply_last, len(blocks1), rest), [jax.ShapeDtyp...]
  transfers between devices with their start and end apart: 29 -> 29, of which waited for: 8 -> 8; matrix products, arithmetic and copies ran while one was open for 0% -> 0% of each run, Pallas kernels for 13% -> 11%
where the time goes in v4:
time: 91.5 us; the launch traced here: 90.5 us
  starting transfers between devices  52.8 us (58%)
  waiting for transfers between devices  21.8 us (24%)
  Pallas kernels  13.5 us (15%)
  local copies, waits for them, and re-layouts  1.41 us (2%)
  between operations  1.01 us (1%)
    ppermute x28, starting transfers between devices, move(): return lax.ppermute(array, ('dp', 'shard'), pairs)  49 us
    ppermute x28, waiting for transfers between devices, move(): return lax.ppermute(array, ('dp', 'shard'), pairs)  21.8 us
    all_to_all x1, starting transfers between devices, exchange(): return lax.all_to_all(everywhere, 'shard', 0, 0, axis_index_groups=chips)  3.85 us
    pallas_call x6, Pallas kernels, chosen(): here = call(body, outs, arrays=len(arrays), flops=cost)(*arrays)  3.34 us
    pallas_call x1, Pallas kernels, gather_step(): pl.pallas_call(columns, out_shape=[jax.ShapeDtypeStruct((tokens, half), F...  2.09 us
    pallas_call x1, Pallas kernels, gather_step(): call(functools.partial(multiply, len(blocks0)), [jax.ShapeDtypeStruct((cu...  1.99 us
  transfers between devices with their start and end apart: 29, of which 8 were waited for; matrix products, arithmetic and copies ran while one was open for 0% of the time, Pallas kernels for 11%

profile of v4, /device:TPU:0, one launch (start us, length us, event | category | flops | bytes accessed | tf_op | source)
XLA Modules:
  0.0 90.5 jit_solution(831375027474614630)
XLA Ops:
  0.6 1.6 %shard_map.85.refs_0_ = f32[264,128]{1,0:T(8,128)} custom-call(bf16[128,256]{1,0:T(8,128)(2,1)} %bitcast.8, s32[1,256]{1,0:T(1,128)} %bitcast.9, f32[1,128]{1,0:T(1,128)} %state_hbm.1), custom_call_target="tpu_custom_call" | custom-call | tf_op jit(solution)/shard_map/pallas_call | solution.py:410
  2.3 3.1 %collective-permute-start = (f32[264,128]{1,0:T(8,128)}, f32[264,128]{1,0:T(8,128)S(1)}, u32[]{:S(2)}, u32[]{:S(2)}) collective-permute-start(f32[264,128]{1,0:T(8,128)} %shard_map.85.refs_0_), channel_id=1, source_target_pairs={{0,8},{1,9},{2,10},{3,11},{4,12},{5,13},{6,14},{7,15},{8,16},{9,17... | collective-permute-start | bytes 405512 | tf_op jit(solution)/shard_map/ppermute | solution.py:402
  5.3 2.1 %collective-permute-start.1 = (f32[264,128]{1,0:T(8,128)}, f32[264,128]{1,0:T(8,128)S(1)}, u32[]{:S(2)}, u32[]{:S(2)}) collective-permute-start(f32[264,128]{1,0:T(8,128)} %shard_map.85.refs_0_), channel_id=1, source_target_pairs={{0,24},{1,25},{2,26},{3,27},{4,28},{5,29},{6,30},{7,31},{8,0},{9,1... | collective-permute-start | bytes 405512 | tf_op jit(solution)/shard_map/ppermute | solution.py:402
  8.4 2.1 %shard_map.88 = (f32[128,512]{1,0:T(8,128)}, f32[128,512]{1,0:T(8,128)}, f32[128,512]{1,0:T(8,128)}, f32[128,512]{1,0:T(8,128)}) custom-call(bf16[128,2,4096]{2,1,0:T(2,128)(2,1)} %inputs_hbm.1), custom_call_target="tpu_custom_call" | custom-call | tf_op jit(solution)/shard_map/pallas_call | solution.py:423
  10.5 3.5 %collective-permute-start.3 = (f32[128,512]{1,0:T(8,128)}, f32[128,512]{1,0:T(8,128)S(1)}, u32[]{:S(2)}, u32[]{:S(2)}) collective-permute-start(f32[128,512]{1,0:T(8,128)} %get-tuple-element.29.own), channel_id=1, source_target_pairs={{0,8},{1,9},{2,10},{3,11},{4,12},{5,13},{6,14},{7,15},{8,16},{9,17... | collective-permute-start | bytes 786440 | tf_op jit(solution)/shard_map/ppermute | solution.py:402
  15.3 4.7 %collective-permute-done.2.refs_3_ = f32[264,128]{1,0:T(8,128)S(1)} collective-permute-done((f32[264,128]{1,0:T(8,128)}, f32[264,128]{1,0:T(8,128)S(1)}, u32[]{:S(2)}, u32[]{:S(2)}) %collective-permute-start.2) | collective-permute-done | bytes 135200 | tf_op jit(solution)/shard_map/ppermute | solution.py:402
  20.3 1.4 %copy-done = f32[4,264,512]{2,1,0:T(8,128)} copy-done((f32[4,264,512]{2,1,0:T(8,128)}, f32[4,264,512]{2,1,0:T(8,128)S(1)}, u32[]{:S(2)}) %copy-start) | copy-done | bytes 2162712
  21.7 3.8 %all-to-all-start = ((f32[4,264,512]{2,1,0:T(8,128)}), f32[4,264,512]{2,1,0:T(8,128)S(1)}, u32[]{:S(2)}, u32[]{:S(2)}) async-start(f32[4,264,512]{2,1,0:T(8,128)} %copy-done), calls=%async_computation | async-start | bytes 4325376 | tf_op jit(solution)/shard_map/all_to_all | solution.py:441
  28.2 4.6 %collective-permute-start.15 = (f32[128,512]{1,0:T(8,128)S(1)}, f32[128,512]{1,0:T(8,128)S(1)}, u32[]{:S(2)}, u32[]{:S(2)}) collective-permute-start(f32[128,512]{1,0:T(8,128)S(1)} %copy-done.4), channel_id=1, source_target_pairs={{0,8},{1,9},{2,10},{3,11},{4,12},{5,13},{6,14},{7,15},{8,16},{9,17... | collective-permute-start | bytes 786440 | tf_op jit(solution)/shard_map/ppermute | solution.py:402
  34.1 4.6 %collective-permute-start.7 = (f32[128,512]{1,0:T(8,128)S(1)}, f32[128,512]{1,0:T(8,128)S(1)}, u32[]{:S(2)}, u32[]{:S(2)}) collective-permute-start(f32[128,512]{1,0:T(8,128)S(1)} %collective-permute-done.5.up2), channel_id=1, source_target_pairs={{0,8},{1,9},{2,10},{3,11},{4,12},{5,13},{6,14},{7,15},{8,16},{9,17... | collective-permute-start | bytes 786440 | tf_op jit(solution)/shard_map/ppermute | solution.py:402
  40.7 4.6 %collective-permute-start.17 = (f32[128,512]{1,0:T(8,128)S(1)}, f32[128,512]{1,0:T(8,128)S(1)}, u32[]{:S(2)}, u32[]{:S(2)}) collective-permute-start(f32[128,512]{1,0:T(8,128)S(1)} %collective-permute-done.15.up1), channel_id=1, source_target_pairs={{0,8},{1,9},{2,10},{3,11},{4,12},{5,13},{6,14},{7,15},{8,16},{9,17... | collective-permute-start | bytes 786440 | tf_op jit(solution)/shard_map/ppermute | solution.py:402
  45.3 1.4 %collective-permute-start.18 = (f32[128,512]{1,0:T(8,128)S(1)}, f32[128,512]{1,0:T(8,128)S(1)}, u32[]{:S(2)}, u32[]{:S(2)}) collective-permute-start(f32[128,512]{1,0:T(8,128)S(1)} %collective-permute-done.16.down1), channel_id=1, source_target_pairs={{8,0},{9,1},{10,2},{11,3},{12,4},{13,5},{14,6},{15,7},{16,8},{17,9... | collective-permute-start | bytes 786440 | tf_op jit(solution)/shard_map/ppermute | solution.py:402
  48.8 2.7 %collective-permute-done.17.up2 = f32[128,512]{1,0:T(8,128)S(1)} collective-permute-done((f32[128,512]{1,0:T(8,128)S(1)}, f32[128,512]{1,0:T(8,128)S(1)}, u32[]{:S(2)}, u32[]{:S(2)}) %collective-permute-start.17) | collective-permute-done | bytes 262176 | tf_op jit(solution)/shard_map/ppermute | solution.py:402
  51.5 5.1 %collective-permute-start.19 = (f32[128,512]{1,0:T(8,128)S(1)}, f32[128,512]{1,0:T(8,128)}, u32[]{:S(2)}, u32[]{:S(2)}) collective-permute-start(f32[128,512]{1,0:T(8,128)S(1)} %collective-permute-done.17.up2), channel_id=1, source_target_pairs={{0,8},{1,9},{2,10},{3,11},{4,12},{5,13},{6,14},{7,15},{8,16},{9,17... | collective-permute-start | bytes 786440 | tf_op jit(solution)/shard_map/ppermute | solution.py:402
  59.1 2.0 %shard_map.92 = (f32[96,1024]{1,0:T(8,128)S(1)}, f32[96,1024]{1,0:T(8,128)S(1)}, f32[96,1024]{1,0:T(8,128)S(1)}, f32[96,1024]{1,0:T(8,128)S(1)}, bf16[512,1024]{1,0:T(8,128)(2,1)S(1)}) custom-call(bf16[384,512]{1,0:T(8,128)(2,1)S(1)} %get-tuple-element.28.slot_terms, f32[128,512]{1,0:T(8,128)S(1)} %copy-done.7, f32[128,512]{1,0:T(8,128)S(1)} %copy-done.8, ...), custom_call_target="tpu_custom_call" | custom-call | flops 1300000000 | tf_op jit(solution)/shard_map/pallas_call | solution.py:481
  61.1 2.1 %collective-permute-start.12 = (f32[96,1024]{1,0:T(8,128)S(1)}, f32[96,1024]{1,0:T(8,128)S(1)}, u32[]{:S(2)}, u32[]{:S(2)}) collective-permute-start(f32[96,1024]{1,0:T(8,128)S(1)} %get-tuple-element.32), channel_id=1, source_target_pairs={{0,2},{1,3},{2,0},{3,1},{4,6},{5,7},{6,4},{7,5},{8,10},{9,11},{10,... | collective-permute-start | bytes 1179656 | tf_op jit(solution)/shard_map/ppermute | solution.py:402
  63.2 1.5 %collective-permute-start.13 = (f32[96,1024]{1,0:T(8,128)S(1)}, f32[96,1024]{1,0:T(8,128)S(1)}, u32[]{:S(2)}, u32[]{:S(2)}) collective-permute-start(f32[96,1024]{1,0:T(8,128)S(1)} %get-tuple-element.33), channel_id=1, source_target_pairs={{0,4},{1,5},{2,6},{3,7},{4,0},{5,1},{6,2},{7,3},{8,12},{9,13},{10,... | collective-permute-start | bytes 1179656 | tf_op jit(solution)/shard_map/ppermute | solution.py:402
  64.7 1.5 %collective-permute-done.20.down3 = f32[128,512]{1,0:T(8,128)} collective-permute-done((f32[128,512]{1,0:T(8,128)S(1)}, f32[128,512]{1,0:T(8,128)}, u32[]{:S(2)}, u32[]{:S(2)}) %collective-permute-start.20) | collective-permute-done | bytes 262176 | tf_op jit(solution)/shard_map/ppermute | solution.py:402
  66.2 2.9 %collective-permute-start.14 = (f32[96,1024]{1,0:T(8,128)S(1)}, f32[96,1024]{1,0:T(8,128)S(1)}, u32[]{:S(2)}, u32[]{:S(2)}) collective-permute-start(f32[96,1024]{1,0:T(8,128)S(1)} %get-tuple-element.34), channel_id=1, source_target_pairs={{0,6},{1,7},{2,4},{3,5},{4,2},{5,3},{6,0},{7,1},{8,14},{9,15},{10,... | collective-permute-start | bytes 1179656 | tf_op jit(solution)/shard_map/ppermute | solution.py:402
  73.2 2.9 %collective-permute-start.27 = (f32[288,128]{1,0:T(8,128)S(1)}, f32[288,128]{1,0:T(8,128)S(1)}, u32[]{:S(2)}, u32[]{:S(2)}) collective-permute-start(f32[288,128]{1,0:T(8,128)S(1)} %get-tuple-element.46), channel_id=1, source_target_pairs={{0,6},{1,7},{2,4},{3,5},{4,2},{5,3},{6,0},{7,1},{8,14},{9,15},{10,... | collective-permute-start | bytes 442376 | tf_op jit(solution)/shard_map/ppermute | solution.py:402
  76.1 6.5 %collective-permute-done.13.refs_2_ = f32[96,1024]{1,0:T(8,128)S(1)} collective-permute-done((f32[96,1024]{1,0:T(8,128)S(1)}, f32[96,1024]{1,0:T(8,128)S(1)}, u32[]{:S(2)}, u32[]{:S(2)}) %collective-permute-start.13) | collective-permute-done | bytes 393248 | tf_op jit(solution)/shard_map/ppermute | solution.py:402
  83.3 1.4 %collective-permute-done.25.refs_5_ = f32[288,128]{1,0:T(8,128)S(1)} collective-permute-done((f32[288,128]{1,0:T(8,128)S(1)}, f32[288,128]{1,0:T(8,128)S(1)}, u32[]{:S(2)}, u32[]{:S(2)}) %collective-permute-start.25) | collective-permute-done | bytes 147488 | tf_op jit(solution)/shard_map/ppermute | solution.py:402
  84.7 4.0 %collective-permute-done.26.refs_6_ = f32[288,128]{1,0:T(8,128)S(1)} collective-permute-done((f32[288,128]{1,0:T(8,128)S(1)}, f32[288,128]{1,0:T(8,128)S(1)}, u32[]{:S(2)}, u32[]{:S(2)}) %collective-permute-start.26) | collective-permute-done | bytes 147488 | tf_op jit(solution)/shard_map/ppermute | solution.py:402
  88.8 1.7 %shard_map.99 = (bf16[128,4096]{1,0:T(8,128)(2,1)}, f32[1,128]{1,0:T(1,128)}, f32[4,4096]{1,0:T(4,128)}) custom-call(f32[96,1024]{1,0:T(8,128)S(1)} %get-tuple-element.31.refs_0_, f32[96,1024]{1,0:T(8,128)S(1)} %collective-permute-done.12.refs_1_, f32[96,1024]{1,0:T(8,128)S(1)} %collective-permute-done.13.refs_2_, ...), custom_call_target="tpu_custom_call" | custom-call | bytes 4194304 | tf_op jit(solution)/shard_map/pallas_call | solution.py:510
  (71 shorter events, 17.8 us)
Async XLA Ops:
  2.3 13.0 %collective-permute-start = (f32[264,128]{1,0:T(8,128)}, f32[264,128]{1,0:T(8,128)S(1)}, u32[]{:S(2)}, u32[]{:S(2)}) collective-permute-start(f32[264,128]{1,0:T(8,128)} %shard_map.85.refs_0_), channel_id=1, source_target_pairs={{0,8},{1,9},{2,10},{3,11},{4,12},{5,13},{6,14},{7,15},{8,16},{9,17... | collective-permute-start | bytes 405512 | tf_op jit(solution)/shard_map/ppermute | solution.py:402
  5.3 10.0 %collective-permute-start.1 = (f32[264,128]{1,0:T(8,128)}, f32[264,128]{1,0:T(8,128)S(1)}, u32[]{:S(2)}, u32[]{:S(2)}) collective-permute-start(f32[264,128]{1,0:T(8,128)} %shard_map.85.refs_0_), channel_id=1, source_target_pairs={{0,24},{1,25},{2,26},{3,27},{4,28},{5,29},{6,30},{7,31},{8,0},{9,1... | collective-permute-start | bytes 405512 | tf_op jit(solution)/shard_map/ppermute | solution.py:402
  7.4 12.6 %collective-permute-start.2 = (f32[264,128]{1,0:T(8,128)}, f32[264,128]{1,0:T(8,128)S(1)}, u32[]{:S(2)}, u32[]{:S(2)}) collective-permute-start(f32[264,128]{1,0:T(8,128)} %shard_map.85.refs_0_), channel_id=1, source_target_pairs={{0,16},{1,17},{2,18},{3,19},{4,20},{5,21},{6,22},{7,23},{8,24},{9,... | collective-permute-start | bytes 405512 | tf_op jit(solution)/shard_map/ppermute | solution.py:402
  10.5 15.0 %collective-permute-start.3 = (f32[128,512]{1,0:T(8,128)}, f32[128,512]{1,0:T(8,128)S(1)}, u32[]{:S(2)}, u32[]{:S(2)}) collective-permute-start(f32[128,512]{1,0:T(8,128)} %get-tuple-element.29.own), channel_id=1, source_target_pairs={{0,8},{1,9},{2,10},{3,11},{4,12},{5,13},{6,14},{7,15},{8,16},{9,17... | collective-permute-start | bytes 786440 | tf_op jit(solution)/shard_map/ppermute | solution.py:402
  14.0 12.9 %collective-permute-start.4 = (f32[128,512]{1,0:T(8,128)}, f32[128,512]{1,0:T(8,128)S(1)}, u32[]{:S(2)}, u32[]{:S(2)}) collective-permute-start(f32[128,512]{1,0:T(8,128)} %get-tuple-element.29.own), channel_id=1, source_target_pairs={{8,0},{9,1},{10,2},{11,3},{12,4},{13,5},{14,6},{15,7},{16,8},{17,9... | collective-permute-start | bytes 786440 | tf_op jit(solution)/shard_map/ppermute | solution.py:402
  21.7 36.3 %all-to-all-start = ((f32[4,264,512]{2,1,0:T(8,128)}), f32[4,264,512]{2,1,0:T(8,128)S(1)}, u32[]{:S(2)}, u32[]{:S(2)}) async-start(f32[4,264,512]{2,1,0:T(8,128)} %copy-done), calls=%async_computation | async-start | bytes 4325376 | tf_op jit(solution)/shard_map/all_to_all | solution.py:441
  26.9 11.8 %collective-permute-start.6 = (f32[128,512]{1,0:T(8,128)S(1)}, f32[128,512]{1,0:T(8,128)S(1)}, u32[]{:S(2)}, u32[]{:S(2)}) collective-permute-start(f32[128,512]{1,0:T(8,128)S(1)} %collective-permute-done.4.down1), channel_id=1, source_target_pairs={{8,0},{9,1},{10,2},{11,3},{12,4},{13,5},{14,6},{15,7},{16,8},{17,9... | collective-permute-start | bytes 786440 | tf_op jit(solution)/shard_map/ppermute | solution.py:402
  28.2 12.5 %collective-permute-start.15 = (f32[128,512]{1,0:T(8,128)S(1)}, f32[128,512]{1,0:T(8,128)S(1)}, u32[]{:S(2)}, u32[]{:S(2)}) collective-permute-start(f32[128,512]{1,0:T(8,128)S(1)} %copy-done.4), channel_id=1, source_target_pairs={{0,8},{1,9},{2,10},{3,11},{4,12},{5,13},{6,14},{7,15},{8,16},{9,17... | collective-permute-start | bytes 786440 | tf_op jit(solution)/shard_map/ppermute | solution.py:402
  32.8 12.5 %collective-permute-start.16 = (f32[128,512]{1,0:T(8,128)S(1)}, f32[128,512]{1,0:T(8,128)S(1)}, u32[]{:S(2)}, u32[]{:S(2)}) collective-permute-start(f32[128,512]{1,0:T(8,128)S(1)} %copy-done.4), channel_id=1, source_target_pairs={{8,0},{9,1},{10,2},{11,3},{12,4},{13,5},{14,6},{15,7},{16,8},{17,9... | collective-permute-start | bytes 786440 | tf_op jit(solution)/shard_map/ppermute | solution.py:402
  34.1 13.4 %collective-permute-start.7 = (f32[128,512]{1,0:T(8,128)S(1)}, f32[128,512]{1,0:T(8,128)S(1)}, u32[]{:S(2)}, u32[]{:S(2)}) collective-permute-start(f32[128,512]{1,0:T(8,128)S(1)} %collective-permute-done.5.up2), channel_id=1, source_target_pairs={{0,8},{1,9},{2,10},{3,11},{4,12},{5,13},{6,14},{7,15},{8,16},{9,17... | collective-permute-start | bytes 786440 | tf_op jit(solution)/shard_map/ppermute | solution.py:402
  40.7 17.8 %collective-permute-start.9 = (f32[128,512]{1,0:T(8,128)}, f32[128,512]{1,0:T(8,128)}, u32[]{:S(2)}, u32[]{:S(2)}) collective-permute-start(f32[128,512]{1,0:T(8,128)} %shard_map.89.refs_0_), channel_id=1, source_target_pairs={{0,1},{1,0},{2,3},{3,2},{4,5},{5,4},{6,7},{7,6},{8,9},{9,8},{10,11... | collective-permute-start | bytes 786440 | tf_op jit(solution)/shard_map/ppermute | solution.py:402
  40.7 10.8 %collective-permute-start.17 = (f32[128,512]{1,0:T(8,128)S(1)}, f32[128,512]{1,0:T(8,128)S(1)}, u32[]{:S(2)}, u32[]{:S(2)}) collective-permute-start(f32[128,512]{1,0:T(8,128)S(1)} %collective-permute-done.15.up1), channel_id=1, source_target_pairs={{0,8},{1,9},{2,10},{3,11},{4,12},{5,13},{6,14},{7,15},{8,16},{9,17... | collective-permute-start | bytes 786440 | tf_op jit(solution)/shard_map/ppermute | solution.py:402
  45.3 11.3 %collective-permute-start.18 = (f32[128,512]{1,0:T(8,128)S(1)}, f32[128,512]{1,0:T(8,128)S(1)}, u32[]{:S(2)}, u32[]{:S(2)}) collective-permute-start(f32[128,512]{1,0:T(8,128)S(1)} %collective-permute-done.16.down1), channel_id=1, source_target_pairs={{8,0},{9,1},{10,2},{11,3},{12,4},{13,5},{14,6},{15,7},{16,8},{17,9... | collective-permute-start | bytes 786440 | tf_op jit(solution)/shard_map/ppermute | solution.py:402
  47.5 11.1 %collective-permute-start.10 = (f32[128,512]{1,0:T(8,128)}, f32[128,512]{1,0:T(8,128)}, u32[]{:S(2)}, u32[]{:S(2)}) collective-permute-start(f32[128,512]{1,0:T(8,128)} %shard_map.90.refs_1_), channel_id=1, source_target_pairs={{0,1},{1,0},{2,3},{3,2},{4,5},{5,4},{6,7},{7,6},{8,9},{9,8},{10,11... | collective-permute-start | bytes 786440 | tf_op jit(solution)/shard_map/ppermute | solution.py:402
  48.8 10.4 %collective-permute-start.11 = (f32[128,512]{1,0:T(8,128)}, f32[128,512]{1,0:T(8,128)}, u32[]{:S(2)}, u32[]{:S(2)}) collective-permute-start(f32[128,512]{1,0:T(8,128)} %shard_map.91.refs_2_), channel_id=1, source_target_pairs={{0,1},{1,0},{2,3},{3,2},{4,5},{5,4},{6,7},{7,6},{8,9},{9,8},{10,11... | collective-permute-start | bytes 786440 | tf_op jit(solution)/shard_map/ppermute | solution.py:402
  51.5 11.7 %collective-permute-start.19 = (f32[128,512]{1,0:T(8,128)S(1)}, f32[128,512]{1,0:T(8,128)}, u32[]{:S(2)}, u32[]{:S(2)}) collective-permute-start(f32[128,512]{1,0:T(8,128)S(1)} %collective-permute-done.17.up2), channel_id=1, source_target_pairs={{0,8},{1,9},{2,10},{3,11},{4,12},{5,13},{6,14},{7,15},{8,16},{9,17... | collective-permute-start | bytes 786440 | tf_op jit(solution)/shard_map/ppermute | solution.py:402
  58.5 11.7 %collective-permute-start.21 = (f32[128,512]{1,0:T(8,128)S(1)}, f32[128,512]{1,0:T(8,128)S(1)}, u32[]{:S(2)}, u32[]{:S(2)}) collective-permute-start(f32[128,512]{1,0:T(8,128)S(1)} %shard_map.93.refs_0_), channel_id=1, source_target_pairs={{0,1},{1,0},{2,3},{3,2},{4,5},{5,4},{6,7},{7,6},{8,9},{9,8},{10,11... | collective-permute-start | bytes 786440 | tf_op jit(solution)/shard_map/ppermute | solution.py:402
  58.6 11.7 %collective-permute-start.22 = (f32[128,512]{1,0:T(8,128)S(1)}, f32[128,512]{1,0:T(8,128)S(1)}, u32[]{:S(2)}, u32[]{:S(2)}) collective-permute-start(f32[128,512]{1,0:T(8,128)S(1)} %shard_map.94.refs_1_), channel_id=1, source_target_pairs={{0,1},{1,0},{2,3},{3,2},{4,5},{5,4},{6,7},{7,6},{8,9},{9,8},{10,11... | collective-permute-start | bytes 786440 | tf_op jit(solution)/shard_map/ppermute | solution.py:402
  61.1 12.1 %collective-permute-start.12 = (f32[96,1024]{1,0:T(8,128)S(1)}, f32[96,1024]{1,0:T(8,128)S(1)}, u32[]{:S(2)}, u32[]{:S(2)}) collective-permute-start(f32[96,1024]{1,0:T(8,128)S(1)} %get-tuple-element.32), channel_id=1, source_target_pairs={{0,2},{1,3},{2,0},{3,1},{4,6},{5,7},{6,4},{7,5},{8,10},{9,11},{10,... | collective-permute-start | bytes 1179656 | tf_op jit(solution)/shard_map/ppermute | solution.py:402
  63.2 19.4 %collective-permute-start.13 = (f32[96,1024]{1,0:T(8,128)S(1)}, f32[96,1024]{1,0:T(8,128)S(1)}, u32[]{:S(2)}, u32[]{:S(2)}) collective-permute-start(f32[96,1024]{1,0:T(8,128)S(1)} %get-tuple-element.33), channel_id=1, source_target_pairs={{0,4},{1,5},{2,6},{3,7},{4,0},{5,1},{6,2},{7,3},{8,12},{9,13},{10,... | collective-permute-start | bytes 1179656 | tf_op jit(solution)/shard_map/ppermute | solution.py:402
  66.2 16.9 %collective-permute-start.14 = (f32[96,1024]{1,0:T(8,128)S(1)}, f32[96,1024]{1,0:T(8,128)S(1)}, u32[]{:S(2)}, u32[]{:S(2)}) collective-permute-start(f32[96,1024]{1,0:T(8,128)S(1)} %get-tuple-element.34), channel_id=1, source_target_pairs={{0,6},{1,7},{2,4},{3,5},{4,2},{5,3},{6,0},{7,1},{8,14},{9,15},{10,... | collective-permute-start | bytes 1179656 | tf_op jit(solution)/shard_map/ppermute | solution.py:402
  72.5 12.2 %collective-permute-start.25 = (f32[288,128]{1,0:T(8,128)S(1)}, f32[288,128]{1,0:T(8,128)S(1)}, u32[]{:S(2)}, u32[]{:S(2)}) collective-permute-start(f32[288,128]{1,0:T(8,128)S(1)} %get-tuple-element.44), channel_id=1, source_target_pairs={{0,2},{1,3},{2,0},{3,1},{4,6},{5,7},{6,4},{7,5},{8,10},{9,11},{10,... | collective-permute-start | bytes 442376 | tf_op jit(solution)/shard_map/ppermute | solution.py:402
  73.1 15.6 %collective-permute-start.26 = (f32[288,128]{1,0:T(8,128)S(1)}, f32[288,128]{1,0:T(8,128)S(1)}, u32[]{:S(2)}, u32[]{:S(2)}) collective-permute-start(f32[288,128]{1,0:T(8,128)S(1)} %get-tuple-element.45), channel_id=1, source_target_pairs={{0,4},{1,5},{2,6},{3,7},{4,0},{5,1},{6,2},{7,3},{8,12},{9,13},{10,... | collective-permute-start | bytes 442376 | tf_op jit(solution)/shard_map/ppermute | solution.py:402
  73.2 15.6 %collective-permute-start.27 = (f32[288,128]{1,0:T(8,128)S(1)}, f32[288,128]{1,0:T(8,128)S(1)}, u32[]{:S(2)}, u32[]{:S(2)}) collective-permute-start(f32[288,128]{1,0:T(8,128)S(1)} %get-tuple-element.46), channel_id=1, source_target_pairs={{0,6},{1,7},{2,4},{3,5},{4,2},{5,3},{6,0},{7,1},{8,14},{9,15},{10,... | collective-permute-start | bytes 442376 | tf_op jit(solution)/shard_map/ppermute | solution.py:402
  (16 other events, 126.3 us)

commit v5 on v4

--- a/solution.py
+++ b/solution.py
@@ -153,7 +153,8 @@
     for c in range(2):
         for side in range(2):
             at = pl.multiple_of((core ^ side) * half, 128)
-            outs[2 * c + side][...] = inputs_ref[:, c, pl.ds(at, half)].astype(F32)
+            out = outs[2 * c + side]
+            out[...] = inputs_ref[:, c, pl.ds(at, half)].astype(F32).astype(out.dtype)
 
 
 def spread(*refs):
@@ -422,7 +423,7 @@
     )(head_terms[:, 0, :], owner_list[:, :, 0], row_state)
     own0, near0, own1, near1 = pl.pallas_call(
         columns,
-        out_shape=[jax.ShapeDtypeStruct((tokens, half), F32)] * 4,
+        out_shape=[jax.ShapeDtypeStruct((tokens, half), kind) for kind in (F32, BF16)] * 2,
         in_specs=[anywhere],
         out_specs=[in_vmem] * 4,
         scratch_shapes=[pltpu.VMEM((tokens, 2, span), BF16), pltpu.SemaphoreType.DMA(())],

time: 91.5 us -> 91.5 us (level)
  transfers between devices with their start and end apart: 29 -> 29, of which waited for: 8 -> 8; matrix products, arithmetic and copies ran while one was open for 0% -> 0% of each run, Pallas kernels for 11% -> 12%
where the time goes in v5:
time: 91.5 us; the launch traced here: 90.5 us
  starting transfers between devices  52.8 us (58%)
  waiting for transfers between devices  21.3 us (23%)
  Pallas kernels  13.9 us (15%)
  local copies, waits for them, and re-layouts  1.41 us (2%)
  between operations  1.01 us (1%)
    ppermute x28, starting transfers between devices, move(): return lax.ppermute(array, ('dp', 'shard'), pairs)  49 us
    ppermute x28, waiting for transfers between devices, move(): return lax.ppermute(array, ('dp', 'shard'), pairs)  21.3 us
    all_to_all x1, starting transfers between devices, exchange(): return lax.all_to_all(everywhere, 'shard', 0, 0, axis_index_groups=chips)  3.85 us
    pallas_call x6, Pallas kernels, chosen(): here = call(body, outs, arrays=len(arrays), flops=cost)(*arrays)  3.34 us
    pallas_call x1, Pallas kernels, gather_step(): pl.pallas_call(columns, out_shape=[jax.ShapeDtypeStruct((tokens, half), k...  2.56 us
    pallas_call x1, Pallas kernels, gather_step(): call(functools.partial(multiply, len(blocks0)), [jax.ShapeDtypeStruct((cu...  2 us
  transfers between devices with their start and end apart: 29, of which 8 were waited for; matrix products, arithmetic and copies ran while one was open for 0% of the time, Pallas kernels for 12%

profile of v5, /device:TPU:0, one launch (start us, length us, event | category | flops | bytes accessed | tf_op | source)
XLA Modules:
  0.0 90.5 jit_solution(10817792900635162307)
XLA Ops:
  0.6 1.6 %shard_map.85.refs_0_ = f32[264,128]{1,0:T(8,128)} custom-call(bf16[128,256]{1,0:T(8,128)(2,1)} %bitcast.8, s32[1,256]{1,0:T(1,128)} %bitcast.9, f32[1,128]{1,0:T(1,128)} %state_hbm.1), custom_call_target="tpu_custom_call" | custom-call | tf_op jit(solution)/shard_map/pallas_call | solution.py:411
  2.3 3.1 %collective-permute-start = (f32[264,128]{1,0:T(8,128)}, f32[264,128]{1,0:T(8,128)S(1)}, u32[]{:S(2)}, u32[]{:S(2)}) collective-permute-start(f32[264,128]{1,0:T(8,128)} %shard_map.85.refs_0_), channel_id=1, source_target_pairs={{0,8},{1,9},{2,10},{3,11},{4,12},{5,13},{6,14},{7,15},{8,16},{9,17... | collective-permute-start | bytes 405512 | tf_op jit(solution)/shard_map/ppermute | solution.py:403
  5.3 2.1 %collective-permute-start.1 = (f32[264,128]{1,0:T(8,128)}, f32[264,128]{1,0:T(8,128)S(1)}, u32[]{:S(2)}, u32[]{:S(2)}) collective-permute-start(f32[264,128]{1,0:T(8,128)} %shard_map.85.refs_0_), channel_id=1, source_target_pairs={{0,24},{1,25},{2,26},{3,27},{4,28},{5,29},{6,30},{7,31},{8,0},{9,1... | collective-permute-start | bytes 405512 | tf_op jit(solution)/shard_map/ppermute | solution.py:403
  8.4 2.6 %shard_map.88 = (f32[128,512]{1,0:T(8,128)}, bf16[128,512]{1,0:T(8,128)(2,1)}, f32[128,512]{1,0:T(8,128)}, bf16[128,512]{1,0:T(8,128)(2,1)}) custom-call(bf16[128,2,4096]{2,1,0:T(2,128)(2,1)} %inputs_hbm.1), custom_call_target="tpu_custom_call" | custom-call | tf_op jit(solution)/shard_map/pallas_call | solution.py:424
  10.9 3.5 %collective-permute-start.3 = (f32[128,512]{1,0:T(8,128)}, f32[128,512]{1,0:T(8,128)S(1)}, u32[]{:S(2)}, u32[]{:S(2)}) collective-permute-start(f32[128,512]{1,0:T(8,128)} %get-tuple-element.29.own), channel_id=1, source_target_pairs={{0,8},{1,9},{2,10},{3,11},{4,12},{5,13},{6,14},{7,15},{8,16},{9,17... | collective-permute-start | bytes 786440 | tf_op jit(solution)/shard_map/ppermute | solution.py:403
  15.8 4.2 %collective-permute-done.2.refs_3_ = f32[264,128]{1,0:T(8,128)S(1)} collective-permute-done((f32[264,128]{1,0:T(8,128)}, f32[264,128]{1,0:T(8,128)S(1)}, u32[]{:S(2)}, u32[]{:S(2)}) %collective-permute-start.2) | collective-permute-done | bytes 135200 | tf_op jit(solution)/shard_map/ppermute | solution.py:403
  20.3 1.4 %copy-done = f32[4,264,512]{2,1,0:T(8,128)} copy-done((f32[4,264,512]{2,1,0:T(8,128)}, f32[4,264,512]{2,1,0:T(8,128)S(1)}, u32[]{:S(2)}) %copy-start) | copy-done | bytes 2162712
  21.7 3.8 %all-to-all-start = ((f32[4,264,512]{2,1,0:T(8,128)}), f32[4,264,512]{2,1,0:T(8,128)S(1)}, u32[]{:S(2)}, u32[]{:S(2)}) async-start(f32[4,264,512]{2,1,0:T(8,128)} %copy-done), calls=%async_computation | async-start | bytes 4325376 | tf_op jit(solution)/shard_map/all_to_all | solution.py:442
  28.2 4.6 %collective-permute-start.15 = (f32[128,512]{1,0:T(8,128)S(1)}, f32[128,512]{1,0:T(8,128)S(1)}, u32[]{:S(2)}, u32[]{:S(2)}) collective-permute-start(f32[128,512]{1,0:T(8,128)S(1)} %copy-done.4), channel_id=1, source_target_pairs={{0,8},{1,9},{2,10},{3,11},{4,12},{5,13},{6,14},{7,15},{8,16},{9,17... | collective-permute-start | bytes 786440 | tf_op jit(solution)/shard_map/ppermute | solution.py:403
  34.1 4.6 %collective-permute-start.7 = (f32[128,512]{1,0:T(8,128)S(1)}, f32[128,512]{1,0:T(8,128)S(1)}, u32[]{:S(2)}, u32[]{:S(2)}) collective-permute-start(f32[128,512]{1,0:T(8,128)S(1)} %collective-permute-done.5.up2), channel_id=1, source_target_pairs={{0,8},{1,9},{2,10},{3,11},{4,12},{5,13},{6,14},{7,15},{8,16},{9,17... | collective-permute-start | bytes 786440 | tf_op jit(solution)/shard_map/ppermute | solution.py:403
  40.7 4.6 %collective-permute-start.17 = (f32[128,512]{1,0:T(8,128)S(1)}, f32[128,512]{1,0:T(8,128)S(1)}, u32[]{:S(2)}, u32[]{:S(2)}) collective-permute-start(f32[128,512]{1,0:T(8,128)S(1)} %collective-permute-done.15.up1), channel_id=1, source_target_pairs={{0,8},{1,9},{2,10},{3,11},{4,12},{5,13},{6,14},{7,15},{8,16},{9,17... | collective-permute-start | bytes 786440 | tf_op jit(solution)/shard_map/ppermute | solution.py:403
  45.3 1.4 %collective-permute-start.18 = (f32[128,512]{1,0:T(8,128)S(1)}, f32[128,512]{1,0:T(8,128)S(1)}, u32[]{:S(2)}, u32[]{:S(2)}) collective-permute-start(f32[128,512]{1,0:T(8,128)S(1)} %collective-permute-done.16.down1), channel_id=1, source_target_pairs={{8,0},{9,1},{10,2},{11,3},{12,4},{13,5},{14,6},{15,7},{16,8},{17,9... | collective-permute-start | bytes 786440 | tf_op jit(solution)/shard_map/ppermute | solution.py:403
  48.8 2.7 %collective-permute-done.17.up2 = f32[128,512]{1,0:T(8,128)S(1)} collective-permute-done((f32[128,512]{1,0:T(8,128)S(1)}, f32[128,512]{1,0:T(8,128)S(1)}, u32[]{:S(2)}, u32[]{:S(2)}) %collective-permute-start.17) | collective-permute-done | bytes 262176 | tf_op jit(solution)/shard_map/ppermute | solution.py:403
  51.5 5.1 %collective-permute-start.19 = (f32[128,512]{1,0:T(8,128)S(1)}, f32[128,512]{1,0:T(8,128)}, u32[]{:S(2)}, u32[]{:S(2)}) collective-permute-start(f32[128,512]{1,0:T(8,128)S(1)} %collective-permute-done.17.up2), channel_id=1, source_target_pairs={{0,8},{1,9},{2,10},{3,11},{4,12},{5,13},{6,14},{7,15},{8,16},{9,17... | collective-permute-start | bytes 786440 | tf_op jit(solution)/shard_map/ppermute | solution.py:403
  59.1 2.0 %shard_map.92 = (f32[96,1024]{1,0:T(8,128)S(1)}, f32[96,1024]{1,0:T(8,128)S(1)}, f32[96,1024]{1,0:T(8,128)S(1)}, f32[96,1024]{1,0:T(8,128)S(1)}, bf16[512,1024]{1,0:T(8,128)(2,1)S(1)}) custom-call(bf16[384,512]{1,0:T(8,128)(2,1)S(1)} %get-tuple-element.28.slot_terms, f32[128,512]{1,0:T(8,128)S(1)} %copy-done.6, bf16[128,512]{1,0:T(8,128)(2,1)S(1)} %copy-done.10, ...), custom_call_target="tpu_custom_call" | custom-call | flops 1300000000 | tf_op jit(solution)/shard_map/pallas_call | solution.py:482
  61.1 2.1 %collective-permute-start.12 = (f32[96,1024]{1,0:T(8,128)S(1)}, f32[96,1024]{1,0:T(8,128)S(1)}, u32[]{:S(2)}, u32[]{:S(2)}) collective-permute-start(f32[96,1024]{1,0:T(8,128)S(1)} %get-tuple-element.32), channel_id=1, source_target_pairs={{0,2},{1,3},{2,0},{3,1},{4,6},{5,7},{6,4},{7,5},{8,10},{9,11},{10,... | collective-permute-start | bytes 1179656 | tf_op jit(solution)/shard_map/ppermute | solution.py:403
  63.2 1.5 %collective-permute-start.13 = (f32[96,1024]{1,0:T(8,128)S(1)}, f32[96,1024]{1,0:T(8,128)S(1)}, u32[]{:S(2)}, u32[]{:S(2)}) collective-permute-start(f32[96,1024]{1,0:T(8,128)S(1)} %get-tuple-element.33), channel_id=1, source_target_pairs={{0,4},{1,5},{2,6},{3,7},{4,0},{5,1},{6,2},{7,3},{8,12},{9,13},{10,... | collective-permute-start | bytes 1179656 | tf_op jit(solution)/shard_map/ppermute | solution.py:403
  64.7 1.5 %collective-permute-done.20.down3 = f32[128,512]{1,0:T(8,128)} collective-permute-done((f32[128,512]{1,0:T(8,128)S(1)}, f32[128,512]{1,0:T(8,128)}, u32[]{:S(2)}, u32[]{:S(2)}) %collective-permute-start.20) | collective-permute-done | bytes 262176 | tf_op jit(solution)/shard_map/ppermute | solution.py:403
  66.2 2.9 %collective-permute-start.14 = (f32[96,1024]{1,0:T(8,128)S(1)}, f32[96,1024]{1,0:T(8,128)S(1)}, u32[]{:S(2)}, u32[]{:S(2)}) collective-permute-start(f32[96,1024]{1,0:T(8,128)S(1)} %get-tuple-element.34), channel_id=1, source_target_pairs={{0,6},{1,7},{2,4},{3,5},{4,2},{5,3},{6,0},{7,1},{8,14},{9,15},{10,... | collective-permute-start | bytes 1179656 | tf_op jit(solution)/shard_map/ppermute | solution.py:403
  73.2 2.9 %collective-permute-start.27 = (f32[288,128]{1,0:T(8,128)S(1)}, f32[288,128]{1,0:T(8,128)S(1)}, u32[]{:S(2)}, u32[]{:S(2)}) collective-permute-start(f32[288,128]{1,0:T(8,128)S(1)} %get-tuple-element.46), channel_id=1, source_target_pairs={{0,6},{1,7},{2,4},{3,5},{4,2},{5,3},{6,0},{7,1},{8,14},{9,15},{10,... | collective-permute-start | bytes 442376 | tf_op jit(solution)/shard_map/ppermute | solution.py:403
  76.1 6.6 %collective-permute-done.13.refs_2_ = f32[96,1024]{1,0:T(8,128)S(1)} collective-permute-done((f32[96,1024]{1,0:T(8,128)S(1)}, f32[96,1024]{1,0:T(8,128)S(1)}, u32[]{:S(2)}, u32[]{:S(2)}) %collective-permute-start.13) | collective-permute-done | bytes 393248 | tf_op jit(solution)/shard_map/ppermute | solution.py:403
  83.3 1.4 %collective-permute-done.25.refs_5_ = f32[288,128]{1,0:T(8,128)S(1)} collective-permute-done((f32[288,128]{1,0:T(8,128)S(1)}, f32[288,128]{1,0:T(8,128)S(1)}, u32[]{:S(2)}, u32[]{:S(2)}) %collective-permute-start.25) | collective-permute-done | bytes 147488 | tf_op jit(solution)/shard_map/ppermute | solution.py:403
  84.7 4.0 %collective-permute-done.26.refs_6_ = f32[288,128]{1,0:T(8,128)S(1)} collective-permute-done((f32[288,128]{1,0:T(8,128)S(1)}, f32[288,128]{1,0:T(8,128)S(1)}, u32[]{:S(2)}, u32[]{:S(2)}) %collective-permute-start.26) | collective-permute-done | bytes 147488 | tf_op jit(solution)/shard_map/ppermute | solution.py:403
  88.8 1.7 %shard_map.99 = (bf16[128,4096]{1,0:T(8,128)(2,1)}, f32[1,128]{1,0:T(1,128)}, f32[4,4096]{1,0:T(4,128)}) custom-call(f32[96,1024]{1,0:T(8,128)S(1)} %get-tuple-element.31.refs_0_, f32[96,1024]{1,0:T(8,128)S(1)} %collective-permute-done.12.refs_1_, f32[96,1024]{1,0:T(8,128)S(1)} %collective-permute-done.13.refs_2_, ...), custom_call_target="tpu_custom_call" | custom-call | bytes 4194304 | tf_op jit(solution)/shard_map/pallas_call | solution.py:511
  (71 shorter events, 17.8 us)
Async XLA Ops:
  2.3 13.5 %collective-permute-start = (f32[264,128]{1,0:T(8,128)}, f32[264,128]{1,0:T(8,128)S(1)}, u32[]{:S(2)}, u32[]{:S(2)}) collective-permute-start(f32[264,128]{1,0:T(8,128)} %shard_map.85.refs_0_), channel_id=1, source_target_pairs={{0,8},{1,9},{2,10},{3,11},{4,12},{5,13},{6,14},{7,15},{8,16},{9,17... | collective-permute-start | bytes 405512 | tf_op jit(solution)/shard_map/ppermute | solution.py:403
  5.3 10.4 %collective-permute-start.1 = (f32[264,128]{1,0:T(8,128)}, f32[264,128]{1,0:T(8,128)S(1)}, u32[]{:S(2)}, u32[]{:S(2)}) collective-permute-start(f32[264,128]{1,0:T(8,128)} %shard_map.85.refs_0_), channel_id=1, source_target_pairs={{0,24},{1,25},{2,26},{3,27},{4,28},{5,29},{6,30},{7,31},{8,0},{9,1... | collective-permute-start | bytes 405512 | tf_op jit(solution)/shard_map/ppermute | solution.py:403
  7.4 12.6 %collective-permute-start.2 = (f32[264,128]{1,0:T(8,128)}, f32[264,128]{1,0:T(8,128)S(1)}, u32[]{:S(2)}, u32[]{:S(2)}) collective-permute-start(f32[264,128]{1,0:T(8,128)} %shard_map.85.refs_0_), channel_id=1, source_target_pairs={{0,16},{1,17},{2,18},{3,19},{4,20},{5,21},{6,22},{7,23},{8,24},{9,... | collective-permute-start | bytes 405512 | tf_op jit(solution)/shard_map/ppermute | solution.py:403
  10.9 14.6 %collective-permute-start.3 = (f32[128,512]{1,0:T(8,128)}, f32[128,512]{1,0:T(8,128)S(1)}, u32[]{:S(2)}, u32[]{:S(2)}) collective-permute-start(f32[128,512]{1,0:T(8,128)} %get-tuple-element.29.own), channel_id=1, source_target_pairs={{0,8},{1,9},{2,10},{3,11},{4,12},{5,13},{6,14},{7,15},{8,16},{9,17... | collective-permute-start | bytes 786440 | tf_op jit(solution)/shard_map/ppermute | solution.py:403
  14.5 12.4 %collective-permute-start.4 = (f32[128,512]{1,0:T(8,128)}, f32[128,512]{1,0:T(8,128)S(1)}, u32[]{:S(2)}, u32[]{:S(2)}) collective-permute-start(f32[128,512]{1,0:T(8,128)} %get-tuple-element.29.own), channel_id=1, source_target_pairs={{8,0},{9,1},{10,2},{11,3},{12,4},{13,5},{14,6},{15,7},{16,8},{17,9... | collective-permute-start | bytes 786440 | tf_op jit(solution)/shard_map/ppermute | solution.py:403
  21.7 36.3 %all-to-all-start = ((f32[4,264,512]{2,1,0:T(8,128)}), f32[4,264,512]{2,1,0:T(8,128)S(1)}, u32[]{:S(2)}, u32[]{:S(2)}) async-start(f32[4,264,512]{2,1,0:T(8,128)} %copy-done), calls=%async_computation | async-start | bytes 4325376 | tf_op jit(solution)/shard_map/all_to_all | solution.py:442
  26.9 11.8 %collective-permute-start.6 = (f32[128,512]{1,0:T(8,128)S(1)}, f32[128,512]{1,0:T(8,128)S(1)}, u32[]{:S(2)}, u32[]{:S(2)}) collective-permute-start(f32[128,512]{1,0:T(8,128)S(1)} %collective-permute-done.4.down1), channel_id=1, source_target_pairs={{8,0},{9,1},{10,2},{11,3},{12,4},{13,5},{14,6},{15,7},{16,8},{17,9... | collective-permute-start | bytes 786440 | tf_op jit(solution)/shard_map/ppermute | solution.py:403
  28.2 12.5 %collective-permute-start.15 = (f32[128,512]{1,0:T(8,128)S(1)}, f32[128,512]{1,0:T(8,128)S(1)}, u32[]{:S(2)}, u32[]{:S(2)}) collective-permute-start(f32[128,512]{1,0:T(8,128)S(1)} %copy-done.4), channel_id=1, source_target_pairs={{0,8},{1,9},{2,10},{3,11},{4,12},{5,13},{6,14},{7,15},{8,16},{9,17... | collective-permute-start | bytes 786440 | tf_op jit(solution)/shard_map/ppermute | solution.py:403
  32.8 12.5 %collective-permute-start.16 = (f32[128,512]{1,0:T(8,128)S(1)}, f32[128,512]{1,0:T(8,128)S(1)}, u32[]{:S(2)}, u32[]{:S(2)}) collective-permute-start(f32[128,512]{1,0:T(8,128)S(1)} %copy-done.4), channel_id=1, source_target_pairs={{8,0},{9,1},{10,2},{11,3},{12,4},{13,5},{14,6},{15,7},{16,8},{17,9... | collective-permute-start | bytes 786440 | tf_op jit(solution)/shard_map/ppermute | solution.py:403
  34.1 13.4 %collective-permute-start.7 = (f32[128,512]{1,0:T(8,128)S(1)}, f32[128,512]{1,0:T(8,128)S(1)}, u32[]{:S(2)}, u32[]{:S(2)}) collective-permute-start(f32[128,512]{1,0:T(8,128)S(1)} %collective-permute-done.5.up2), channel_id=1, source_target_pairs={{0,8},{1,9},{2,10},{3,11},{4,12},{5,13},{6,14},{7,15},{8,16},{9,17... | collective-permute-start | bytes 786440 | tf_op jit(solution)/shard_map/ppermute | solution.py:403
  40.7 17.8 %collective-permute-start.9 = (f32[128,512]{1,0:T(8,128)}, f32[128,512]{1,0:T(8,128)}, u32[]{:S(2)}, u32[]{:S(2)}) collective-permute-start(f32[128,512]{1,0:T(8,128)} %shard_map.89.refs_0_), channel_id=1, source_target_pairs={{0,1},{1,0},{2,3},{3,2},{4,5},{5,4},{6,7},{7,6},{8,9},{9,8},{10,11... | collective-permute-start | bytes 786440 | tf_op jit(solution)/shard_map/ppermute | solution.py:403
  40.7 10.8 %collective-permute-start.17 = (f32[128,512]{1,0:T(8,128)S(1)}, f32[128,512]{1,0:T(8,128)S(1)}, u32[]{:S(2)}, u32[]{:S(2)}) collective-permute-start(f32[128,512]{1,0:T(8,128)S(1)} %collective-permute-done.15.up1), channel_id=1, source_target_pairs={{0,8},{1,9},{2,10},{3,11},{4,12},{5,13},{6,14},{7,15},{8,16},{9,17... | collective-permute-start | bytes 786440 | tf_op jit(solution)/shard_map/ppermute | solution.py:403
  45.3 11.3 %collective-permute-start.18 = (f32[128,512]{1,0:T(8,128)S(1)}, f32[128,512]{1,0:T(8,128)S(1)}, u32[]{:S(2)}, u32[]{:S(2)}) collective-permute-start(f32[128,512]{1,0:T(8,128)S(1)} %collective-permute-done.16.down1), channel_id=1, source_target_pairs={{8,0},{9,1},{10,2},{11,3},{12,4},{13,5},{14,6},{15,7},{16,8},{17,9... | collective-permute-start | bytes 786440 | tf_op jit(solution)/shard_map/ppermute | solution.py:403
  47.5 11.1 %collective-permute-start.10 = (f32[128,512]{1,0:T(8,128)}, f32[128,512]{1,0:T(8,128)}, u32[]{:S(2)}, u32[]{:S(2)}) collective-permute-start(f32[128,512]{1,0:T(8,128)} %shard_map.90.refs_1_), channel_id=1, source_target_pairs={{0,1},{1,0},{2,3},{3,2},{4,5},{5,4},{6,7},{7,6},{8,9},{9,8},{10,11... | collective-permute-start | bytes 786440 | tf_op jit(solution)/shard_map/ppermute | solution.py:403
  48.7 10.3 %collective-permute-start.11 = (f32[128,512]{1,0:T(8,128)}, f32[128,512]{1,0:T(8,128)}, u32[]{:S(2)}, u32[]{:S(2)}) collective-permute-start(f32[128,512]{1,0:T(8,128)} %shard_map.91.refs_2_), channel_id=1, source_target_pairs={{0,1},{1,0},{2,3},{3,2},{4,5},{5,4},{6,7},{7,6},{8,9},{9,8},{10,11... | collective-permute-start | bytes 786440 | tf_op jit(solution)/shard_map/ppermute | solution.py:403
  51.5 11.7 %collective-permute-start.19 = (f32[128,512]{1,0:T(8,128)S(1)}, f32[128,512]{1,0:T(8,128)}, u32[]{:S(2)}, u32[]{:S(2)}) collective-permute-start(f32[128,512]{1,0:T(8,128)S(1)} %collective-permute-done.17.up2), channel_id=1, source_target_pairs={{0,8},{1,9},{2,10},{3,11},{4,12},{5,13},{6,14},{7,15},{8,16},{9,17... | collective-permute-start | bytes 786440 | tf_op jit(solution)/shard_map/ppermute | solution.py:403
  58.5 11.7 %collective-permute-start.21 = (f32[128,512]{1,0:T(8,128)S(1)}, f32[128,512]{1,0:T(8,128)S(1)}, u32[]{:S(2)}, u32[]{:S(2)}) collective-permute-start(f32[128,512]{1,0:T(8,128)S(1)} %shard_map.93.refs_0_), channel_id=1, source_target_pairs={{0,1},{1,0},{2,3},{3,2},{4,5},{5,4},{6,7},{7,6},{8,9},{9,8},{10,11... | collective-permute-start | bytes 786440 | tf_op jit(solution)/shard_map/ppermute | solution.py:403
  58.6 11.7 %collective-permute-start.22 = (f32[128,512]{1,0:T(8,128)S(1)}, f32[128,512]{1,0:T(8,128)S(1)}, u32[]{:S(2)}, u32[]{:S(2)}) collective-permute-start(f32[128,512]{1,0:T(8,128)S(1)} %shard_map.94.refs_1_), channel_id=1, source_target_pairs={{0,1},{1,0},{2,3},{3,2},{4,5},{5,4},{6,7},{7,6},{8,9},{9,8},{10,11... | collective-permute-start | bytes 786440 | tf_op jit(solution)/shard_map/ppermute | solution.py:403
  61.1 12.1 %collective-permute-start.12 = (f32[96,1024]{1,0:T(8,128)S(1)}, f32[96,1024]{1,0:T(8,128)S(1)}, u32[]{:S(2)}, u32[]{:S(2)}) collective-permute-start(f32[96,1024]{1,0:T(8,128)S(1)} %get-tuple-element.32), channel_id=1, source_target_pairs={{0,2},{1,3},{2,0},{3,1},{4,6},{5,7},{6,4},{7,5},{8,10},{9,11},{10,... | collective-permute-start | bytes 1179656 | tf_op jit(solution)/shard_map/ppermute | solution.py:403
  63.2 19.4 %collective-permute-start.13 = (f32[96,1024]{1,0:T(8,128)S(1)}, f32[96,1024]{1,0:T(8,128)S(1)}, u32[]{:S(2)}, u32[]{:S(2)}) collective-permute-start(f32[96,1024]{1,0:T(8,128)S(1)} %get-tuple-element.33), channel_id=1, source_target_pairs={{0,4},{1,5},{2,6},{3,7},{4,0},{5,1},{6,2},{7,3},{8,12},{9,13},{10,... | collective-permute-start | bytes 1179656 | tf_op jit(solution)/shard_map/ppermute | solution.py:403
  66.2 16.9 %collective-permute-start.14 = (f32[96,1024]{1,0:T(8,128)S(1)}, f32[96,1024]{1,0:T(8,128)S(1)}, u32[]{:S(2)}, u32[]{:S(2)}) collective-permute-start(f32[96,1024]{1,0:T(8,128)S(1)} %get-tuple-element.34), channel_id=1, source_target_pairs={{0,6},{1,7},{2,4},{3,5},{4,2},{5,3},{6,0},{7,1},{8,14},{9,15},{10,... | collective-permute-start | bytes 1179656 | tf_op jit(solution)/shard_map/ppermute | solution.py:403
  72.5 12.3 %collective-permute-start.25 = (f32[288,128]{1,0:T(8,128)S(1)}, f32[288,128]{1,0:T(8,128)S(1)}, u32[]{:S(2)}, u32[]{:S(2)}) collective-permute-start(f32[288,128]{1,0:T(8,128)S(1)} %get-tuple-element.44), channel_id=1, source_target_pairs={{0,2},{1,3},{2,0},{3,1},{4,6},{5,7},{6,4},{7,5},{8,10},{9,11},{10,... | collective-permute-start | bytes 442376 | tf_op jit(solution)/shard_map/ppermute | solution.py:403
  73.1 15.6 %collective-permute-start.26 = (f32[288,128]{1,0:T(8,128)S(1)}, f32[288,128]{1,0:T(8,128)S(1)}, u32[]{:S(2)}, u32[]{:S(2)}) collective-permute-start(f32[288,128]{1,0:T(8,128)S(1)} %get-tuple-element.45), channel_id=1, source_target_pairs={{0,4},{1,5},{2,6},{3,7},{4,0},{5,1},{6,2},{7,3},{8,12},{9,13},{10,... | collective-permute-start | bytes 442376 | tf_op jit(solution)/shard_map/ppermute | solution.py:403
  73.2 15.6 %collective-permute-start.27 = (f32[288,128]{1,0:T(8,128)S(1)}, f32[288,128]{1,0:T(8,128)S(1)}, u32[]{:S(2)}, u32[]{:S(2)}) collective-permute-start(f32[288,128]{1,0:T(8,128)S(1)} %get-tuple-element.46), channel_id=1, source_target_pairs={{0,6},{1,7},{2,4},{3,5},{4,2},{5,3},{6,0},{7,1},{8,14},{9,15},{10,... | collective-permute-start | bytes 442376 | tf_op jit(solution)/shard_map/ppermute | solution.py:403
  (16 other events, 126.3 us)

commit v6 on v4

--- a/solution.py
+++ b/solution.py
@@ -151,9 +151,13 @@
     copy.start()
     copy.wait()
     for c in range(2):
-        for side in range(2):
-            at = pl.multiple_of((core ^ side) * half, 128)
-            outs[2 * c + side][...] = inputs_ref[:, c, pl.ds(at, half)].astype(F32)
+        sent, own, near = outs[3 * c : 3 * c + 3]
+        at = pl.multiple_of(core * half, 128)
+        mine = inputs_ref[:, c, pl.ds(at, half)].astype(F32)
+        sent[...] = mine
+        own[...] = mine.astype(BF16)
+        at = pl.multiple_of((1 - core) * half, 128)
+        near[...] = inputs_ref[:, c, pl.ds(at, half)].astype(F32).astype(BF16)
 
 
 def spread(*refs):
@@ -420,11 +424,11 @@
         ],
         compiler_params=pltpu.CompilerParams(vmem_limit_bytes=BEGIN_LIMIT),
     )(head_terms[:, 0, :], owner_list[:, :, 0], row_state)
-    own0, near0, own1, near1 = pl.pallas_call(
+    sent0, own0, near0, sent1, own1, near1 = pl.pallas_call(
         columns,
-        out_shape=[jax.ShapeDtypeStruct((tokens, half), F32)] * 4,
+        out_shape=[jax.ShapeDtypeStruct((tokens, half), kind) for kind in (F32, BF16, BF16)] * 2,
         in_specs=[anywhere],
-        out_specs=[in_vmem] * 4,
+        out_specs=[in_vmem] * 6,
         scratch_shapes=[pltpu.VMEM((tokens, 2, span), BF16), pltpu.SemaphoreType.DMA(())],
         compiler_params=pltpu.CompilerParams(vmem_limit_bytes=BEGIN_LIMIT),
     )(inputs)
@@ -457,11 +461,11 @@
             for m, out in enumerate(outs)
         ]
 
-    up1, down1 = move(own0, upward), move(own0, downward)
+    up1, down1 = move(sent0, upward), move(sent0, downward)
     ha, hb, hc = [move(terms, ring(k)) for k in (1, dp_count - 1, 2)]
     gathered = exchange(terms, ha, hb, hc)
     up2, down2 = move(up1, upward), move(down1, downward)
-    late = lax.optimization_barrier((own1, hc))[0]
+    late = lax.optimization_barrier((sent1, hc))[0]
     nup1, ndown1 = move(late, upward), move(late, downward)
     up3, down3 = move(up2, upward), move(down2, downward)
     blocks0 = joined(COLLECT_FIRST, NEAR_FIRST, 1, up1, down1, up2, down2, up3, down3)

time: 91.5 us -> 91.4 us (level)
  waiting for transfers between devices: 21.8 us -> 20.7 us
  Pallas kernels: 13.5 us -> 14.6 us
    pallas_call x1, Pallas kernels: 2.09 us -> 3.22 us  [gather_step(): pl.pallas_call(columns, out_shape=[jax.ShapeDtypeStruct((tokens, half), k...]
    ppermute x28, waiting for transfers between devices: 21.8 us -> 20.7 us  [move(): return lax.ppermute(array, ('dp', 'shard'), pairs)]
  transfers between devices with their start and end apart: 29 -> 29, of which waited for: 8 -> 8; matrix products, arithmetic and copies ran while one was open for 0% -> 0% of each run, Pallas kernels for 11% -> 13%
where the time goes in v6:
time: 91.4 us; the launch traced here: 90.5 us
  starting transfers between devices  52.7 us (58%)
  waiting for transfers between devices  20.7 us (23%)
  Pallas kernels  14.6 us (16%)
  local copies, waits for them, and re-layouts  1.39 us (2%)
  between operations  0.99 us (1%)
    ppermute x28, starting transfers between devices, move(): return lax.ppermute(array, ('dp', 'shard'), pairs)  48.9 us
    ppermute x28, waiting for transfers between devices, move(): return lax.ppermute(array, ('dp', 'shard'), pairs)  20.7 us
    all_to_all x1, starting transfers between devices, exchange(): return lax.all_to_all(everywhere, 'shard', 0, 0, axis_index_groups=chips)  3.85 us
    pallas_call x6, Pallas kernels, chosen(): here = call(body, outs, arrays=len(arrays), flops=cost)(*arrays)  3.39 us
    pallas_call x1, Pallas kernels, gather_step(): pl.pallas_call(columns, out_shape=[jax.ShapeDtypeStruct((tokens, half), k...  3.22 us
    pallas_call x1, Pallas kernels, gather_step(): call(functools.partial(multiply, len(blocks0)), [jax.ShapeDtypeStruct((cu...  1.99 us
  transfers between devices with their start and end apart: 29, of which 8 were waited for; matrix products, arithmetic and copies ran while one was open for 0% of the time, Pallas kernels for 13%

profile of v6, /device:TPU:0, one launch (start us, length us, event | category | flops | bytes accessed | tf_op | source)
XLA Modules:
  0.0 90.5 jit_solution(3567848893320295256)
XLA Ops:
  0.6 1.6 %shard_map.85.refs_0_ = f32[264,128]{1,0:T(8,128)} custom-call(bf16[128,256]{1,0:T(8,128)(2,1)} %bitcast.8, s32[1,256]{1,0:T(1,128)} %bitcast.9, f32[1,128]{1,0:T(1,128)} %state_hbm.1), custom_call_target="tpu_custom_call" | custom-call | tf_op jit(solution)/shard_map/pallas_call | solution.py:414
  2.3 3.1 %collective-permute-start = (f32[264,128]{1,0:T(8,128)}, f32[264,128]{1,0:T(8,128)S(1)}, u32[]{:S(2)}, u32[]{:S(2)}) collective-permute-start(f32[264,128]{1,0:T(8,128)} %shard_map.85.refs_0_), channel_id=1, source_target_pairs={{0,8},{1,9},{2,10},{3,11},{4,12},{5,13},{6,14},{7,15},{8,16},{9,17... | collective-permute-start | bytes 405512 | tf_op jit(solution)/shard_map/ppermute | solution.py:406
  5.3 2.1 %collective-permute-start.1 = (f32[264,128]{1,0:T(8,128)}, f32[264,128]{1,0:T(8,128)S(1)}, u32[]{:S(2)}, u32[]{:S(2)}) collective-permute-start(f32[264,128]{1,0:T(8,128)} %shard_map.85.refs_0_), channel_id=1, source_target_pairs={{0,24},{1,25},{2,26},{3,27},{4,28},{5,29},{6,30},{7,31},{8,0},{9,1... | collective-permute-start | bytes 405512 | tf_op jit(solution)/shard_map/ppermute | solution.py:406
  8.4 3.2 %shard_map.88 = (f32[128,512]{1,0:T(8,128)}, bf16[128,512]{1,0:T(8,128)(2,1)}, bf16[128,512]{1,0:T(8,128)(2,1)}, f32[128,512]{1,0:T(8,128)}, bf16[128,512]{1,0:T(8,128)(2,1)}, /*index=5*/bf16[128,512]{1,0:T(8,128)(2,1)}) custom-call(bf16[128,2,4096]{2,1,0:T(2,128)(2,1)} %inputs_hbm.1), custom_call_target="tpu_custom_call" | custom-call | tf_op jit(solution)/shard_map/pallas_call | solution.py:427
  11.6 3.5 %collective-permute-start.3 = (f32[128,512]{1,0:T(8,128)}, f32[128,512]{1,0:T(8,128)S(1)}, u32[]{:S(2)}, u32[]{:S(2)}) collective-permute-start(f32[128,512]{1,0:T(8,128)} %get-tuple-element.33), channel_id=1, source_target_pairs={{0,8},{1,9},{2,10},{3,11},{4,12},{5,13},{6,14},{7,15},{8,16},{9,17... | collective-permute-start | bytes 786440 | tf_op jit(solution)/shard_map/ppermute | solution.py:406
  16.4 3.5 %collective-permute-done.2.refs_3_ = f32[264,128]{1,0:T(8,128)S(1)} collective-permute-done((f32[264,128]{1,0:T(8,128)}, f32[264,128]{1,0:T(8,128)S(1)}, u32[]{:S(2)}, u32[]{:S(2)}) %collective-permute-start.2) | collective-permute-done | bytes 135200 | tf_op jit(solution)/shard_map/ppermute | solution.py:406
  20.3 1.4 %copy-done = f32[4,264,512]{2,1,0:T(8,128)} copy-done((f32[4,264,512]{2,1,0:T(8,128)}, f32[4,264,512]{2,1,0:T(8,128)S(1)}, u32[]{:S(2)}) %copy-start) | copy-done | bytes 2162712
  21.6 3.8 %all-to-all-start = ((f32[4,264,512]{2,1,0:T(8,128)}), f32[4,264,512]{2,1,0:T(8,128)S(1)}, u32[]{:S(2)}, u32[]{:S(2)}) async-start(f32[4,264,512]{2,1,0:T(8,128)} %copy-done), calls=%async_computation | async-start | bytes 4325376 | tf_op jit(solution)/shard_map/all_to_all | solution.py:445
  25.5 1.4 %collective-permute-start.5 = (f32[128,512]{1,0:T(8,128)S(1)}, f32[128,512]{1,0:T(8,128)S(1)}, u32[]{:S(2)}, u32[]{:S(2)}) collective-permute-start(f32[128,512]{1,0:T(8,128)S(1)} %collective-permute-done.3.up1), channel_id=1, source_target_pairs={{0,8},{1,9},{2,10},{3,11},{4,12},{5,13},{6,14},{7,15},{8,16},{9,17... | collective-permute-start | bytes 786440 | tf_op jit(solution)/shard_map/ppermute | solution.py:406
  28.2 4.6 %collective-permute-start.15 = (f32[128,512]{1,0:T(8,128)S(1)}, f32[128,512]{1,0:T(8,128)S(1)}, u32[]{:S(2)}, u32[]{:S(2)}) collective-permute-start(f32[128,512]{1,0:T(8,128)S(1)} %copy-done.8), channel_id=1, source_target_pairs={{0,8},{1,9},{2,10},{3,11},{4,12},{5,13},{6,14},{7,15},{8,16},{9,17... | collective-permute-start | bytes 786440 | tf_op jit(solution)/shard_map/ppermute | solution.py:406
  34.1 4.6 %collective-permute-start.7 = (f32[128,512]{1,0:T(8,128)S(1)}, f32[128,512]{1,0:T(8,128)S(1)}, u32[]{:S(2)}, u32[]{:S(2)}) collective-permute-start(f32[128,512]{1,0:T(8,128)S(1)} %collective-permute-done.5.up2), channel_id=1, source_target_pairs={{0,8},{1,9},{2,10},{3,11},{4,12},{5,13},{6,14},{7,15},{8,16},{9,17... | collective-permute-start | bytes 786440 | tf_op jit(solution)/shard_map/ppermute | solution.py:406
  40.7 4.6 %collective-permute-start.17 = (f32[128,512]{1,0:T(8,128)S(1)}, f32[128,512]{1,0:T(8,128)S(1)}, u32[]{:S(2)}, u32[]{:S(2)}) collective-permute-start(f32[128,512]{1,0:T(8,128)S(1)} %collective-permute-done.15.up1), channel_id=1, source_target_pairs={{0,8},{1,9},{2,10},{3,11},{4,12},{5,13},{6,14},{7,15},{8,16},{9,17... | collective-permute-start | bytes 786440 | tf_op jit(solution)/shard_map/ppermute | solution.py:406
  48.7 2.7 %collective-permute-done.17.up2 = f32[128,512]{1,0:T(8,128)S(1)} collective-permute-done((f32[128,512]{1,0:T(8,128)S(1)}, f32[128,512]{1,0:T(8,128)S(1)}, u32[]{:S(2)}, u32[]{:S(2)}) %collective-permute-start.17) | collective-permute-done | bytes 262176 | tf_op jit(solution)/shard_map/ppermute | solution.py:406
  51.4 5.1 %collective-permute-start.19 = (f32[128,512]{1,0:T(8,128)S(1)}, f32[128,512]{1,0:T(8,128)}, u32[]{:S(2)}, u32[]{:S(2)}) collective-permute-start(f32[128,512]{1,0:T(8,128)S(1)} %collective-permute-done.17.up2), channel_id=1, source_target_pairs={{0,8},{1,9},{2,10},{3,11},{4,12},{5,13},{6,14},{7,15},{8,16},{9,17... | collective-permute-start | bytes 786440 | tf_op jit(solution)/shard_map/ppermute | solution.py:406
  59.1 2.0 %shard_map.92 = (f32[96,1024]{1,0:T(8,128)S(1)}, f32[96,1024]{1,0:T(8,128)S(1)}, f32[96,1024]{1,0:T(8,128)S(1)}, f32[96,1024]{1,0:T(8,128)S(1)}, bf16[512,1024]{1,0:T(8,128)(2,1)S(1)}) custom-call(bf16[384,512]{1,0:T(8,128)(2,1)S(1)} %get-tuple-element.30.slot_terms, bf16[128,512]{1,0:T(8,128)(2,1)S(1)} %copy-done.6, bf16[128,512]{1,0:T(8,128)(2,1)S(1)} %copy-done.7, ...), custom_call_target="tpu_custom_call" | custom-call | flops 1300000000 | tf_op jit(solution)/shard_map/pallas_call | solution.py:485
  61.1 2.1 %collective-permute-start.12 = (f32[96,1024]{1,0:T(8,128)S(1)}, f32[96,1024]{1,0:T(8,128)S(1)}, u32[]{:S(2)}, u32[]{:S(2)}) collective-permute-start(f32[96,1024]{1,0:T(8,128)S(1)} %get-tuple-element.35), channel_id=1, source_target_pairs={{0,2},{1,3},{2,0},{3,1},{4,6},{5,7},{6,4},{7,5},{8,10},{9,11},{10,... | collective-permute-start | bytes 1179656 | tf_op jit(solution)/shard_map/ppermute | solution.py:406
  63.2 1.5 %collective-permute-start.13 = (f32[96,1024]{1,0:T(8,128)S(1)}, f32[96,1024]{1,0:T(8,128)S(1)}, u32[]{:S(2)}, u32[]{:S(2)}) collective-permute-start(f32[96,1024]{1,0:T(8,128)S(1)} %get-tuple-element.36), channel_id=1, source_target_pairs={{0,4},{1,5},{2,6},{3,7},{4,0},{5,1},{6,2},{7,3},{8,12},{9,13},{10,... | collective-permute-start | bytes 1179656 | tf_op jit(solution)/shard_map/ppermute | solution.py:406
  64.6 1.5 %collective-permute-done.20.down3 = f32[128,512]{1,0:T(8,128)} collective-permute-done((f32[128,512]{1,0:T(8,128)S(1)}, f32[128,512]{1,0:T(8,128)}, u32[]{:S(2)}, u32[]{:S(2)}) %collective-permute-start.20) | collective-permute-done | bytes 262176 | tf_op jit(solution)/shard_map/ppermute | solution.py:406
  66.2 2.9 %collective-permute-start.14 = (f32[96,1024]{1,0:T(8,128)S(1)}, f32[96,1024]{1,0:T(8,128)S(1)}, u32[]{:S(2)}, u32[]{:S(2)}) collective-permute-start(f32[96,1024]{1,0:T(8,128)S(1)} %get-tuple-element.37), channel_id=1, source_target_pairs={{0,6},{1,7},{2,4},{3,5},{4,2},{5,3},{6,0},{7,1},{8,14},{9,15},{10,... | collective-permute-start | bytes 1179656 | tf_op jit(solution)/shard_map/ppermute | solution.py:406
  73.2 2.9 %collective-permute-start.27 = (f32[288,128]{1,0:T(8,128)S(1)}, f32[288,128]{1,0:T(8,128)S(1)}, u32[]{:S(2)}, u32[]{:S(2)}) collective-permute-start(f32[288,128]{1,0:T(8,128)S(1)} %get-tuple-element.50), channel_id=1, source_target_pairs={{0,6},{1,7},{2,4},{3,5},{4,2},{5,3},{6,0},{7,1},{8,14},{9,15},{10,... | collective-permute-start | bytes 442376 | tf_op jit(solution)/shard_map/ppermute | solution.py:406
  76.1 6.6 %collective-permute-done.13.refs_2_ = f32[96,1024]{1,0:T(8,128)S(1)} collective-permute-done((f32[96,1024]{1,0:T(8,128)S(1)}, f32[96,1024]{1,0:T(8,128)S(1)}, u32[]{:S(2)}, u32[]{:S(2)}) %collective-permute-start.13) | collective-permute-done | bytes 393248 | tf_op jit(solution)/shard_map/ppermute | solution.py:406
  83.3 1.4 %collective-permute-done.25.refs_5_ = f32[288,128]{1,0:T(8,128)S(1)} collective-permute-done((f32[288,128]{1,0:T(8,128)S(1)}, f32[288,128]{1,0:T(8,128)S(1)}, u32[]{:S(2)}, u32[]{:S(2)}) %collective-permute-start.25) | collective-permute-done | bytes 147488 | tf_op jit(solution)/shard_map/ppermute | solution.py:406
  84.7 4.0 %collective-permute-done.26.refs_6_ = f32[288,128]{1,0:T(8,128)S(1)} collective-permute-done((f32[288,128]{1,0:T(8,128)S(1)}, f32[288,128]{1,0:T(8,128)S(1)}, u32[]{:S(2)}, u32[]{:S(2)}) %collective-permute-start.26) | collective-permute-done | bytes 147488 | tf_op jit(solution)/shard_map/ppermute | solution.py:406
  88.8 1.7 %shard_map.99 = (bf16[128,4096]{1,0:T(8,128)(2,1)}, f32[1,128]{1,0:T(1,128)}, f32[4,4096]{1,0:T(4,128)}) custom-call(f32[96,1024]{1,0:T(8,128)S(1)} %get-tuple-element.34.refs_0_, f32[96,1024]{1,0:T(8,128)S(1)} %collective-permute-done.12.refs_1_, f32[96,1024]{1,0:T(8,128)S(1)} %collective-permute-done.13.refs_2_, ...), custom_call_target="tpu_custom_call" | custom-call | bytes 4194304 | tf_op jit(solution)/shard_map/pallas_call | solution.py:514
  (67 shorter events, 17.8 us)
Async XLA Ops:
  2.3 14.1 %collective-permute-start = (f32[264,128]{1,0:T(8,128)}, f32[264,128]{1,0:T(8,128)S(1)}, u32[]{:S(2)}, u32[]{:S(2)}) collective-permute-start(f32[264,128]{1,0:T(8,128)} %shard_map.85.refs_0_), channel_id=1, source_target_pairs={{0,8},{1,9},{2,10},{3,11},{4,12},{5,13},{6,14},{7,15},{8,16},{9,17... | collective-permute-start | bytes 405512 | tf_op jit(solution)/shard_map/ppermute | solution.py:406
  5.3 11.1 %collective-permute-start.1 = (f32[264,128]{1,0:T(8,128)}, f32[264,128]{1,0:T(8,128)S(1)}, u32[]{:S(2)}, u32[]{:S(2)}) collective-permute-start(f32[264,128]{1,0:T(8,128)} %shard_map.85.refs_0_), channel_id=1, source_target_pairs={{0,24},{1,25},{2,26},{3,27},{4,28},{5,29},{6,30},{7,31},{8,0},{9,1... | collective-permute-start | bytes 405512 | tf_op jit(solution)/shard_map/ppermute | solution.py:406
  7.4 12.5 %collective-permute-start.2 = (f32[264,128]{1,0:T(8,128)}, f32[264,128]{1,0:T(8,128)S(1)}, u32[]{:S(2)}, u32[]{:S(2)}) collective-permute-start(f32[264,128]{1,0:T(8,128)} %shard_map.85.refs_0_), channel_id=1, source_target_pairs={{0,16},{1,17},{2,18},{3,19},{4,20},{5,21},{6,22},{7,23},{8,24},{9,... | collective-permute-start | bytes 405512 | tf_op jit(solution)/shard_map/ppermute | solution.py:406
  11.6 13.9 %collective-permute-start.3 = (f32[128,512]{1,0:T(8,128)}, f32[128,512]{1,0:T(8,128)S(1)}, u32[]{:S(2)}, u32[]{:S(2)}) collective-permute-start(f32[128,512]{1,0:T(8,128)} %get-tuple-element.33), channel_id=1, source_target_pairs={{0,8},{1,9},{2,10},{3,11},{4,12},{5,13},{6,14},{7,15},{8,16},{9,17... | collective-permute-start | bytes 786440 | tf_op jit(solution)/shard_map/ppermute | solution.py:406
  15.1 11.7 %collective-permute-start.4 = (f32[128,512]{1,0:T(8,128)}, f32[128,512]{1,0:T(8,128)S(1)}, u32[]{:S(2)}, u32[]{:S(2)}) collective-permute-start(f32[128,512]{1,0:T(8,128)} %get-tuple-element.33), channel_id=1, source_target_pairs={{8,0},{9,1},{10,2},{11,3},{12,4},{13,5},{14,6},{15,7},{16,8},{17,9... | collective-permute-start | bytes 786440 | tf_op jit(solution)/shard_map/ppermute | solution.py:406
  21.6 36.3 %all-to-all-start = ((f32[4,264,512]{2,1,0:T(8,128)}), f32[4,264,512]{2,1,0:T(8,128)S(1)}, u32[]{:S(2)}, u32[]{:S(2)}) async-start(f32[4,264,512]{2,1,0:T(8,128)} %copy-done), calls=%async_computation | async-start | bytes 4325376 | tf_op jit(solution)/shard_map/all_to_all | solution.py:445
  26.9 11.8 %collective-permute-start.6 = (f32[128,512]{1,0:T(8,128)S(1)}, f32[128,512]{1,0:T(8,128)S(1)}, u32[]{:S(2)}, u32[]{:S(2)}) collective-permute-start(f32[128,512]{1,0:T(8,128)S(1)} %collective-permute-done.4.down1), channel_id=1, source_target_pairs={{8,0},{9,1},{10,2},{11,3},{12,4},{13,5},{14,6},{15,7},{16,8},{17,9... | collective-permute-start | bytes 786440 | tf_op jit(solution)/shard_map/ppermute | solution.py:406
  28.2 12.5 %collective-permute-start.15 = (f32[128,512]{1,0:T(8,128)S(1)}, f32[128,512]{1,0:T(8,128)S(1)}, u32[]{:S(2)}, u32[]{:S(2)}) collective-permute-start(f32[128,512]{1,0:T(8,128)S(1)} %copy-done.8), channel_id=1, source_target_pairs={{0,8},{1,9},{2,10},{3,11},{4,12},{5,13},{6,14},{7,15},{8,16},{9,17... | collective-permute-start | bytes 786440 | tf_op jit(solution)/shard_map/ppermute | solution.py:406
  32.7 12.5 %collective-permute-start.16 = (f32[128,512]{1,0:T(8,128)S(1)}, f32[128,512]{1,0:T(8,128)S(1)}, u32[]{:S(2)}, u32[]{:S(2)}) collective-permute-start(f32[128,512]{1,0:T(8,128)S(1)} %copy-done.8), channel_id=1, source_target_pairs={{8,0},{9,1},{10,2},{11,3},{12,4},{13,5},{14,6},{15,7},{16,8},{17,9... | collective-permute-start | bytes 786440 | tf_op jit(solution)/shard_map/ppermute | solution.py:406
  34.1 13.3 %collective-permute-start.7 = (f32[128,512]{1,0:T(8,128)S(1)}, f32[128,512]{1,0:T(8,128)S(1)}, u32[]{:S(2)}, u32[]{:S(2)}) collective-permute-start(f32[128,512]{1,0:T(8,128)S(1)} %collective-permute-done.5.up2), channel_id=1, source_target_pairs={{0,8},{1,9},{2,10},{3,11},{4,12},{5,13},{6,14},{7,15},{8,16},{9,17... | collective-permute-start | bytes 786440 | tf_op jit(solution)/shard_map/ppermute | solution.py:406
  40.7 17.8 %collective-permute-start.9 = (f32[128,512]{1,0:T(8,128)}, f32[128,512]{1,0:T(8,128)}, u32[]{:S(2)}, u32[]{:S(2)}) collective-permute-start(f32[128,512]{1,0:T(8,128)} %shard_map.89.refs_0_), channel_id=1, source_target_pairs={{0,1},{1,0},{2,3},{3,2},{4,5},{5,4},{6,7},{7,6},{8,9},{9,8},{10,11... | collective-permute-start | bytes 786440 | tf_op jit(solution)/shard_map/ppermute | solution.py:406
  40.7 10.8 %collective-permute-start.17 = (f32[128,512]{1,0:T(8,128)S(1)}, f32[128,512]{1,0:T(8,128)S(1)}, u32[]{:S(2)}, u32[]{:S(2)}) collective-permute-start(f32[128,512]{1,0:T(8,128)S(1)} %collective-permute-done.15.up1), channel_id=1, source_target_pairs={{0,8},{1,9},{2,10},{3,11},{4,12},{5,13},{6,14},{7,15},{8,16},{9,17... | collective-permute-start | bytes 786440 | tf_op jit(solution)/shard_map/ppermute | solution.py:406
  45.3 11.3 %collective-permute-start.18 = (f32[128,512]{1,0:T(8,128)S(1)}, f32[128,512]{1,0:T(8,128)S(1)}, u32[]{:S(2)}, u32[]{:S(2)}) collective-permute-start(f32[128,512]{1,0:T(8,128)S(1)} %collective-permute-done.16.down1), channel_id=1, source_target_pairs={{8,0},{9,1},{10,2},{11,3},{12,4},{13,5},{14,6},{15,7},{16,8},{17,9... | collective-permute-start | bytes 786440 | tf_op jit(solution)/shard_map/ppermute | solution.py:406
  47.3 11.3 %collective-permute-start.10 = (f32[128,512]{1,0:T(8,128)}, f32[128,512]{1,0:T(8,128)}, u32[]{:S(2)}, u32[]{:S(2)}) collective-permute-start(f32[128,512]{1,0:T(8,128)} %shard_map.90.refs_1_), channel_id=1, source_target_pairs={{0,1},{1,0},{2,3},{3,2},{4,5},{5,4},{6,7},{7,6},{8,9},{9,8},{10,11... | collective-permute-start | bytes 786440 | tf_op jit(solution)/shard_map/ppermute | solution.py:406
  48.7 10.4 %collective-permute-start.11 = (f32[128,512]{1,0:T(8,128)}, f32[128,512]{1,0:T(8,128)}, u32[]{:S(2)}, u32[]{:S(2)}) collective-permute-start(f32[128,512]{1,0:T(8,128)} %shard_map.91.refs_2_), channel_id=1, source_target_pairs={{0,1},{1,0},{2,3},{3,2},{4,5},{5,4},{6,7},{7,6},{8,9},{9,8},{10,11... | collective-permute-start | bytes 786440 | tf_op jit(solution)/shard_map/ppermute | solution.py:406
  51.4 11.7 %collective-permute-start.19 = (f32[128,512]{1,0:T(8,128)S(1)}, f32[128,512]{1,0:T(8,128)}, u32[]{:S(2)}, u32[]{:S(2)}) collective-permute-start(f32[128,512]{1,0:T(8,128)S(1)} %collective-permute-done.17.up2), channel_id=1, source_target_pairs={{0,8},{1,9},{2,10},{3,11},{4,12},{5,13},{6,14},{7,15},{8,16},{9,17... | collective-permute-start | bytes 786440 | tf_op jit(solution)/shard_map/ppermute | solution.py:406
  58.5 11.7 %collective-permute-start.21 = (f32[128,512]{1,0:T(8,128)S(1)}, f32[128,512]{1,0:T(8,128)S(1)}, u32[]{:S(2)}, u32[]{:S(2)}) collective-permute-start(f32[128,512]{1,0:T(8,128)S(1)} %shard_map.93.refs_0_), channel_id=1, source_target_pairs={{0,1},{1,0},{2,3},{3,2},{4,5},{5,4},{6,7},{7,6},{8,9},{9,8},{10,11... | collective-permute-start | bytes 786440 | tf_op jit(solution)/shard_map/ppermute | solution.py:406
  58.6 11.7 %collective-permute-start.22 = (f32[128,512]{1,0:T(8,128)S(1)}, f32[128,512]{1,0:T(8,128)S(1)}, u32[]{:S(2)}, u32[]{:S(2)}) collective-permute-start(f32[128,512]{1,0:T(8,128)S(1)} %shard_map.94.refs_1_), channel_id=1, source_target_pairs={{0,1},{1,0},{2,3},{3,2},{4,5},{5,4},{6,7},{7,6},{8,9},{9,8},{10,11... | collective-permute-start | bytes 786440 | tf_op jit(solution)/shard_map/ppermute | solution.py:406
  61.1 12.1 %collective-permute-start.12 = (f32[96,1024]{1,0:T(8,128)S(1)}, f32[96,1024]{1,0:T(8,128)S(1)}, u32[]{:S(2)}, u32[]{:S(2)}) collective-permute-start(f32[96,1024]{1,0:T(8,128)S(1)} %get-tuple-element.35), channel_id=1, source_target_pairs={{0,2},{1,3},{2,0},{3,1},{4,6},{5,7},{6,4},{7,5},{8,10},{9,11},{10,... | collective-permute-start | bytes 1179656 | tf_op jit(solution)/shard_map/ppermute | solution.py:406
  63.2 19.4 %collective-permute-start.13 = (f32[96,1024]{1,0:T(8,128)S(1)}, f32[96,1024]{1,0:T(8,128)S(1)}, u32[]{:S(2)}, u32[]{:S(2)}) collective-permute-start(f32[96,1024]{1,0:T(8,128)S(1)} %get-tuple-element.36), channel_id=1, source_target_pairs={{0,4},{1,5},{2,6},{3,7},{4,0},{5,1},{6,2},{7,3},{8,12},{9,13},{10,... | collective-permute-start | bytes 1179656 | tf_op jit(solution)/shard_map/ppermute | solution.py:406
  66.2 16.9 %collective-permute-start.14 = (f32[96,1024]{1,0:T(8,128)S(1)}, f32[96,1024]{1,0:T(8,128)S(1)}, u32[]{:S(2)}, u32[]{:S(2)}) collective-permute-start(f32[96,1024]{1,0:T(8,128)S(1)} %get-tuple-element.37), channel_id=1, source_target_pairs={{0,6},{1,7},{2,4},{3,5},{4,2},{5,3},{6,0},{7,1},{8,14},{9,15},{10,... | collective-permute-start | bytes 1179656 | tf_op jit(solution)/shard_map/ppermute | solution.py:406
  72.5 12.2 %collective-permute-start.25 = (f32[288,128]{1,0:T(8,128)S(1)}, f32[288,128]{1,0:T(8,128)S(1)}, u32[]{:S(2)}, u32[]{:S(2)}) collective-permute-start(f32[288,128]{1,0:T(8,128)S(1)} %get-tuple-element.48), channel_id=1, source_target_pairs={{0,2},{1,3},{2,0},{3,1},{4,6},{5,7},{6,4},{7,5},{8,10},{9,11},{10,... | collective-permute-start | bytes 442376 | tf_op jit(solution)/shard_map/ppermute | solution.py:406
  73.1 15.6 %collective-permute-start.26 = (f32[288,128]{1,0:T(8,128)S(1)}, f32[288,128]{1,0:T(8,128)S(1)}, u32[]{:S(2)}, u32[]{:S(2)}) collective-permute-start(f32[288,128]{1,0:T(8,128)S(1)} %get-tuple-element.49), channel_id=1, source_target_pairs={{0,4},{1,5},{2,6},{3,7},{4,0},{5,1},{6,2},{7,3},{8,12},{9,13},{10,... | collective-permute-start | bytes 442376 | tf_op jit(solution)/shard_map/ppermute | solution.py:406
  73.2 15.6 %collective-permute-start.27 = (f32[288,128]{1,0:T(8,128)S(1)}, f32[288,128]{1,0:T(8,128)S(1)}, u32[]{:S(2)}, u32[]{:S(2)}) collective-permute-start(f32[288,128]{1,0:T(8,128)S(1)} %get-tuple-element.50), channel_id=1, source_target_pairs={{0,6},{1,7},{2,4},{3,5},{4,2},{5,3},{6,0},{7,1},{8,14},{9,15},{10,... | collective-permute-start | bytes 442376 | tf_op jit(solution)/shard_map/ppermute | solution.py:406
  (14 other events, 103.8 us)
